TPU v7x, 512 devices: a whole 4x4x16 slice. The times are simulated.
512 devices in a mesh: prefix: 64 (over z, x), tensor: 8 (over y, core).
Axes of the slice: x: 4, y: 4, z: 16, core: 2. Of those that a mesh axis runs over, the one named last changes fastest.
Arguments:
- queries: bfloat16 [4096, 3, 4096], P('prefix', None, 'tensor'), may hold values from -100 to 100
- prefix_cache: bfloat16 [64, 8, 128, 2304], P('prefix', 'tensor'), may hold values from -10 to 10
- suffix_cache: bfloat16 [4096, 8, 128, 80], P('prefix', 'tensor'), may hold values from -10 to 10
- suffix_lengths: int32 [4096], P('prefix'), may hold values from 50 to 80, as said below
- request_prefix: int32 [4096, 1], replicated, may hold values from 0 to 63; in each aligned block of 64 rows (0 to 63, 64 to 127, ...) at most 2 rows name the same one
- prefix_owner: int32 [64], replicated, may hold values from 0 to 63, each once
- out_proj: bfloat16 [4096, 2880], P('tensor'), may hold values from -0.25 to 0.25
Outputs:
- output: bfloat16 [4096, 3, 2880], P('prefix', None, 'tensor')
Inputs may be any that keep to these rules, and one draw needn't show every extreme that they name: `request_prefix`: the requests of one device name any one prefix at most 2 times. `prefix_owner`: each stored index holds exactly one prefix. `suffix_lengths`: every device homes a request whose suffix cache is full.
All inputs are finite; a program needn't handle non-finite values.
Results may differ from a plain program's by a relative error of at most 0.017.
Values may be sent and summed in bfloat16 or wider, within the bound.
No kernel may reach another device: no remote copies, remote signals or barrier semaphores. Data moves between devices by JAX's collectives and lax.ppermute only.
A program may use at most 128 MiB of HBM per device.

v0:
```python
import math

import jax
import jax.numpy as jnp
from jax import lax
from jax.sharding import PartitionSpec as P


def softmax_partial(scores, value_rows, form, usable):
    if usable is not None:
        scores = jnp.where(usable, scores, -jnp.inf)
    highest = jnp.max(scores, axis=-1, keepdims=True)
    weight = jnp.exp(scores - highest)
    weight_sum = jnp.sum(weight, axis=-1)
    numer = jnp.einsum(
        form, weight.astype(jnp.bfloat16), value_rows, preferred_element_type=jnp.float32
    )
    return (numer / weight_sum[..., None], highest[..., 0] + jnp.log(weight_sum))


def source_group(source_count, rows_each):
    target = max(1, 1024 // rows_each)
    return math.gcd(source_count, 1 << target.bit_length() - 1)


def serve_prefix(received, cache_rows, step_count, kv_dev, group_size, head_dim):
    source_count, row_count, row_width = received.shape
    key_rows = cache_rows[:, :head_dim, :]
    value_rows = cache_rows[:, head_dim:, :]
    scale = 1.0 / math.sqrt(head_dim)
    sources = source_group(source_count, row_count * step_count * kv_dev * group_size)
    blocks = received.reshape(
        source_count // sources, sources * row_count, step_count, kv_dev, group_size, head_dim
    )

    def one_block(query_block):
        scores = (
            jnp.einsum(
                "nsvgd,vdl->nsvgl", query_block, key_rows, preferred_element_type=jnp.float32
            )
            * scale
        )
        return softmax_partial(scores, value_rows, "nsvgl,vdl->nsvgd", None)

    part_out, part_lse = lax.map(one_block, blocks)
    return (
        part_out.reshape(source_count, row_count, row_width),
        part_lse.reshape(source_count, row_count, row_width // head_dim),
    )


def send_back(partials):
    return (
        lax.all_to_all(partials[0], "prefix", split_axis=0, concat_axis=0, tiled=True),
        lax.all_to_all(partials[1], "prefix", split_axis=0, concat_axis=0, tiled=True),
    )


def shards(
    queries, prefix_cache, suffix_cache, suffix_lengths, request_prefix, prefix_owner, out_proj
):
    req_dev, step_count, query_width = queries.shape
    kv_dev = prefix_cache.shape[1]
    head_dim = prefix_cache.shape[2] // 2
    group_size = query_width // (kv_dev * head_dim)
    prefix_count = lax.axis_size("prefix")
    capacity = 2 * req_dev // prefix_count
    slot_count = prefix_count * capacity
    own_index = lax.axis_index("prefix")
    row_width = step_count * query_width
    chosen_prefix = request_prefix[:, 0].reshape(prefix_count, req_dev)
    destination = prefix_owner[request_prefix[:, 0]].reshape(prefix_count, req_dev)
    same_prefix = chosen_prefix[:, :, None] == chosen_prefix[:, None, :]
    earlier = jnp.arange(req_dev)[None, :] < jnp.arange(req_dev)[:, None]
    rank = jnp.sum(jnp.logical_and(same_prefix, earlier[None]), axis=2)
    codes = destination * capacity + rank
    own_codes = lax.dynamic_index_in_dim(codes, own_index, 0, keepdims=False)
    flat_queries = queries.reshape(req_dev, row_width)
    cache_rows = prefix_cache[0]
    codes_flat = codes.reshape(-1)
    empty_rows = jnp.zeros((slot_count, row_width), jnp.bfloat16)
    shard_rows = lax.all_gather(flat_queries, "prefix", axis=0, tiled=True)
    row_count = shard_rows.shape[0]
    source = jnp.arange(row_count, dtype=jnp.int32) // req_dev
    target = jnp.where(
        codes_flat // capacity == own_index, source * capacity + codes_flat % capacity, slot_count
    )
    received = empty_rows.at[target].set(shard_rows, mode="drop")
    serve_received = received.reshape(prefix_count, capacity, row_width)
    homed_out, homed_lse = send_back(
        serve_prefix(serve_received, cache_rows, step_count, kv_dev, group_size, head_dim)
    )
    prefix_out = homed_out.reshape(slot_count, row_width)[own_codes]
    prefix_out = prefix_out.reshape(req_dev, step_count, kv_dev, group_size, head_dim)
    prefix_lse = homed_lse.reshape(slot_count, row_width // head_dim)[own_codes]
    prefix_lse = prefix_lse.reshape(req_dev, step_count, kv_dev, group_size)
    query_heads = queries.reshape(req_dev, step_count, kv_dev, group_size, head_dim)
    scale = 1.0 / math.sqrt(head_dim)
    suffix_scores = (
        jnp.einsum(
            "rsvgd,rvdl->rsvgl",
            query_heads,
            suffix_cache[:, :, :head_dim, :],
            preferred_element_type=jnp.float32,
        )
        * scale
    )
    positions = jnp.arange(suffix_cache.shape[3], dtype=jnp.int32)
    limits = (
        suffix_lengths[:, None]
        - (step_count - 1)
        + jnp.arange(step_count, dtype=jnp.int32)[None, :]
    )
    usable = positions[None, None, None, None, :] < limits[:, :, None, None, None]
    suffix_out, suffix_lse = softmax_partial(
        suffix_scores, suffix_cache[:, :, head_dim:, :], "rsvgl,rvdl->rsvgd", usable
    )
    total_lse = jnp.logaddexp(prefix_lse, suffix_lse)
    attention = (
        prefix_out * jnp.exp(prefix_lse - total_lse)[..., None]
        + suffix_out * jnp.exp(suffix_lse - total_lse)[..., None]
    )
    attention = attention.astype(jnp.bfloat16).reshape(req_dev * step_count, query_width)
    projected = jnp.dot(attention, out_proj, preferred_element_type=jnp.float32)
    projected = projected.astype(jnp.bfloat16).reshape(req_dev, step_count, out_proj.shape[1])
    return (
        lax.psum_scatter(projected, "tensor", scatter_dimension=2, tiled=True)
        .astype(jnp.float32)
        .astype(jnp.bfloat16)
    )


def solution(mesh):
    return jax.shard_map(
        shards,
        mesh=mesh,
        in_specs=(
            P("prefix", None, "tensor"),
            P("prefix", "tensor", None, None),
            P("prefix", "tensor", None, None),
            P("prefix"),
            P(),
            P(),
            P("tensor", None),
        ),
        out_specs=P("prefix", None, "tensor"),
        check_vma=False,
    )
```

profile of v0, /device:TPU:1, one launch (start us, length us, event | category | flops | bytes accessed | tf_op | source)
XLA Modules:
  0.0 490.8 jit_solution(9650980140495372606)
XLA Ops:
  6.5 1.8 copy.61
  8.4 1.6 fusion.77
  10.0 2.1 fusion.76
  12.0 0.5 broadcast.747
  12.6 6.0 %compare_select_fusion.2 = (s32[4096,1]{0,1:T(1,128)S(1)}, s32[4096,1]{0,1:T(1,128)S(1)}, s32[4096]{0:T(1024)S(1)}) fusion(s32[]{:T(128)} %bitcast.75, s32[]{:T(128)} %bitcast.76, s32[]{:T(128)} %bitcast.77, s32[]{:T(128)} %bitcast.78, s32[]{:T(128)} %bitcast.79, s32[]{:T(128)} %bitcast.81, s32[]{:T(128)} %bitcast.80, s32[4096,1]{0,1:T(1,128)} %param.13, ...), kind=kLoop, calls=%fused_computation.107 | loop fusion | flops 61440 | bytes 65568 | tf_op jit(solution)/shard_map/gather | solution.py:72
  18.6 0.1 eq.30
  18.7 1.9 convert_reduce_fusion
  20.6 0.7 reduce_sum.30
  21.2 2.1 fusion.74
  23.3 2.1 fusion.75
  25.4 2.9 compare_reduce_fusion.56
  28.3 36.3 %select_multiply_fusion = s32[4096]{0:T(1024)S(1)} fusion(pred[4096]{0:T(1024)(128)(4,1)S(1)} %get-tuple-element.96, pred[4096]{0:T(1024)(128)(4,1)S(1)} %get-tuple-element.95, pred[4096]{0:T(1024)(128)(4,1)S(1)} %get-tuple-element.94, pred[4096]{0:T(1024)(128)(4,1)S(1)} %get-tuple-element.93, pred[4096]{0:T(1024)(128)(4,1)S(1)} %get-tuple-element.92, ...), kind=kLoop, calls=%fused_computation.127 | loop fusion | flops 237568 | bytes 266468 | tf_op jit(solution)/shard_map/mul | solution.py:76
  64.6 1.1 fusion.73
  65.7 1.5 compare_select_fusion
  67.2 117.4 %all-gather.2.cloned.1.call-done = bf16[4096,1536]{1,0:T(8,128)(2,1)} async-done(((bf16[64,1536]{1,0:T(8,128)(2,1)}), bf16[4096,1536]{1,0:T(8,128)(2,1)}) %all-gather.2.cloned.1.call-update) | async-done | bytes 12582928 | tf_op jit(solution)/shard_map/all_gather | solution.py:82
  184.6 20.2 %scatter_custom_fusion = bf16[128,1536]{1,0:T(8,128)(2,1)} fusion(s32[4096]{0:T(1024)} %bitcast.279, bf16[4096,1536]{1,0:T(8,128)(2,1)} %all-gather.2.cloned.1.call-done, bf16[]{:T(256)} %constant.77.clone.1), kind=kCustom, calls=%fused_computation.45 | custom fusion | bytes 393728 | tf_op jit(solution)/shard_map/scatter | solution.py:88
  204.8 2.3 reshape_reshape.3
  207.1 24.2 %while.12 = (s32[]{:T(128)}, f32[4,32,3,1,8,64]{5,4,2,1,3,0:T(8,128)}, f32[4,32,3,1,8]{4,2,1,3,0:T(4,128)}, bf16[4,32,3,1,8,64]{5,4,2,1,3,0:T(8,128)(2,1)}, bf16...) while((s32[]{:T(128)}, f32[4,32,3,1,8,64]{5,4,2,1,3,0:T(8,128)}, ...), condition=%wide.region_5.6_spmd, body=%wide.region_2.5_spmd.sunk | while | flops 467188992 | bytes 22500448 | solution.py:45
  207.1 2.1 bitcast_reduce_fusion.2
  209.2 1.3 fusion.87
  210.6 2.0 fusion.88
  212.6 0.6 bitcast_dynamic-update-slice_fusion.2
  213.2 2.1 bitcast_reduce_fusion.2
  215.3 1.3 fusion.87
  216.6 2.0 fusion.88
  218.6 0.6 bitcast_dynamic-update-slice_fusion.2
  219.3 2.1 bitcast_reduce_fusion.2
  221.3 1.3 fusion.87
  222.7 2.0 fusion.88
  224.7 0.6 bitcast_dynamic-update-slice_fusion.2
  225.3 2.1 bitcast_reduce_fusion.2
  227.4 1.3 fusion.87
  228.7 2.0 fusion.88
  230.7 0.6 bitcast_dynamic-update-slice_fusion.2
  231.3 1.8 reshape.422
  233.1 10.7 %all-to-all-start.1 = ((f32[64,2,24]{2,1,0:T(2,128)}), f32[64,2,24]{2,1,0:T(2,128)S(1)}, u32[]{:S(2)}, u32[]{:S(2)}) async-start(f32[64,2,24]{2,1,0:T(2,128)} %reshape.422), calls=%async_computation.1 | async-start | bytes 131072 | tf_op jit(solution)/shard_map/all_to_all | solution.py:55
  243.9 2.9 reshape.419
  246.8 11.1 %all-to-all-done.1 = f32[64,2,24]{2,1,0:T(2,128)S(1)} async-done(((f32[64,2,24]{2,1,0:T(2,128)}), f32[64,2,24]{2,1,0:T(2,128)S(1)}, u32[]{:S(2)}, u32[]{:S(2)}) %all-to-all-start.1) | async-done | bytes 12320 | tf_op jit(solution)/shard_map/all_to_all | solution.py:55
  257.9 5.5 %all-to-all-start = ((f32[64,2,1536]{2,1,0:T(2,128)}), f32[64,2,1536]{2,1,0:T(2,128)}, u32[]{:S(2)}, u32[]{:S(2)}) async-start(f32[64,2,1536]{2,1,0:T(2,128)} %reshape.419), calls=%async_computation | async-start | bytes 1572864 | tf_op jit(solution)/shard_map/all_to_all | solution.py:54
  263.3 0.3 reduce-scatter.4.cloned.1.call-start
  263.7 1.0 reshape.426
  264.7 0.1 iota_add_fusion
  264.8 0.1 iota_compare_fusion
  264.9 3.1 fusion.78
  268.0 0.1 copy.47
  268.1 1.7 fusion.59
  269.8 0.1 copy.46
  269.9 0.7 fusion.71
  270.6 0.6 gather_fusion.1
  271.3 0.8 copy.48
  272.1 0.8 copy.50
  272.8 29.2 %all-to-all-done = f32[64,2,1536]{2,1,0:T(2,128)} async-done(((f32[64,2,1536]{2,1,0:T(2,128)}), f32[64,2,1536]{2,1,0:T(2,128)}, u32[]{:S(2)}, u32[]{:S(2)}) %all-to-all-start) | async-done | bytes 786464 | tf_op jit(solution)/shard_map/all_to_all | solution.py:54
  302.0 2.6 reshape.420
  304.6 2.0 gather_fusion
  306.6 1.1 reshape.421
  307.7 3.8 fusion.55
  311.5 1.3 reshape.429
  312.8 2.1 convolution_convert_fusion
  314.9 2.7 reshape.430
  317.7 39.7 %copy.56 = bf16[64,3,2880]{1,0,2:T(8,128)(2,1)} copy(bf16[64,3,2880]{2,1,0:T(4,128)(2,1)S(1)} %reshape.430) | data formatting | bytes 2211840
  357.3 68.6 %reshape.671 = bf16[2880,192]{1,0:T(8,128)(2,1)} reshape(bf16[2880,64,3]{2,1,0:T(8,128)(2,1)} %bitcast.271) | data formatting | bytes 2211840
  426.0 35.8 %reduce-scatter.4.cloned.1.call-done = bf16[360,192]{1,0:T(8,128)(2,1)} async-done(((bf16[2880,192]{1,0:T(8,128)(2,1)}), bf16[360,192]{1,0:T(8,128)(2,1)}) %reduce-scatter.4.cloned.1.call-update) | async-done | bytes 138256
  461.8 14.3 %reshape.672 = bf16[360,64,3]{2,1,0:T(8,128)(2,1)} reshape(bf16[360,192]{1,0:T(8,128)(2,1)} %reduce-scatter.4.cloned.1.call-done) | data formatting | bytes 276480
  476.1 7.9 %copy.51 = bf16[64,3,360]{2,0,1:T(8,128)(2,1)} copy(bf16[64,3,360]{1,0,2:T(8,128)(2,1)} %bitcast.272) | data formatting | bytes 276480 | tf_op jit(solution)/shard_map/reduce_scatter | solution.py:127
  (23 shorter events, 0.3 us)
Async XLA Ops:
  6.5 306.2 %copy-start = (bf16[512,2880]{0,1:T(8,128)(2,1)S(1)}, bf16[512,2880]{0,1:T(8,128)(2,1)}, u32[]{:S(2)}) copy-start(bf16[512,2880]{0,1:T(8,128)(2,1)} %param.15) | copy-start | bytes 8847364
  6.5 178.1 %all-gather.2.cloned.1.call-start = ((), (), s32[]{:S(2)}) async-start(), calls=%async_computation.3 | async-start | bytes 12779520 | tf_op jit(solution)/shard_map/all_gather | solution.py:82
  20.5 44.1 %copy-start.4 = (s32[64,64]{1,0:T(8,128)}, s32[64,64]{1,0:T(8,128)S(1)}, u32[]{:S(2)}) copy-start(s32[64,64]{1,0:T(8,128)S(1)} %convert_reduce_fusion) | copy-start | bytes 49156
  231.3 32.4 %copy-start.2 = (bf16[64,3,512]{2,0,1:T(8,128)(2,1)S(1)}, bf16[64,3,512]{2,0,1:T(8,128)(2,1)}, u32[]{:S(2)}) copy-start(bf16[64,3,512]{2,0,1:T(8,128)(2,1)} %param.9) | copy-start | bytes 589828
  231.3 33.3 %copy-start.5 = (s32[64]{0:T(128)S(1)}, s32[64]{0:T(128)}, u32[]{:S(2)}) copy-start(s32[64]{0:T(128)} %param.12) | copy-start | bytes 772
  233.1 24.7 %all-to-all-start.1 = ((f32[64,2,24]{2,1,0:T(2,128)}), f32[64,2,24]{2,1,0:T(2,128)S(1)}, u32[]{:S(2)}, u32[]{:S(2)}) async-start(f32[64,2,24]{2,1,0:T(2,128)} %reshape.422), calls=%async_computation.1 | async-start | bytes 131072 | tf_op jit(solution)/shard_map/all_to_all | solution.py:55
  257.9 44.1 %all-to-all-start = ((f32[64,2,1536]{2,1,0:T(2,128)}), f32[64,2,1536]{2,1,0:T(2,128)}, u32[]{:S(2)}, u32[]{:S(2)}) async-start(f32[64,2,1536]{2,1,0:T(2,128)} %reshape.419), calls=%async_computation | async-start | bytes 1572864 | tf_op jit(solution)/shard_map/all_to_all | solution.py:54
  263.3 198.4 %reduce-scatter.4.cloned.1.call-start = ((), (), s32[]{:S(2)}) async-start(), calls=%async_computation.4 | async-start | bytes 1658880
  269.8 32.2 %copy-start.3 = (f32[64,3,8]{2,1,0:T(4,128)}, f32[64,3,8]{2,1,0:T(4,128)S(1)}, u32[]{:S(2)}) copy-start(f32[64,3,8]{2,1,0:T(4,128)S(1)} %fusion.59) | copy-start | bytes 18436
  476.1 7.9 %copy-start.1 = (bf16[512,2880]{0,1:T(8,128)(2,1)S(1)}, bf16[512,2880]{0,1:T(8,128)(2,1)}, u32[]{:S(2)}) copy-start(bf16[512,2880]{0,1:T(8,128)(2,1)} %param.15) | copy-start | bytes 8847364
Sparse Core Ops, SparseCore 0:
  10.3 174.2 all-gather.1
  426.1 35.6 reduce-scatter.3
where the time goes:
time: 493 us; the launch traced here: 491 us
  waiting for transfers between devices  194 us (39%)
  local copies, waits for them, and re-layouts  183 us (37%)
  other arithmetic  59.1 us (12%)
  matrix products  25.4 us (5%)
  starting transfers between devices  16.5 us (3%)
  between operations  13.6 us (3%)
    unnamed x16, local copies, waits for them, and re-layouts  123 us
    all_gather x1, waiting for transfers between devices, shards(): shard_rows = lax.all_gather(flat_queries, 'prefix', axis=0, tiled=True)  117 us
    mul x1, other arithmetic, shards(): codes = destination * capacity + rank  36.3 us
    unnamed x3, waiting for transfers between devices  35.9 us
    all_to_all x1, waiting for transfers between devices, send_back(): lax.all_to_all(partials[0], 'prefix', split_axis=0, concat_axis=0, tiled=...  29.2 us
    scatter x1, local copies, waits for them, and re-layouts, shards(): received = empty_rows.at[target].set(shard_rows, mode='drop')  20.2 us
    dot_general x5, matrix products, softmax_partial(): jnp.einsum(form, weight.astype(jnp.bfloat16), value_rows, preferred_eleme...  11.8 us
    all_to_all x1, waiting for transfers between devices, send_back(): lax.all_to_all(partials[1], 'prefix', split_axis=0, concat_axis=0, tiled=...  11.1 us
  transfers between devices with their start and end apart: 4, of which 4 were waited for; matrix products, arithmetic and copies ran while one was open for 14% of the time, Pallas kernels for 0%

commit v1 on v0

v1 whole, which is shorter than its diff:
```python
import functools

import jax
import jax.numpy as jnp
from jax import lax
from jax.experimental import pallas as pl
from jax.experimental.pallas import tpu as pltpu
from jax.sharding import PartitionSpec as P

LANES = 128
HALF = 64
X_SIZE = 4
CAPACITY = 2
GROUPS = X_SIZE * CAPACITY
STEPS = 3
ROWS = 12
PAD_ROWS = 16
SCALE = 0.125
VMEM_LIMIT = 56 * 1024 * 1024


def lane_iota(rows):
    return lax.broadcasted_iota(jnp.int32, (rows, LANES), 1)


def split_heads(rows):
    low = lane_iota(rows.shape[0]) < HALF
    even = jnp.where(low, rows, 0.0)
    odd = jnp.where(low, pltpu.roll(rows, HALF, 1), 0.0)
    return even, odd


def join_heads(even, odd):
    low = lane_iota(even.shape[0]) < HALF
    return jnp.where(low, pltpu.roll(even, HALF, 1), odd)


def nt_dot(left, right):
    return lax.dot_general(
        left, right, (((1,), (1,)), ((), ())), preferred_element_type=jnp.float32
    )


def route_kernel(me_ref, prefix_ref, owner_ref, q_ref, send_ref, rows_ref, code_ref, taken, source, qs, acc):
    requests = q_ref.shape[1]
    z_size = send_ref.shape[0]
    x_own = me_ref[0] % X_SIZE

    def clear(i, _):
        taken[i] = 0
        return 0

    lax.fori_loop(0, owner_ref.shape[0], clear, 0)

    def clear_source(i, _):
        source[i] = 0
        return 0

    lax.fori_loop(0, z_size * GROUPS, clear_source, 0)

    def place(r, _):
        name = prefix_ref[me_ref[0] * requests + r]
        owner = owner_ref[name]
        rank = taken[name]
        taken[name] = rank + 1
        offset = (owner % X_SIZE - x_own + X_SIZE) % X_SIZE
        code = (owner // X_SIZE) * GROUPS + offset * CAPACITY + rank
        code_ref[r] = code
        source[code] = r
        return 0

    lax.fori_loop(0, requests, place, 0)
    zeros = jnp.zeros((requests, LANES), jnp.float32)
    for i in range(PAD_ROWS):
        if i < ROWS:
            step, pair = divmod(i, ROWS // STEPS)
            value = q_ref[step, :, pair * LANES : (pair + 1) * LANES].astype(jnp.float32)
        else:
            value = zeros
        qs[pl.ds(i, requests, stride=PAD_ROWS), :] = value
    rows_ref[...] = qs[...].astype(jnp.bfloat16)

    def fill(z, _):
        for slot in range(GROUPS):
            r = source[z * GROUPS + slot]
            block = qs[pl.ds(pl.multiple_of(r * PAD_ROWS, PAD_ROWS), PAD_ROWS), :]
            acc[slot * ROWS : (slot + 1) * ROWS, :] = block[:ROWS]
        send_ref[z] = acc[...].astype(jnp.bfloat16)
        return 0

    lax.fori_loop(0, z_size, fill, 0)


def route(me, prefixes, owner, q3, z_size):
    requests = q3.shape[1]
    smem = pl.BlockSpec(memory_space=pltpu.SMEM)
    vmem = pl.BlockSpec(memory_space=pltpu.VMEM)
    return pl.pallas_call(
        route_kernel,
        out_shape=(
            jax.ShapeDtypeStruct((z_size, GROUPS * ROWS, LANES), jnp.bfloat16),
            jax.ShapeDtypeStruct((requests * PAD_ROWS, LANES), jnp.bfloat16),
            jax.ShapeDtypeStruct((requests,), jnp.int32),
        ),
        in_specs=[smem, smem, smem, vmem],
        out_specs=(vmem, vmem, smem),
        scratch_shapes=[
            pltpu.SMEM((owner.shape[0],), jnp.int32),
            pltpu.SMEM((z_size * GROUPS,), jnp.int32),
            pltpu.VMEM((requests * PAD_ROWS, LANES), jnp.float32),
            pltpu.VMEM((GROUPS * ROWS, LANES), jnp.float32),
        ],
        compiler_params=pltpu.CompilerParams(vmem_limit_bytes=VMEM_LIMIT),
        name="route",
    )(me, prefixes, owner, q3)


SUFFIX_BLOCK = 8


def suffix_kernel(length_ref, q_ref, kv_ref, out_ref, lse_ref):
    base = pl.program_id(0) * SUFFIX_BLOCK
    positions = kv_ref.shape[1]
    shape = (2 * PAD_ROWS, positions)
    step = lax.broadcasted_iota(jnp.int32, shape, 0) % PAD_ROWS // (ROWS // STEPS)
    past = lax.broadcasted_iota(jnp.int32, shape, 1) - step
    low = lane_iota(PAD_ROWS) < HALF
    for r in range(SUFFIX_BLOCK):
        rows = slice(r * PAD_ROWS, (r + 1) * PAD_ROWS)
        even, odd = split_heads(q_ref[rows].astype(jnp.float32) * SCALE)
        query = jnp.concatenate([even, odd], axis=0).astype(jnp.bfloat16)
        cache = kv_ref[r]
        scores = nt_dot(query, cache)
        usable = past < length_ref[base + r] - (STEPS - 1)
        scores = jnp.where(usable, scores, -jnp.inf)
        highest = jnp.max(scores, axis=1, keepdims=True)
        weight = jnp.exp(scores - highest)
        total = jnp.sum(weight, axis=1, keepdims=True)
        mixed = jnp.dot(weight.astype(jnp.bfloat16), cache, preferred_element_type=jnp.float32)
        mixed = mixed / total
        lse = highest + jnp.log(total)
        out_ref[rows] = join_heads(mixed[:PAD_ROWS], mixed[PAD_ROWS:])
        lse_ref[rows] = jnp.where(low, lse[:PAD_ROWS], lse[PAD_ROWS:])


def suffix_attention(lengths, q_rows, kv):
    requests, positions, _ = kv.shape
    block = SUFFIX_BLOCK * PAD_ROWS
    row_spec = pl.BlockSpec((block, LANES), lambda i: (i, 0))
    shape = jax.ShapeDtypeStruct((requests * PAD_ROWS, LANES), jnp.float32)
    return pl.pallas_call(
        suffix_kernel,
        grid=(requests // SUFFIX_BLOCK,),
        out_shape=(shape, shape),
        in_specs=[
            pl.BlockSpec(memory_space=pltpu.SMEM),
            row_spec,
            pl.BlockSpec((SUFFIX_BLOCK, positions, LANES), lambda i: (i, 0, 0)),
        ],
        out_specs=(row_spec, row_spec),
        compiler_params=pltpu.CompilerParams(vmem_limit_bytes=VMEM_LIMIT),
        cost_estimate=pl.CostEstimate(
            flops=4 * requests * 32 * 128 * 80 * 8, bytes_accessed=8_000_000, transcendentals=0
        ),
        name="suffix",
    )(lengths, q_rows, kv)


SOURCE_BLOCK = 8
PIECES = 3


def prefix_kernel(me_ref, recv_ref, kv_ref, ret_ref, cache, queries, acc):
    group, block = pl.program_id(0), pl.program_id(1)
    span = CAPACITY * ROWS
    rows = SOURCE_BLOCK * span

    @pl.when(jnp.logical_and(group == 0, block == 0))
    def _():
        queries[...] = recv_ref[...].astype(jnp.float32) * SCALE
        cache[LANES:, :] = jnp.ones_like(cache[LANES:, :])

    @pl.when(block == 0)
    def _():
        cache[:LANES, :] = kv_ref[0]

    sources = pl.ds(block * SOURCE_BLOCK, SOURCE_BLOCK)
    place = pl.ds(pl.multiple_of(group * span, 8), span)
    both = split_heads(queries[sources, place, :].reshape(rows, LANES))
    results = []
    for query in both:
        scores = jnp.dot(
            query.astype(jnp.bfloat16), cache[:LANES, :], preferred_element_type=jnp.float32
        )
        highest = jnp.max(scores, axis=1, keepdims=True)
        weight = jnp.exp(scores - highest).astype(jnp.bfloat16)
        mixed = nt_dot(weight, cache[...])
        total = mixed[:, LANES:]
        results.append((mixed[:, :LANES] / total, highest + jnp.log(total)))
    low = lane_iota(rows) < HALF
    acc[sources, place, :] = join_heads(results[0][0], results[1][0]).reshape(
        SOURCE_BLOCK, span, LANES
    )
    lse = jnp.where(low, results[0][1], results[1][1])
    high_part = lse.astype(jnp.bfloat16)
    rest = lse - high_part.astype(jnp.float32)
    mid_part = rest.astype(jnp.bfloat16)
    low_part = (rest - mid_part.astype(jnp.float32)).astype(jnp.bfloat16)
    lane = lane_iota(rows) % HALF
    row = lax.broadcasted_iota(jnp.int32, (rows, LANES), 0) % ROWS
    packed = jnp.zeros((rows, LANES), jnp.float32)
    for i, part in enumerate((high_part, mid_part, low_part)):
        packed = jnp.where(lane == row + i * ROWS, part.astype(jnp.float32), packed)
    slots = SOURCE_BLOCK * CAPACITY
    pick = lax.broadcasted_iota(jnp.int32, (slots, rows), 1) // ROWS
    pick = (pick == lax.broadcasted_iota(jnp.int32, (slots, rows), 0)).astype(jnp.bfloat16)
    lse_rows = jnp.dot(pick, packed.astype(jnp.bfloat16), preferred_element_type=jnp.float32)
    for g in range(X_SIZE):

        @pl.when(group == g)
        def _():
            for source in range(SOURCE_BLOCK):
                acc[block * SOURCE_BLOCK + source, GROUPS * ROWS + g * CAPACITY : GROUPS * ROWS + (g + 1) * CAPACITY, :] = (
                    lse_rows[source * CAPACITY : (source + 1) * CAPACITY]
                )

    last = jnp.logical_and(group == pl.num_programs(0) - 1, block == pl.num_programs(1) - 1)

    @pl.when(last)
    def _():
        ret_ref[...] = acc[...].astype(jnp.bfloat16)


def prefix_attention(me, recv, kv):
    z_size = recv.shape[0]
    length = kv.shape[2]
    whole = lambda *shape: pl.BlockSpec(shape, lambda g, b, me: (0,) * len(shape))
    out_rows = GROUPS * ROWS + GROUPS
    return pl.pallas_call(
        prefix_kernel,
        out_shape=jax.ShapeDtypeStruct((z_size, out_rows, LANES), jnp.bfloat16),
        grid_spec=pltpu.PrefetchScalarGridSpec(
            num_scalar_prefetch=1,
            grid=(X_SIZE, z_size // SOURCE_BLOCK),
            in_specs=[
                whole(*recv.shape),
                pl.BlockSpec((1, LANES, length), lambda g, b, me: ((me[0] + g) % X_SIZE, 0, 0)),
            ],
            out_specs=whole(z_size, out_rows, LANES),
            scratch_shapes=[
                pltpu.VMEM((2 * LANES, length), jnp.bfloat16),
                pltpu.VMEM(recv.shape, jnp.float32),
                pltpu.VMEM((z_size, out_rows, LANES), jnp.float32),
            ],
        ),
        compiler_params=pltpu.CompilerParams(vmem_limit_bytes=VMEM_LIMIT),
        cost_estimate=pl.CostEstimate(
            flops=8_000_000_000, bytes_accessed=4_000_000, transcendentals=0
        ),
        name="prefix",
    )(me, recv, kv)


def merge_kernel(code_ref, ret_ref, suffix_ref, suffix_lse_ref, w_ref, out_ref, spread, picked, merged, left):
    z_size = ret_ref.shape[0]
    requests = code_ref.shape[0]
    slot_rows = GROUPS * PAD_ROWS

    @pl.when(pl.program_id(0) == 0)
    def _():
        for z in range(z_size):
            block = ret_ref[z].astype(jnp.float32)
            for slot in range(GROUPS):
                spread[z, slot * PAD_ROWS : slot * PAD_ROWS + ROWS, :] = block[slot * ROWS : (slot + 1) * ROWS]
                spread[z, slot * PAD_ROWS + ROWS : slot * PAD_ROWS + ROWS + 1, :] = block[
                    GROUPS * ROWS + slot : GROUPS * ROWS + slot + 1
                ]

        def pick(r, _):
            code = code_ref[r]
            start = pl.multiple_of(code % GROUPS * PAD_ROWS, PAD_ROWS)
            picked[pl.ds(pl.multiple_of(r * PAD_ROWS, PAD_ROWS), PAD_ROWS), :] = spread[
                code // GROUPS, pl.ds(start, PAD_ROWS), :
            ]
            return 0

        lax.fori_loop(0, requests, pick, 0, unroll=8)
        total_rows = requests * PAD_ROWS
        packed = picked[pl.ds(ROWS, requests, stride=PAD_ROWS), :].astype(jnp.bfloat16)
        owner = lax.broadcasted_iota(jnp.int32, (total_rows, requests), 0) // PAD_ROWS
        owner = owner == lax.broadcasted_iota(jnp.int32, (total_rows, requests), 1)
        copies = jnp.dot(owner.astype(jnp.bfloat16), packed, preferred_element_type=jnp.float32)
        lane = lane_iota(total_rows) % HALF
        row = lax.broadcasted_iota(jnp.int32, (total_rows, LANES), 0) % PAD_ROWS
        own = jnp.logical_and(lane < PIECES * ROWS, lane % ROWS == row)
        copies = jnp.where(own, copies, 0.0).astype(jnp.bfloat16)
        same_half = lax.broadcasted_iota(jnp.int32, (LANES, LANES), 0) // HALF
        same_half = same_half == lane_iota(LANES) // HALF
        prefix_lse = jnp.dot(copies, same_half.astype(jnp.bfloat16), preferred_element_type=jnp.float32)
        gap = prefix_lse - suffix_lse_ref[...]
        small = jnp.exp(-jnp.abs(gap))
        large_weight = 1.0 / (1.0 + small)
        small_weight = small * large_weight
        prefix_first = gap >= 0.0
        merged[...] = picked[...] * jnp.where(prefix_first, large_weight, small_weight) + suffix_ref[
            ...
        ] * jnp.where(prefix_first, small_weight, large_weight)
        pairs = ROWS // STEPS
        for step in range(STEPS):
            for pair in range(pairs):
                left[step * requests : (step + 1) * requests, pair * LANES : (pair + 1) * LANES] = merged[
                    pl.ds(step * pairs + pair, requests, stride=PAD_ROWS), :
                ].astype(jnp.bfloat16)

    out_ref[0] = nt_dot(left[...], w_ref[0]).astype(jnp.bfloat16)


def merge_project(codes, ret, suffix_out, suffix_lse, weights, parts):
    requests = codes.shape[0]
    width = weights.shape[0] // parts
    depth = weights.shape[1]
    total_rows = requests * PAD_ROWS
    whole = lambda array: pl.BlockSpec(array.shape, lambda t: (0,) * array.ndim)
    return pl.pallas_call(
        merge_kernel,
        grid=(parts,),
        out_shape=jax.ShapeDtypeStruct((parts, STEPS * requests, width), jnp.bfloat16),
        in_specs=[
            pl.BlockSpec(memory_space=pltpu.SMEM),
            whole(ret),
            whole(suffix_out),
            whole(suffix_lse),
            pl.BlockSpec((1, width, depth), lambda t: (t, 0, 0)),
        ],
        out_specs=pl.BlockSpec((1, STEPS * requests, width), lambda t: (t, 0, 0)),
        scratch_shapes=[
            pltpu.VMEM((ret.shape[0], GROUPS * PAD_ROWS, LANES), jnp.float32),
            pltpu.VMEM((total_rows, LANES), jnp.float32),
            pltpu.VMEM((total_rows, LANES), jnp.float32),
            pltpu.VMEM((STEPS * requests, depth), jnp.bfloat16),
        ],
        compiler_params=pltpu.CompilerParams(vmem_limit_bytes=VMEM_LIMIT),
        name="merge",
    )(codes, ret, suffix_out, suffix_lse, weights.reshape(parts, width, depth))


def shards(queries, prefix_cache, suffix_cache, suffix_lengths, request_prefix, prefix_owner, out_proj):
    prefix_size = lax.axis_size("prefix")
    tensor_size = lax.axis_size("tensor")
    z_size = prefix_size // X_SIZE
    x_groups = [[z * X_SIZE + x for x in range(X_SIZE)] for z in range(z_size)]
    z_groups = [[z * X_SIZE + x for z in range(z_size)] for x in range(X_SIZE)]
    me = lax.axis_index("prefix").astype(jnp.int32).reshape(1)
    kv = lax.all_gather(prefix_cache[0, 0], "prefix", axis=0, axis_index_groups=x_groups)
    q3 = queries.transpose(1, 0, 2)
    send, q_rows, codes = route(me, request_prefix.reshape(-1), prefix_owner, q3, z_size)
    recv = lax.all_to_all(
        send, "prefix", split_axis=0, concat_axis=0, axis_index_groups=z_groups, tiled=True
    )
    suffix_rows = suffix_cache[:, 0].transpose(0, 2, 1)
    suffix_out, suffix_lse = suffix_attention(suffix_lengths, q_rows, suffix_rows)
    ret = prefix_attention(me, recv, kv)
    homed = lax.all_to_all(
        ret, "prefix", split_axis=0, concat_axis=0, axis_index_groups=z_groups, tiled=True
    )
    parts = merge_project(codes, homed, suffix_out, suffix_lse, out_proj.T, tensor_size)
    parts = lax.all_to_all(parts, "tensor", split_axis=0, concat_axis=0, tiled=True)
    summed = jnp.sum(parts.astype(jnp.float32), axis=0).astype(jnp.bfloat16)
    return summed.reshape(STEPS, queries.shape[0], -1).transpose(1, 0, 2)


def solution(mesh):
    return jax.shard_map(
        shards,
        mesh=mesh,
        in_specs=(
            P("prefix", None, "tensor"),
            P("prefix", "tensor", None, None),
            P("prefix", "tensor", None, None),
            P("prefix"),
            P(),
            P(),
            P("tensor", None),
        ),
        out_specs=P("prefix", None, "tensor"),
        check_vma=False,
    )
```

time: 493 us -> 148 us (0.30)
  waiting for transfers between devices: 194 us -> 11.7 us
  local copies, waits for them, and re-layouts: 183 us -> 0.75 us
  blocking collectives: 0 us -> 60.9 us
  other arithmetic: 59.1 us -> 0.88 us
  Pallas kernels: 0 us -> 47.3 us
  matrix products: 25.4 us -> 0 us
    unnamed x16 -> x2, local copies, waits for them, and re-layouts: 123 us -> 0.75 us
    all_gather x1, waiting for transfers between devices: 117 us -> 8.96 us  [shards(): lax.all_gather(prefix_cache[0, 0], 'prefix', axis=0, axis_index_groups=x_...]
    all_to_all x0 -> x2, blocking collectives: none -> 60.9 us  [the longest x1 33.9 us: shards(): lax.all_to_all(send, 'prefix', split_axis=0, concat_axis=0, axis_index_gr...]
    pallas_call x0 -> x4, Pallas kernels: none -> 47.3 us  [the longest x1 17.9 us: suffix_attention(): pl.pallas_call(suffix_kernel, grid=(requests // SUFFIX_BLOCK,), out_shape...]
    all_to_all x2 -> x1, waiting for transfers between devices: 40.3 us -> 2.06 us  [shards(): lax.all_to_all(ret, 'prefix', split_axis=0, concat_axis=0, axis_index_gro...]
    mul x1 -> x0, other arithmetic: 36.3 us -> none  [shards(): codes = destination * capacity + rank]
    unnamed x3 -> x1, waiting for transfers between devices: 35.9 us -> 0.71 us
    dot_general x11 -> x0, matrix products: 25.4 us -> none  [the longest x5 11.8 us: softmax_partial(): jnp.einsum(form, weight.astype(jnp.bfloat16), value_rows, preferred_eleme...]
  transfers between devices with their start and end apart: 4 -> 2, of which waited for: 4 -> 2; matrix products, arithmetic and copies ran while one was open for 14% -> 0% of each run, Pallas kernels for 0% -> 16%
where the time goes in v1:
time: 148 us; the launch traced here: 147 us
  blocking collectives  60.9 us (41%)
  Pallas kernels  47.3 us (32%)
  between operations  13.4 us (9%)
  starting transfers between devices  12 us (8%)
  waiting for transfers between devices  11.7 us (8%)
    all_to_all x1, blocking collectives, shards(): lax.all_to_all(send, 'prefix', split_axis=0, concat_axis=0, axis_index_gr...  33.9 us
    all_to_all x1, blocking collectives, shards(): lax.all_to_all(parts, 'tensor', split_axis=0, concat_axis=0, tiled=True)  27 us
    pallas_call x1, Pallas kernels, suffix_attention(): pl.pallas_call(suffix_kernel, grid=(requests // SUFFIX_BLOCK,), out_shape...  17.9 us
    pallas_call x1, Pallas kernels, prefix_attention(): pl.pallas_call(prefix_kernel, out_shape=jax.ShapeDtypeStruct((z_size, out...  15.7 us
    all_to_all x1, starting transfers between devices, shards(): lax.all_to_all(ret, 'prefix', split_axis=0, concat_axis=0, axis_index_gro...  12 us
    all_gather x1, waiting for transfers between devices, shards(): lax.all_gather(prefix_cache[0, 0], 'prefix', axis=0, axis_index_groups=x_...  8.96 us
    pallas_call x1, Pallas kernels, merge_project(): pl.pallas_call(merge_kernel, grid=(parts,), out_shape=jax.ShapeDtypeStruc...  8.34 us
    pallas_call x1, Pallas kernels, route(): pl.pallas_call(route_kernel, out_shape=(jax.ShapeDtypeStruct((z_size, GRO...  5.37 us
  transfers between devices with their start and end apart: 2, of which 2 were waited for; matrix products, arithmetic and copies ran while one was open for 0% of the time, Pallas kernels for 16%

profile of v1, /device:TPU:1, one launch (start us, length us, event | category | flops | bytes accessed | tf_op | source)
XLA Modules:
  0.0 147.0 jit_solution(14610014516949313809)
XLA Ops:
  6.5 0.0 all-gather.3.cloned.1.call-start
  6.5 0.7 all-gather.3.cloned.1.call-update
  7.3 5.4 %route.1 = (bf16[16,96,128]{2,1,0:T(8,128)(2,1)}, bf16[1024,128]{1,0:T(8,128)(2,1)}, s32[64]{0:T(128)}) custom-call(s32[1]{0:T(128)} %bitcast.me_ref, s32[4096]{0:T(1024)} %bitcast.15, s32[64]{0:T(128)} %owner_ref.1, bf16[3,64,512]{2,1,0:T(8,128)(2,1)} %bitcast.14), custom_call_target="tpu_custom_call" | custom-call | tf_op jit(solution)/shard_map/route/pallas_call | solution.py:98
  12.6 33.9 %all_to_all.15.recv_ref = bf16[16,96,128]{2,1,0:T(8,128)(2,1)} all-to-all(bf16[16,96,128]{2,1,0:T(8,128)(2,1)} %get-tuple-element.11), channel_id=1, replica_groups={{0,32,64,96,128,160,192,224,256,288,320,352,384,416,448,480},{8,40,72,1..., dimensions={0} | all-to-all | bytes 786432 | tf_op jit(solution)/shard_map/all_to_all | solution.py:357
  46.5 9.0 %all-gather.3.cloned.1.call-done = bf16[4,1,128,2304]{3,2,1,0:T(8,128)(2,1)} async-done(((bf16[1,1,128,2304]{3,2,1,0:T(8,128)(2,1)}), bf16[4,1,128,2304]{3,2,1,0:T(8,128)(2,1)}) %all-gather.3.cloned.1.call-update) | async-done | bytes 2359312 | tf_op jit(solution)/shard_map/all_gather | solution.py:354
  55.5 15.7 %prefix.1 = bf16[16,104,128]{2,1,0:T(8,128)(2,1)} custom-call(s32[1]{0:T(128)} %bitcast.me_ref, bf16[16,96,128]{2,1,0:T(8,128)(2,1)} %all_to_all.15.recv_ref, bf16[4,128,2304]{2,1,0:T(8,128)(2,1)} %bitcast.16), custom_call_target="tpu_custom_call" | custom-call | flops 8000000000 | bytes 4000000 | tf_op jit(solution)/shard_map/prefix/pallas_call | solution.py:239
  71.2 12.0 %all-to-all-start.1 = ((bf16[16,104,128]{2,1,0:T(8,128)(2,1)}), bf16[16,104,128]{2,1,0:T(8,128)(2,1)S(1)}, u32[]{:S(2)}, u32[]{:S(2)}) async-start(bf16[16,104,128]{2,1,0:T(8,128)(2,1)} %prefix.1), calls=%async_computation.1 | async-start | bytes 851968 | tf_op jit(solution)/shard_map/all_to_all | solution.py:363
  83.2 17.9 %suffix.1 = (f32[1024,128]{1,0:T(8,128)}, f32[1024,128]{1,0:T(8,128)}) custom-call(s32[64]{0:T(128)} %length_ref.1, bf16[1024,128]{1,0:T(8,128)(2,1)} %get-tuple-element.12.q_ref, bf16[64,80,128]{2,1,0:T(8,128)(2,1)} %bitcast.17), custom_call_target="tpu_custom_call" | custom-call | flops 671088640 | bytes 8000000 | tf_op jit(solution)/shard_map/suffix/pallas_call | solution.py:151
  101.1 2.1 %all-to-all-done.1.ret_ref = bf16[16,104,128]{2,1,0:T(8,128)(2,1)S(1)} async-done(((bf16[16,104,128]{2,1,0:T(8,128)(2,1)}), bf16[16,104,128]{2,1,0:T(8,128)(2,1)S(1)}, u32[]{:S(2)}, u32[]{:S(2)}) %all-to-all-start.1) | async-done | bytes 426016 | tf_op jit(solution)/shard_map/all_to_all | solution.py:363
  103.1 0.0 copy-start
  103.1 0.8 copy-done
  103.9 8.3 %merge.1 = bf16[8,192,360]{2,1,0:T(8,128)(2,1)} custom-call(s32[64]{0:T(128)} %get-tuple-element.10.code_ref, bf16[16,104,128]{2,1,0:T(8,128)(2,1)} %copy-done, f32[1024,128]{1,0:T(8,128)} %get-tuple-element.13.suffix_ref, f32[1024,128]{1,0:T(8,128)} %get-tuple-element.14.suffix_lse_ref, bf16[8,360,512]{2,1,0:T(8,128)(2,1)} %bitcast.13), custom_call_target="tpu_custom_call" | custom-call | tf_op jit(solution)/shard_map/merge/pallas_call | solution.py:324
  112.2 27.0 %all_to_all.16 = bf16[8,192,360]{2,1,0:T(8,128)(2,1)S(1)} all-to-all(bf16[8,192,360]{2,1,0:T(8,128)(2,1)} %merge.1), channel_id=1, replica_groups=mesh['prefix'=64,'tensor'=8] {'tensor'}, dimensions={0} | all-to-all | bytes 2211840 | tf_op jit(solution)/shard_map/all_to_all | solution.py:367
  139.2 0.9 reduce_sum.12
Async XLA Ops:
  6.5 48.9 %all-gather.3.cloned.1.call-start = ((), (), s32[]{:S(2)}) async-start(), calls=%async_computation.3 | async-start | bytes 2949120 | tf_op jit(solution)/shard_map/all_gather | solution.py:354
  71.2 31.9 %all-to-all-start.1 = ((bf16[16,104,128]{2,1,0:T(8,128)(2,1)}), bf16[16,104,128]{2,1,0:T(8,128)(2,1)S(1)}, u32[]{:S(2)}, u32[]{:S(2)}) async-start(bf16[16,104,128]{2,1,0:T(8,128)(2,1)} %prefix.1), calls=%async_computation.1 | async-start | bytes 851968 | tf_op jit(solution)/shard_map/all_to_all | solution.py:363
  103.1 0.8 copy-start
Sparse Core Ops, SparseCore 0:
  9.5 45.9 all-gather.2

commit v2 on v1

v2 whole, which is shorter than its diff:
```python
import functools

import jax
import jax.numpy as jnp
from jax import lax
from jax.experimental import pallas as pl
from jax.experimental.pallas import tpu as pltpu
from jax.sharding import PartitionSpec as P

LANES = 128
HALF = 64
X_SIZE = 4
CORES = 2
CAPACITY = 2
GROUPS = X_SIZE * CAPACITY
STEPS = 3
ROWS = 12
PAD_ROWS = 16
SCALE = 0.125
VMEM_LIMIT = 56 * 1024 * 1024


def lane_iota(rows):
    return lax.broadcasted_iota(jnp.int32, (rows, LANES), 1)


def split_heads(rows):
    low = lane_iota(rows.shape[0]) < HALF
    even = jnp.where(low, rows, 0.0)
    odd = jnp.where(low, pltpu.roll(rows, HALF, 1), 0.0)
    return even, odd


def join_heads(even, odd):
    low = lane_iota(even.shape[0]) < HALF
    return jnp.where(low, pltpu.roll(even, HALF, 1), odd)


def nt_dot(left, right):
    return lax.dot_general(
        left, right, (((1,), (1,)), ((), ())), preferred_element_type=jnp.float32
    )


def spread_queries(q_ref, qs):
    requests = q_ref.shape[1]
    for i in range(PAD_ROWS):
        if i < ROWS:
            step, pair = divmod(i, ROWS // STEPS)
            value = q_ref[step, :, pair * LANES : (pair + 1) * LANES].astype(jnp.float32)
        else:
            value = jnp.zeros((requests, LANES), jnp.float32)
        qs[pl.ds(i, requests, stride=PAD_ROWS), :] = value


def route_kernel(me_ref, prefix_ref, owner_ref, q_ref, send_ref, code_ref, taken, source, qs, acc):
    requests = q_ref.shape[1]
    z_size = send_ref.shape[0]
    me = me_ref[0]
    x_own = me & (X_SIZE - 1)
    for i in range(owner_ref.shape[0]):
        taken[i] = 0
    for i in range(z_size * GROUPS):
        source[i] = 0

    def place(r, _):
        name = prefix_ref[me * requests + r]
        owner = owner_ref[name]
        rank = taken[name]
        taken[name] = rank + 1
        offset = (owner - x_own) & (X_SIZE - 1)
        code = (owner >> 2) * GROUPS + offset * CAPACITY + rank
        code_ref[r] = code
        source[code] = r
        return 0

    lax.fori_loop(0, requests, place, 0, unroll=8)
    spread_queries(q_ref, qs)

    def fill(z, _):
        for slot in range(GROUPS):
            r = source[z * GROUPS + slot]
            block = qs[pl.ds(pl.multiple_of(r * PAD_ROWS, PAD_ROWS), PAD_ROWS), :]
            acc[z, slot * ROWS : (slot + 1) * ROWS, :] = block[:ROWS]
        return 0

    lax.fori_loop(0, z_size, fill, 0, unroll=4)
    send_ref[...] = acc[...].astype(jnp.bfloat16)


def route(me, prefixes, owner, q3, z_size):
    requests = q3.shape[1]
    smem = pl.BlockSpec(memory_space=pltpu.SMEM)
    vmem = pl.BlockSpec(memory_space=pltpu.VMEM)
    shape = (z_size, GROUPS * ROWS, LANES)
    return pl.pallas_call(
        route_kernel,
        out_shape=(
            jax.ShapeDtypeStruct(shape, jnp.bfloat16),
            jax.ShapeDtypeStruct((requests,), jnp.int32),
        ),
        in_specs=[smem, smem, smem, vmem],
        out_specs=(vmem, smem),
        scratch_shapes=[
            pltpu.SMEM((owner.shape[0],), jnp.int32),
            pltpu.SMEM((z_size * GROUPS,), jnp.int32),
            pltpu.VMEM((requests * PAD_ROWS, LANES), jnp.float32),
            pltpu.VMEM(shape, jnp.float32),
        ],
        compiler_params=pltpu.CompilerParams(vmem_limit_bytes=VMEM_LIMIT),
        name="route",
    )(me, prefixes, owner, q3)


SUFFIX_BLOCK = 4


def suffix_kernel(length_ref, q_ref, kv_ref, out_ref, lse_ref, qs):
    spread_queries(q_ref, qs)
    requests, positions, _ = kv_ref.shape
    rows = SUFFIX_BLOCK * PAD_ROWS
    shape = (2 * rows, SUFFIX_BLOCK * positions)
    row = lax.broadcasted_iota(jnp.int32, shape, 0) % rows
    request = row // PAD_ROWS
    step = row % PAD_ROWS // (ROWS // STEPS)
    place = lax.broadcasted_iota(jnp.int32, shape, 1) - request * positions
    past = jnp.where(place >= 0, place - step, 2 * positions)
    request_rows = lax.broadcasted_iota(jnp.int32, (2 * rows, 1), 0) % rows // PAD_ROWS
    low = lane_iota(rows) < HALF

    def some(i, _):
        here = pl.ds(pl.multiple_of(i * rows, rows), rows)
        even, odd = split_heads(qs[here, :] * SCALE)
        query = jnp.concatenate([even, odd], axis=0).astype(jnp.bfloat16)
        cache = kv_ref[pl.ds(i * SUFFIX_BLOCK, SUFFIX_BLOCK)].reshape(-1, LANES)
        limit = jnp.zeros((2 * rows, 1), jnp.int32)
        for r in range(SUFFIX_BLOCK):
            limit = jnp.where(request_rows == r, length_ref[i * SUFFIX_BLOCK + r] - (STEPS - 1), limit)
        scores = jnp.where(past < limit, nt_dot(query, cache), -jnp.inf)
        highest = jnp.max(scores, axis=1, keepdims=True)
        weight = jnp.exp(scores - highest)
        total = jnp.sum(weight, axis=1, keepdims=True)
        mixed = jnp.dot(weight.astype(jnp.bfloat16), cache, preferred_element_type=jnp.float32)
        mixed = mixed / total
        lse = highest + jnp.log(total)
        out_ref[here, :] = join_heads(mixed[:rows], mixed[rows:])
        lse_ref[here, :] = jnp.where(low, lse[:rows], lse[rows:])
        return 0

    lax.fori_loop(0, requests // SUFFIX_BLOCK, some, 0, unroll=2)


def suffix_attention(lengths, q3, kv):
    requests = kv.shape[0]
    vmem = pl.BlockSpec(memory_space=pltpu.VMEM)
    shape = jax.ShapeDtypeStruct((requests * PAD_ROWS, LANES), jnp.float32)
    return pl.pallas_call(
        suffix_kernel,
        out_shape=(shape, shape),
        in_specs=[pl.BlockSpec(memory_space=pltpu.SMEM), vmem, vmem],
        out_specs=(vmem, vmem),
        scratch_shapes=[pltpu.VMEM((requests * PAD_ROWS, LANES), jnp.float32)],
        compiler_params=pltpu.CompilerParams(vmem_limit_bytes=VMEM_LIMIT),
        cost_estimate=pl.CostEstimate(
            flops=8_000_000_000, bytes_accessed=8_000_000, transcendentals=0
        ),
        name="suffix",
    )(lengths, q3, kv)


CHUNKS = 2


def prefix_kernel(me_ref, recv_ref, kv_ref, ret_ref, values, queries, acc):
    group = pl.program_id(0)
    z_size = recv_ref.shape[0]
    span = CAPACITY * ROWS
    rows = z_size * span

    @pl.when(group == 0)
    def _():
        queries[...] = recv_ref[...].astype(jnp.float32) * SCALE
        values[HALF:, :] = jnp.ones_like(values[HALF:, :])

    values[:HALF, :] = kv_ref[0, HALF:]
    place = pl.ds(pl.multiple_of(group * span, 8), span)
    query = jnp.concatenate(split_heads(queries[:, place, :].reshape(rows, LANES)), axis=0)
    query = query.astype(jnp.bfloat16)
    size = 2 * rows // CHUNKS
    scores, weights, mixes = [None] * CHUNKS, [None] * CHUNKS, []
    for stage in range(CHUNKS + 2):
        if stage < CHUNKS:
            here = query[stage * size : (stage + 1) * size]
            scores[stage] = jnp.dot(here, kv_ref[0], preferred_element_type=jnp.float32)
        if stage >= 2:
            weight, highest = weights[stage - 2]
            mixed = nt_dot(weight, values[...])
            low = lane_iota(size) < HALF
            total = jnp.where(low, pltpu.roll(mixed, HALF, 1), mixed)
            mixes.append((mixed / total, highest + jnp.log(total)))
        if 1 <= stage <= CHUNKS:
            highest = jnp.max(scores[stage - 1], axis=1, keepdims=True)
            weight = jnp.exp(scores[stage - 1] - highest).astype(jnp.bfloat16)
            weights[stage - 1] = (weight, highest)
    half = CHUNKS // 2
    low = lane_iota(size) < HALF
    lse = []
    for i in range(half):
        out = jnp.where(low, mixes[i][0], pltpu.roll(mixes[i + half][0], HALF, 1))
        sources = slice(i * z_size // half, (i + 1) * z_size // half)
        acc[sources, place, :] = out.reshape(z_size // half, span, LANES)
        lse.append(jnp.where(low, mixes[i][1], mixes[i + half][1]))
    lse = jnp.concatenate(lse, axis=0)
    lane = lax.broadcasted_iota(jnp.int32, (span, LANES), 1) & (HALF - 1)
    row = lax.broadcasted_iota(jnp.int32, (span, LANES), 0)
    row = jnp.where(row < ROWS, row, row - ROWS)
    high_part = lse.astype(jnp.bfloat16).astype(jnp.float32)
    rest = lse - high_part
    mid_part = rest.astype(jnp.bfloat16).astype(jnp.float32)
    packed = jnp.zeros((z_size, span, LANES), jnp.float32)
    for i, part in enumerate((high_part, mid_part, rest - mid_part)):
        part = part.reshape(z_size, span, LANES)
        packed = jnp.where((lane == row + i * ROWS)[None], part, packed)
    packed = packed.reshape(rows, LANES).astype(jnp.bfloat16)
    shape = (z_size * GROUPS, rows)
    slot = lax.broadcasted_iota(jnp.int32, shape, 0)
    inside = (slot & (GROUPS - 1)) // CAPACITY == group
    slot = slot // GROUPS * CAPACITY + (slot & (CAPACITY - 1))
    first = lax.broadcasted_iota(jnp.int32, shape, 1) - slot * ROWS
    pick = jnp.logical_and(inside, jnp.logical_and(first >= 0, first < ROWS))
    lse_rows = jnp.dot(pick.astype(jnp.bfloat16), packed, preferred_element_type=jnp.float32)
    lse_rows = lse_rows.reshape(z_size, GROUPS, LANES)
    own = lax.broadcasted_iota(jnp.int32, (GROUPS, LANES), 0) // CAPACITY == group
    acc[:, GROUPS * ROWS :, :] = jnp.where(own[None], lse_rows, acc[:, GROUPS * ROWS :, :])

    @pl.when(group == pl.num_programs(0) - 1)
    def _():
        ret_ref[...] = acc[...].astype(jnp.bfloat16)


def prefix_attention(me, recv, kv):
    z_size = recv.shape[0]
    length = kv.shape[2]
    whole = lambda *shape: pl.BlockSpec(shape, lambda g, me: (0,) * len(shape))
    out_rows = GROUPS * ROWS + GROUPS
    return pl.pallas_call(
        prefix_kernel,
        out_shape=jax.ShapeDtypeStruct((z_size, out_rows, LANES), jnp.bfloat16),
        grid_spec=pltpu.PrefetchScalarGridSpec(
            num_scalar_prefetch=1,
            grid=(X_SIZE,),
            in_specs=[
                whole(*recv.shape),
                pl.BlockSpec((1, LANES, length), lambda g, me: ((me[0] + g) % X_SIZE, 0, 0)),
            ],
            out_specs=whole(z_size, out_rows, LANES),
            scratch_shapes=[
                pltpu.VMEM((LANES, length), jnp.bfloat16),
                pltpu.VMEM(recv.shape, jnp.float32),
                pltpu.VMEM((z_size, out_rows, LANES), jnp.float32),
            ],
        ),
        compiler_params=pltpu.CompilerParams(vmem_limit_bytes=VMEM_LIMIT),
        cost_estimate=pl.CostEstimate(
            flops=8_000_000_000, bytes_accessed=4_000_000, transcendentals=0
        ),
        name="prefix",
    )(me, recv, kv)


def merge_kernel(code_ref, ret_ref, suffix_ref, suffix_lse_ref, w_ref, out_ref, wide, picked, packed, merged, left):
    requests = code_ref.shape[0]

    @pl.when(pl.program_id(0) == 0)
    def _():
        wide[...] = ret_ref[...].astype(jnp.float32)
        pair_rows = CAPACITY * ROWS
        for r in range(requests):
            code = code_ref[r]
            z, slot = code // GROUPS, code % GROUPS
            start = pl.multiple_of(slot // CAPACITY * pair_rows, 8)
            pair = wide[z, pl.ds(start, pair_rows), :]
            second = jnp.concatenate([pair[ROWS:], pair[: PAD_ROWS - ROWS]], axis=0)
            picked[r] = jnp.where(slot % CAPACITY == 0, pair[:PAD_ROWS], second)
            packed[r : r + 1, :] = wide[z, pl.ds(GROUPS * ROWS + slot, 1), :]
        lane = lane_iota(PAD_ROWS) % HALF
        row = lax.broadcasted_iota(jnp.int32, (PAD_ROWS, LANES), 0)
        own = jnp.logical_or(lane == row, jnp.logical_or(lane == row + ROWS, lane == row + 2 * ROWS))
        own = jnp.logical_and(own, row < ROWS)
        copies = jnp.where(own[None], packed[...][:, None, :], 0.0).astype(jnp.bfloat16)
        same_half = lax.broadcasted_iota(jnp.int32, (LANES, LANES), 0) // HALF
        same_half = same_half == lane_iota(LANES) // HALF
        prefix_lse = jnp.dot(
            copies.reshape(requests * PAD_ROWS, LANES),
            same_half.astype(jnp.bfloat16),
            preferred_element_type=jnp.float32,
        )
        gap = prefix_lse - suffix_lse_ref[...]
        small = jnp.exp(-jnp.abs(gap))
        large_weight = 1.0 / (1.0 + small)
        small_weight = small * large_weight
        prefix_first = gap >= 0.0
        merged[...] = picked[...].reshape(requests * PAD_ROWS, LANES) * jnp.where(
            prefix_first, large_weight, small_weight
        ) + suffix_ref[...] * jnp.where(prefix_first, small_weight, large_weight)
        pairs = ROWS // STEPS
        for step in range(STEPS):
            for pair in range(pairs):
                left[step * requests : (step + 1) * requests, pair * LANES : (pair + 1) * LANES] = merged[
                    pl.ds(step * pairs + pair, requests, stride=PAD_ROWS), :
                ].astype(jnp.bfloat16)

    for core in range(CORES):
        out_ref[core, 0] = nt_dot(left[...], w_ref[core]).astype(jnp.bfloat16)


def merge_project(codes, ret, suffix_out, suffix_lse, weights, parts):
    requests = codes.shape[0]
    width = weights.shape[0] // parts
    depth = weights.shape[1]
    whole = lambda array: pl.BlockSpec(array.shape, lambda t: (0,) * array.ndim)
    return pl.pallas_call(
        merge_kernel,
        grid=(parts // CORES,),
        out_shape=jax.ShapeDtypeStruct((CORES, parts // CORES, STEPS * requests, width), jnp.bfloat16),
        in_specs=[
            pl.BlockSpec(memory_space=pltpu.SMEM),
            whole(ret),
            whole(suffix_out),
            whole(suffix_lse),
            pl.BlockSpec((CORES, width, depth), lambda t: (t, 0, 0)),
        ],
        out_specs=pl.BlockSpec((CORES, 1, STEPS * requests, width), lambda t: (0, t, 0, 0)),
        scratch_shapes=[
            pltpu.VMEM(ret.shape, jnp.float32),
            pltpu.VMEM((requests, PAD_ROWS, LANES), jnp.float32),
            pltpu.VMEM((requests, LANES), jnp.float32),
            pltpu.VMEM((requests * PAD_ROWS, LANES), jnp.float32),
            pltpu.VMEM((STEPS * requests, depth), jnp.bfloat16),
        ],
        compiler_params=pltpu.CompilerParams(vmem_limit_bytes=VMEM_LIMIT),
        name="merge",
    )(codes, ret, suffix_out, suffix_lse, weights.reshape(parts, width, depth))


def shards(queries, prefix_cache, suffix_cache, suffix_lengths, request_prefix, prefix_owner, out_proj):
    prefix_size = lax.axis_size("prefix")
    tensor_size = lax.axis_size("tensor")
    z_size = prefix_size // X_SIZE
    x_groups = [[z * X_SIZE + x for x in range(X_SIZE)] for z in range(z_size)]
    z_groups = [[z * X_SIZE + x for z in range(z_size)] for x in range(X_SIZE)]
    me = lax.axis_index("prefix").astype(jnp.int32).reshape(1)
    kv = lax.all_gather(prefix_cache[0, 0], "prefix", axis=0, axis_index_groups=x_groups)
    q3 = queries.transpose(1, 0, 2)
    send, codes = route(me, request_prefix.reshape(-1), prefix_owner, q3, z_size)
    recv = lax.all_to_all(
        send, "prefix", split_axis=0, concat_axis=0, axis_index_groups=z_groups, tiled=True
    )
    suffix_rows = suffix_cache[:, 0].transpose(0, 2, 1)
    suffix_out, suffix_lse = suffix_attention(suffix_lengths, q3, suffix_rows)
    recv, suffix_out, suffix_lse = lax.optimization_barrier((recv, suffix_out, suffix_lse))
    ret = prefix_attention(me, recv, kv)
    homed = lax.all_to_all(
        ret, "prefix", split_axis=0, concat_axis=0, axis_index_groups=z_groups, tiled=True
    )
    parts = merge_project(codes, homed, suffix_out, suffix_lse, out_proj.T, tensor_size)
    y_size = tensor_size // CORES
    core_groups = [[y * CORES + c for c in range(CORES)] for y in range(y_size)]
    y_groups = [[y * CORES + c for y in range(y_size)] for c in range(CORES)]
    for groups in (core_groups, y_groups):
        parts = lax.all_to_all(
            parts, "tensor", split_axis=0, concat_axis=0, axis_index_groups=groups, tiled=True
        )
        parts = jnp.sum(parts.astype(jnp.float32), axis=0).astype(jnp.bfloat16)
    return parts.reshape(STEPS, queries.shape[0], -1).transpose(1, 0, 2)


def solution(mesh):
    return jax.shard_map(
        shards,
        mesh=mesh,
        in_specs=(
            P("prefix", None, "tensor"),
            P("prefix", "tensor", None, None),
            P("prefix", "tensor", None, None),
            P("prefix"),
            P(),
            P(),
            P("tensor", None),
        ),
        out_specs=P("prefix", None, "tensor"),
        check_vma=False,
    )
```

time: 148 us -> 139 us (0.939)
  Pallas kernels: 47.3 us -> 29.5 us
  waiting for transfers between devices: 11.7 us -> 21.8 us
  blocking collectives: 60.9 us -> 56.9 us
  starting transfers between devices: 12 us -> 15.8 us
    pallas_call x3, Pallas kernels: 31.6 us -> 17.4 us  [the longest x1 8.73 us: suffix_attention(): pl.pallas_call(suffix_kernel, out_shape=(shape, shape), in_specs=[pl.Bloc...]
    all_to_all x1, waiting for transfers between devices: 2.06 us -> 9.28 us  [shards(): lax.all_to_all(send, 'prefix', split_axis=0, concat_axis=0, axis_index_gr...]
    all_to_all x2 -> x3, blocking collectives: 60.9 us -> 56.9 us  [the longest x1 31.9 us: shards(): lax.all_to_all(ret, 'prefix', split_axis=0, concat_axis=0, axis_index_gro...]
    all_to_all x1, starting transfers between devices: 12 us -> 15.8 us  [shards(): lax.all_to_all(send, 'prefix', split_axis=0, concat_axis=0, axis_index_gr...]
    pallas_call x1, Pallas kernels: 15.7 us -> 12.1 us  [prefix_attention(): pl.pallas_call(prefix_kernel, out_shape=jax.ShapeDtypeStruct((z_size, out...]
    all_gather x1, waiting for transfers between devices: 8.96 us -> 11.8 us  [shards(): lax.all_gather(prefix_cache[0, 0], 'prefix', axis=0, axis_index_groups=x_...]
  transfers between devices with their start and end apart: 2 -> 2, of which waited for: 2 -> 2; matrix products, arithmetic and copies ran while one was open for 0% -> 0% of each run, Pallas kernels for 16% -> 8%
where the time goes in v2:
time: 139 us
  blocking collectives  56.9 us (41%)
  Pallas kernels  29.5 us (21%)
  waiting for transfers between devices  21.8 us (16%)
  starting transfers between devices  15.8 us (11%)
  between operations  13.4 us (10%)
    all_to_all x1, blocking collectives, shards(): lax.all_to_all(ret, 'prefix', split_axis=0, concat_axis=0, axis_index_gro...  31.9 us
    all_to_all x2, blocking collectives, shards(): lax.all_to_all(parts, 'tensor', split_axis=0, concat_axis=0, axis_index_g...  25 us
    all_to_all x1, starting transfers between devices, shards(): lax.all_to_all(send, 'prefix', split_axis=0, concat_axis=0, axis_index_gr...  15.8 us
    pallas_call x1, Pallas kernels, prefix_attention(): pl.pallas_call(prefix_kernel, out_shape=jax.ShapeDtypeStruct((z_size, out...  12.1 us
    all_gather x1, waiting for transfers between devices, shards(): lax.all_gather(prefix_cache[0, 0], 'prefix', axis=0, axis_index_groups=x_...  11.8 us
    all_to_all x1, waiting for transfers between devices, shards(): lax.all_to_all(send, 'prefix', split_axis=0, concat_axis=0, axis_index_gr...  9.28 us
    pallas_call x1, Pallas kernels, suffix_attention(): pl.pallas_call(suffix_kernel, out_shape=(shape, shape), in_specs=[pl.Bloc...  8.73 us
    pallas_call x1, Pallas kernels, merge_project(): pl.pallas_call(merge_kernel, grid=(parts // CORES,), out_shape=jax.ShapeD...  6 us
  transfers between devices with their start and end apart: 2, of which 2 were waited for; matrix products, arithmetic and copies ran while one was open for 0% of the time, Pallas kernels for 8%

profile of v2, /device:TPU:1, one launch (start us, length us, event | category | flops | bytes accessed | tf_op | source)
XLA Modules:
  0.0 138.7 jit_solution(5389561121171704913)
XLA Ops:
  6.5 0.0 all-gather.3.cloned.1.call-start
  6.5 0.7 all-gather.3.cloned.1.call-update
  7.3 2.6 %route.1 = (bf16[16,96,128]{2,1,0:T(8,128)(2,1)}, s32[64]{0:T(128)}) custom-call(s32[1]{0:T(128)} %bitcast.me_ref, s32[4096]{0:T(1024)} %bitcast.16, s32[64]{0:T(128)} %owner_ref.1, bf16[3,64,512]{2,1,0:T(8,128)(2,1)} %bitcast.14), custom_call_target="tpu_custom_call" | custom-call | tf_op jit(solution)/shard_map/route/pallas_call | solution.py:96
  9.9 15.8 %all-to-all-start = ((bf16[16,96,128]{2,1,0:T(8,128)(2,1)}), bf16[16,96,128]{2,1,0:T(8,128)(2,1)S(1)}, u32[]{:S(2)}, u32[]{:S(2)}) async-start(bf16[16,96,128]{2,1,0:T(8,128)(2,1)} %get-tuple-element.13), calls=%async_computation | async-start | bytes 786432 | tf_op jit(solution)/shard_map/all_to_all | solution.py:356
  25.7 8.7 %suffix.1 = (f32[1024,128]{1,0:T(8,128)}, f32[1024,128]{1,0:T(8,128)}) custom-call(s32[64]{0:T(128)} %length_ref.1, bf16[3,64,512]{2,1,0:T(8,128)(2,1)} %bitcast.15, bf16[64,80,128]{2,1,0:T(8,128)(2,1)} %bitcast.18), custom_call_target="tpu_custom_call" | custom-call | flops 8000000000 | bytes 8000000 | tf_op jit(solution)/shard_map/suffix/pallas_call | solution.py:157
  34.4 9.3 %all-to-all-done.recv_ref = bf16[16,96,128]{2,1,0:T(8,128)(2,1)S(1)} async-done(((bf16[16,96,128]{2,1,0:T(8,128)(2,1)}), bf16[16,96,128]{2,1,0:T(8,128)(2,1)S(1)}, u32[]{:S(2)}, u32[]{:S(2)}) %all-to-all-start) | async-done | bytes 393248 | tf_op jit(solution)/shard_map/all_to_all | solution.py:356
  43.7 0.0 copy-start
  43.7 11.8 %all-gather.3.cloned.1.call-done = bf16[4,1,128,2304]{3,2,1,0:T(8,128)(2,1)} async-done(((bf16[1,1,128,2304]{3,2,1,0:T(8,128)(2,1)}), bf16[4,1,128,2304]{3,2,1,0:T(8,128)(2,1)}) %all-gather.3.cloned.1.call-update) | async-done | bytes 2359312 | tf_op jit(solution)/shard_map/all_gather | solution.py:353
  55.5 0.0 copy-done
  55.5 12.1 %prefix.1 = bf16[16,104,128]{2,1,0:T(8,128)(2,1)} custom-call(s32[1]{0:T(128)} %bitcast.me_ref, bf16[16,96,128]{2,1,0:T(8,128)(2,1)} %copy-done, bf16[4,128,2304]{2,1,0:T(8,128)(2,1)} %bitcast.17), custom_call_target="tpu_custom_call" | custom-call | flops 8000000000 | bytes 4000000 | tf_op jit(solution)/shard_map/prefix/pallas_call | solution.py:246
  67.6 31.9 %all_to_all.20.ret_ref = bf16[16,104,128]{2,1,0:T(8,128)(2,1)} all-to-all(bf16[16,104,128]{2,1,0:T(8,128)(2,1)} %prefix.1), channel_id=1, replica_groups={{0,32,64,96,128,160,192,224,256,288,320,352,384,416,448,480},{8,40,72,1..., dimensions={0} | all-to-all | bytes 851968 | tf_op jit(solution)/shard_map/all_to_all | solution.py:363
  99.5 6.0 %merge.1 = bf16[2,4,192,360]{3,2,1,0:T(8,128)(2,1)} custom-call(s32[64]{0:T(128)} %get-tuple-element.12.code_ref, bf16[16,104,128]{2,1,0:T(8,128)(2,1)} %all_to_all.20.ret_ref, f32[1024,128]{1,0:T(8,128)} %get-tuple-element.17.suffix_ref, f32[1024,128]{1,0:T(8,128)} %get-tuple-element.18.suffix_lse_ref, bf16[8,360,512]{2,1,0:T(8,128)(2,1)} %bitcast.13), custom_call_target="tpu_custom_call" | custom-call | tf_op jit(solution)/shard_map/merge/pallas_call | solution.py:322
  105.5 11.5 %all_to_all.21 = bf16[2,4,192,360]{3,2,1,0:T(8,128)(2,1)S(1)} all-to-all(bf16[2,4,192,360]{3,2,1,0:T(8,128)(2,1)} %merge.1), channel_id=1, replica_groups={{0,1},{2,3},{4,5},{6,7},{8,9},{10,11},{12,13},{14,15},{16,17},{18,19},{..., dimensions={0} | all-to-all | bytes 2211840 | tf_op jit(solution)/shard_map/all_to_all | solution.py:371
  117.0 0.5 reduce_sum.24
  117.6 13.5 %all_to_all.22 = bf16[4,192,360]{2,1,0:T(8,128)(2,1)S(1)} all-to-all(bf16[4,192,360]{2,1,0:T(8,128)(2,1)S(1)} %reduce_sum.24), channel_id=1, replica_groups={{0,2,4,6},{1,3,5,7},{8,10,12,14},{9,11,13,15},{16,18,20,22},{17,19,21,2..., dimensions={0} | all-to-all | bytes 1105920 | tf_op jit(solution)/shard_map/all_to_all | solution.py:371
  131.1 0.8 reduce_sum.25
Async XLA Ops:
  6.5 48.9 %all-gather.3.cloned.1.call-start = ((), (), s32[]{:S(2)}) async-start(), calls=%async_computation.4 | async-start | bytes 2949120 | tf_op jit(solution)/shard_map/all_gather | solution.py:353
  9.9 33.8 %all-to-all-start = ((bf16[16,96,128]{2,1,0:T(8,128)(2,1)}), bf16[16,96,128]{2,1,0:T(8,128)(2,1)S(1)}, u32[]{:S(2)}, u32[]{:S(2)}) async-start(bf16[16,96,128]{2,1,0:T(8,128)(2,1)} %get-tuple-element.13), calls=%async_computation | async-start | bytes 786432 | tf_op jit(solution)/shard_map/all_to_all | solution.py:356
  43.7 11.8 %copy-start = (bf16[16,96,128]{2,1,0:T(8,128)(2,1)}, bf16[16,96,128]{2,1,0:T(8,128)(2,1)S(1)}, u32[]{:S(2)}) copy-start(bf16[16,96,128]{2,1,0:T(8,128)(2,1)S(1)} %all-to-all-done.recv_ref) | copy-start | bytes 1179652
Sparse Core Ops, SparseCore 0:
  9.5 45.9 all-gather.2

commit v3 on v2

--- a/solution.py
+++ b/solution.py
@@ -9,10 +9,8 @@
 
 LANES = 128
 HALF = 64
-X_SIZE = 4
 CORES = 2
 CAPACITY = 2
-GROUPS = X_SIZE * CAPACITY
 STEPS = 3
 ROWS = 12
 PAD_ROWS = 16
@@ -55,21 +53,18 @@
 
 def route_kernel(me_ref, prefix_ref, owner_ref, q_ref, send_ref, code_ref, taken, source, qs, acc):
     requests = q_ref.shape[1]
-    z_size = send_ref.shape[0]
+    owners = send_ref.shape[0]
     me = me_ref[0]
-    x_own = me & (X_SIZE - 1)
-    for i in range(owner_ref.shape[0]):
+    for i in range(owners):
         taken[i] = 0
-    for i in range(z_size * GROUPS):
+    for i in range(owners * CAPACITY):
         source[i] = 0
 
     def place(r, _):
         name = prefix_ref[me * requests + r]
-        owner = owner_ref[name]
         rank = taken[name]
         taken[name] = rank + 1
-        offset = (owner - x_own) & (X_SIZE - 1)
-        code = (owner >> 2) * GROUPS + offset * CAPACITY + rank
+        code = owner_ref[name] * CAPACITY + rank
         code_ref[r] = code
         source[code] = r
         return 0
@@ -77,22 +72,22 @@
     lax.fori_loop(0, requests, place, 0, unroll=8)
     spread_queries(q_ref, qs)
 
-    def fill(z, _):
-        for slot in range(GROUPS):
-            r = source[z * GROUPS + slot]
+    def fill(owner, _):
+        for rank in range(CAPACITY):
+            r = source[owner * CAPACITY + rank]
             block = qs[pl.ds(pl.multiple_of(r * PAD_ROWS, PAD_ROWS), PAD_ROWS), :]
-            acc[z, slot * ROWS : (slot + 1) * ROWS, :] = block[:ROWS]
+            acc[owner, rank * ROWS : (rank + 1) * ROWS, :] = block[:ROWS]
         return 0
 
-    lax.fori_loop(0, z_size, fill, 0, unroll=4)
+    lax.fori_loop(0, owners, fill, 0, unroll=16)
     send_ref[...] = acc[...].astype(jnp.bfloat16)
 
 
-def route(me, prefixes, owner, q3, z_size):
+def route(me, prefixes, owner, q3):
     requests = q3.shape[1]
     smem = pl.BlockSpec(memory_space=pltpu.SMEM)
     vmem = pl.BlockSpec(memory_space=pltpu.VMEM)
-    shape = (z_size, GROUPS * ROWS, LANES)
+    shape = (owner.shape[0], CAPACITY * ROWS, LANES)
     return pl.pallas_call(
         route_kernel,
         out_shape=(
@@ -103,7 +98,7 @@
         out_specs=(vmem, smem),
         scratch_shapes=[
             pltpu.SMEM((owner.shape[0],), jnp.int32),
-            pltpu.SMEM((z_size * GROUPS,), jnp.int32),
+            pltpu.SMEM((owner.shape[0] * CAPACITY,), jnp.int32),
             pltpu.VMEM((requests * PAD_ROWS, LANES), jnp.float32),
             pltpu.VMEM(shape, jnp.float32),
         ],
@@ -168,30 +163,28 @@
     )(lengths, q3, kv)
 
 
+SOURCES = 16
 CHUNKS = 2
 
 
-def prefix_kernel(me_ref, recv_ref, kv_ref, ret_ref, values, queries, acc):
-    group = pl.program_id(0)
-    z_size = recv_ref.shape[0]
+def prefix_kernel(recv_ref, kv_ref, ret_ref, values, acc):
     span = CAPACITY * ROWS
-    rows = z_size * span
-
-    @pl.when(group == 0)
+    rows = SOURCES * span
+
+    @pl.when(pl.program_id(0) == 0)
     def _():
-        queries[...] = recv_ref[...].astype(jnp.float32) * SCALE
+        values[:HALF, :] = kv_ref[HALF:]
         values[HALF:, :] = jnp.ones_like(values[HALF:, :])
-
-    values[:HALF, :] = kv_ref[0, HALF:]
-    place = pl.ds(pl.multiple_of(group * span, 8), span)
-    query = jnp.concatenate(split_heads(queries[:, place, :].reshape(rows, LANES)), axis=0)
-    query = query.astype(jnp.bfloat16)
+        acc[...] = jnp.zeros_like(acc)
+
+    received = recv_ref[...].astype(jnp.float32).reshape(rows, LANES) * SCALE
+    query = jnp.concatenate(split_heads(received), axis=0).astype(jnp.bfloat16)
     size = 2 * rows // CHUNKS
     scores, weights, mixes = [None] * CHUNKS, [None] * CHUNKS, []
     for stage in range(CHUNKS + 2):
         if stage < CHUNKS:
             here = query[stage * size : (stage + 1) * size]
-            scores[stage] = jnp.dot(here, kv_ref[0], preferred_element_type=jnp.float32)
+            scores[stage] = jnp.dot(here, kv_ref[...], preferred_element_type=jnp.float32)
         if stage >= 2:
             weight, highest = weights[stage - 2]
             mixed = nt_dot(weight, values[...])
@@ -202,92 +195,65 @@
             highest = jnp.max(scores[stage - 1], axis=1, keepdims=True)
             weight = jnp.exp(scores[stage - 1] - highest).astype(jnp.bfloat16)
             weights[stage - 1] = (weight, highest)
-    half = CHUNKS // 2
-    low = lane_iota(size) < HALF
-    lse = []
-    for i in range(half):
-        out = jnp.where(low, mixes[i][0], pltpu.roll(mixes[i + half][0], HALF, 1))
-        sources = slice(i * z_size // half, (i + 1) * z_size // half)
-        acc[sources, place, :] = out.reshape(z_size // half, span, LANES)
-        lse.append(jnp.where(low, mixes[i][1], mixes[i + half][1]))
-    lse = jnp.concatenate(lse, axis=0)
+    out, lse = (jnp.concatenate([mix[i] for mix in mixes], axis=0) for i in range(2))
+    low = lane_iota(rows) < HALF
+    out = jnp.where(low, out[:rows], pltpu.roll(out[rows:], HALF, 1)).reshape(SOURCES, span, LANES)
+    lse = jnp.where(low, lse[:rows], lse[rows:])
     lane = lax.broadcasted_iota(jnp.int32, (span, LANES), 1) & (HALF - 1)
     row = lax.broadcasted_iota(jnp.int32, (span, LANES), 0)
     row = jnp.where(row < ROWS, row, row - ROWS)
     high_part = lse.astype(jnp.bfloat16).astype(jnp.float32)
     rest = lse - high_part
     mid_part = rest.astype(jnp.bfloat16).astype(jnp.float32)
-    packed = jnp.zeros((z_size, span, LANES), jnp.float32)
+    packed = jnp.zeros((SOURCES, span, LANES), jnp.float32)
     for i, part in enumerate((high_part, mid_part, rest - mid_part)):
-        part = part.reshape(z_size, span, LANES)
+        part = part.reshape(SOURCES, span, LANES)
         packed = jnp.where((lane == row + i * ROWS)[None], part, packed)
-    packed = packed.reshape(rows, LANES).astype(jnp.bfloat16)
-    shape = (z_size * GROUPS, rows)
-    slot = lax.broadcasted_iota(jnp.int32, shape, 0)
-    inside = (slot & (GROUPS - 1)) // CAPACITY == group
-    slot = slot // GROUPS * CAPACITY + (slot & (CAPACITY - 1))
-    first = lax.broadcasted_iota(jnp.int32, shape, 1) - slot * ROWS
-    pick = jnp.logical_and(inside, jnp.logical_and(first >= 0, first < ROWS))
-    lse_rows = jnp.dot(pick.astype(jnp.bfloat16), packed, preferred_element_type=jnp.float32)
-    lse_rows = lse_rows.reshape(z_size, GROUPS, LANES)
-    own = lax.broadcasted_iota(jnp.int32, (GROUPS, LANES), 0) // CAPACITY == group
-    acc[:, GROUPS * ROWS :, :] = jnp.where(own[None], lse_rows, acc[:, GROUPS * ROWS :, :])
-
-    @pl.when(group == pl.num_programs(0) - 1)
-    def _():
-        ret_ref[...] = acc[...].astype(jnp.bfloat16)
-
-
-def prefix_attention(me, recv, kv):
-    z_size = recv.shape[0]
-    length = kv.shape[2]
-    whole = lambda *shape: pl.BlockSpec(shape, lambda g, me: (0,) * len(shape))
-    out_rows = GROUPS * ROWS + GROUPS
+    for rank in range(CAPACITY):
+        mine = slice(rank * ROWS, (rank + 1) * ROWS)
+        acc[:, rank, :ROWS, :] = out[:, mine, :]
+        acc[:, rank, ROWS : ROWS + 1, :] = jnp.sum(packed[:, mine, :], axis=1, keepdims=True)
+    ret_ref[...] = acc[...].astype(jnp.bfloat16)
+
+
+def prefix_attention(recv, kv):
+    sources = recv.shape[0]
+    length = kv.shape[1]
+    out_block = (SOURCES, CAPACITY, PAD_ROWS, LANES)
     return pl.pallas_call(
         prefix_kernel,
-        out_shape=jax.ShapeDtypeStruct((z_size, out_rows, LANES), jnp.bfloat16),
-        grid_spec=pltpu.PrefetchScalarGridSpec(
-            num_scalar_prefetch=1,
-            grid=(X_SIZE,),
-            in_specs=[
-                whole(*recv.shape),
-                pl.BlockSpec((1, LANES, length), lambda g, me: ((me[0] + g) % X_SIZE, 0, 0)),
-            ],
-            out_specs=whole(z_size, out_rows, LANES),
-            scratch_shapes=[
-                pltpu.VMEM((LANES, length), jnp.bfloat16),
-                pltpu.VMEM(recv.shape, jnp.float32),
-                pltpu.VMEM((z_size, out_rows, LANES), jnp.float32),
-            ],
-        ),
+        grid=(sources // SOURCES,),
+        out_shape=jax.ShapeDtypeStruct((sources,) + out_block[1:], jnp.bfloat16),
+        in_specs=[
+            pl.BlockSpec((SOURCES, CAPACITY * ROWS, LANES), lambda i: (i, 0, 0)),
+            pl.BlockSpec((LANES, length), lambda i: (0, 0)),
+        ],
+        out_specs=pl.BlockSpec(out_block, lambda i: (i, 0, 0, 0)),
+        scratch_shapes=[
+            pltpu.VMEM((LANES, length), jnp.bfloat16),
+            pltpu.VMEM(out_block, jnp.float32),
+        ],
         compiler_params=pltpu.CompilerParams(vmem_limit_bytes=VMEM_LIMIT),
         cost_estimate=pl.CostEstimate(
             flops=8_000_000_000, bytes_accessed=4_000_000, transcendentals=0
         ),
         name="prefix",
-    )(me, recv, kv)
-
-
-def merge_kernel(code_ref, ret_ref, suffix_ref, suffix_lse_ref, w_ref, out_ref, wide, picked, packed, merged, left):
+    )(recv, kv)
+
+
+def merge_kernel(code_ref, ret_ref, suffix_ref, suffix_lse_ref, w_ref, out_ref, picked, merged, left):
     requests = code_ref.shape[0]
 
     @pl.when(pl.program_id(0) == 0)
     def _():
-        wide[...] = ret_ref[...].astype(jnp.float32)
-        pair_rows = CAPACITY * ROWS
         for r in range(requests):
             code = code_ref[r]
-            z, slot = code // GROUPS, code % GROUPS
-            start = pl.multiple_of(slot // CAPACITY * pair_rows, 8)
-            pair = wide[z, pl.ds(start, pair_rows), :]
-            second = jnp.concatenate([pair[ROWS:], pair[: PAD_ROWS - ROWS]], axis=0)
-            picked[r] = jnp.where(slot % CAPACITY == 0, pair[:PAD_ROWS], second)
-            packed[r : r + 1, :] = wide[z, pl.ds(GROUPS * ROWS + slot, 1), :]
+            picked[r] = ret_ref[code].astype(jnp.float32)
         lane = lane_iota(PAD_ROWS) % HALF
         row = lax.broadcasted_iota(jnp.int32, (PAD_ROWS, LANES), 0)
         own = jnp.logical_or(lane == row, jnp.logical_or(lane == row + ROWS, lane == row + 2 * ROWS))
         own = jnp.logical_and(own, row < ROWS)
-        copies = jnp.where(own[None], packed[...][:, None, :], 0.0).astype(jnp.bfloat16)
+        copies = jnp.where(own[None], picked[:, ROWS : ROWS + 1, :], 0.0).astype(jnp.bfloat16)
         same_half = lax.broadcasted_iota(jnp.int32, (LANES, LANES), 0) // HALF
         same_half = same_half == lane_iota(LANES) // HALF
         prefix_lse = jnp.dot(
@@ -332,9 +298,7 @@
         ],
         out_specs=pl.BlockSpec((CORES, 1, STEPS * requests, width), lambda t: (0, t, 0, 0)),
         scratch_shapes=[
-            pltpu.VMEM(ret.shape, jnp.float32),
             pltpu.VMEM((requests, PAD_ROWS, LANES), jnp.float32),
-            pltpu.VMEM((requests, LANES), jnp.float32),
             pltpu.VMEM((requests * PAD_ROWS, LANES), jnp.float32),
             pltpu.VMEM((STEPS * requests, depth), jnp.bfloat16),
         ],
@@ -344,25 +308,18 @@
 
 
 def shards(queries, prefix_cache, suffix_cache, suffix_lengths, request_prefix, prefix_owner, out_proj):
-    prefix_size = lax.axis_size("prefix")
     tensor_size = lax.axis_size("tensor")
-    z_size = prefix_size // X_SIZE
-    x_groups = [[z * X_SIZE + x for x in range(X_SIZE)] for z in range(z_size)]
-    z_groups = [[z * X_SIZE + x for z in range(z_size)] for x in range(X_SIZE)]
     me = lax.axis_index("prefix").astype(jnp.int32).reshape(1)
-    kv = lax.all_gather(prefix_cache[0, 0], "prefix", axis=0, axis_index_groups=x_groups)
     q3 = queries.transpose(1, 0, 2)
-    send, codes = route(me, request_prefix.reshape(-1), prefix_owner, q3, z_size)
-    recv = lax.all_to_all(
-        send, "prefix", split_axis=0, concat_axis=0, axis_index_groups=z_groups, tiled=True
-    )
+    send, codes = route(me, request_prefix.reshape(-1), prefix_owner, q3)
+    recv = lax.all_to_all(send, "prefix", split_axis=0, concat_axis=0, tiled=True)
     suffix_rows = suffix_cache[:, 0].transpose(0, 2, 1)
     suffix_out, suffix_lse = suffix_attention(suffix_lengths, q3, suffix_rows)
     recv, suffix_out, suffix_lse = lax.optimization_barrier((recv, suffix_out, suffix_lse))
-    ret = prefix_attention(me, recv, kv)
-    homed = lax.all_to_all(
-        ret, "prefix", split_axis=0, concat_axis=0, axis_index_groups=z_groups, tiled=True
-    )
+    ret = prefix_attention(recv, prefix_cache[0, 0])
+    ret = ret.reshape(ret.shape[0], CAPACITY * PAD_ROWS, LANES)
+    homed = lax.all_to_all(ret, "prefix", split_axis=0, concat_axis=0, tiled=True)
+    homed = homed.reshape(-1, PAD_ROWS, LANES)
     parts = merge_project(codes, homed, suffix_out, suffix_lse, out_proj.T, tensor_size)
     y_size = tensor_size // CORES
     core_groups = [[y * CORES + c for c in range(CORES)] for y in range(y_size)]

time: 139 us -> 127 us (0.914)
  between operations: 13.4 us -> 0.03 us
  waiting for transfers between devices: 21.8 us -> 16.1 us
  blocking collectives: 56.9 us -> 60.4 us
  starting transfers between devices: 15.8 us -> 19.1 us
    all_gather x1 -> x0, waiting for transfers between devices: 11.8 us -> none  [shards(): lax.all_gather(prefix_cache[0, 0], 'prefix', axis=0, axis_index_groups=x_...]
    all_to_all x1, waiting for transfers between devices: 9.28 us -> 16.1 us  [shards(): lax.all_to_all(send, 'prefix', split_axis=0, concat_axis=0, tiled=True)]
    all_to_all x1, blocking collectives: 31.9 us -> 36.9 us  [shards(): lax.all_to_all(ret, 'prefix', split_axis=0, concat_axis=0, tiled=True)]
    all_to_all x1, starting transfers between devices: 15.8 us -> 19.1 us  [shards(): lax.all_to_all(send, 'prefix', split_axis=0, concat_axis=0, tiled=True)]
    all_to_all x2, blocking collectives: 25 us -> 23.5 us  [shards(): lax.all_to_all(parts, 'tensor', split_axis=0, concat_axis=0, axis_index_g...]
  transfers between devices with their start and end apart: 2 -> 1, of which waited for: 2 -> 1; matrix products, arithmetic and copies ran while one was open for 0% -> 0% of each run, Pallas kernels for 8% -> 7%
where the time goes in v3:
time: 127 us; the launch traced here: 126 us
  blocking collectives  60.4 us (48%)
  Pallas kernels  28.4 us (22%)
  starting transfers between devices  19.1 us (15%)
  waiting for transfers between devices  16.1 us (13%)
  other arithmetic  1.3 us (1%)
    all_to_all x1, blocking collectives, shards(): lax.all_to_all(ret, 'prefix', split_axis=0, concat_axis=0, tiled=True)  36.9 us
    all_to_all x2, blocking collectives, shards(): lax.all_to_all(parts, 'tensor', split_axis=0, concat_axis=0, axis_index_g...  23.5 us
    all_to_all x1, starting transfers between devices, shards(): lax.all_to_all(send, 'prefix', split_axis=0, concat_axis=0, tiled=True)  19.1 us
    all_to_all x1, waiting for transfers between devices, shards(): lax.all_to_all(send, 'prefix', split_axis=0, concat_axis=0, tiled=True)  16.1 us
    pallas_call x1, Pallas kernels, prefix_attention(): pl.pallas_call(prefix_kernel, grid=(sources // SOURCES,), out_shape=jax.S...  11.5 us
    pallas_call x1, Pallas kernels, suffix_attention(): pl.pallas_call(suffix_kernel, out_shape=(shape, shape), in_specs=[pl.Bloc...  8.77 us
    pallas_call x1, Pallas kernels, merge_project(): pl.pallas_call(merge_kernel, grid=(parts // CORES,), out_shape=jax.ShapeD...  5.56 us
    pallas_call x1, Pallas kernels, route(): pl.pallas_call(route_kernel, out_shape=(jax.ShapeDtypeStruct(shape, jnp.b...  2.54 us
  transfers between devices with their start and end apart: 1, of which 1 were waited for; matrix products, arithmetic and copies ran while one was open for 0% of the time, Pallas kernels for 7%

profile of v3, /device:TPU:1, one launch (start us, length us, event | category | flops | bytes accessed | tf_op | source)
XLA Modules:
  0.0 126.1 jit_solution(8376066538730411931)
XLA Ops:
  0.0 2.5 %route.1 = (bf16[64,24,128]{2,1,0:T(8,128)(2,1)}, s32[64]{0:T(128)}) custom-call(s32[1]{0:T(128)} %bitcast.me_ref, s32[4096]{0:T(1024)} %bitcast.20, s32[64]{0:T(128)} %owner_ref.1, bf16[3,64,512]{2,1,0:T(8,128)(2,1)} %bitcast.18), custom_call_target="tpu_custom_call" | custom-call | tf_op jit(solution)/shard_map/route/pallas_call | solution.py:91
  2.6 19.1 %all-to-all-start = ((bf16[64,24,128]{2,1,0:T(8,128)(2,1)}), bf16[64,24,128]{2,1,0:T(8,128)(2,1)S(1)}, u32[]{:S(2)}, u32[]{:S(2)}) async-start(bf16[64,24,128]{2,1,0:T(8,128)(2,1)} %get-tuple-element.13), calls=%async_computation | async-start | bytes 786432 | tf_op jit(solution)/shard_map/all_to_all | solution.py:315
  21.7 8.8 %suffix.1 = (f32[1024,128]{1,0:T(8,128)}, f32[1024,128]{1,0:T(8,128)}) custom-call(s32[64]{0:T(128)} %length_ref.1, bf16[3,64,512]{2,1,0:T(8,128)(2,1)} %bitcast.19, bf16[64,80,128]{2,1,0:T(8,128)(2,1)} %bitcast.21), custom_call_target="tpu_custom_call" | custom-call | flops 8000000000 | bytes 8000000 | tf_op jit(solution)/shard_map/suffix/pallas_call | solution.py:152
  30.5 16.1 %all-to-all-done.recv_ref = bf16[64,24,128]{2,1,0:T(8,128)(2,1)S(1)} async-done(((bf16[64,24,128]{2,1,0:T(8,128)(2,1)}), bf16[64,24,128]{2,1,0:T(8,128)(2,1)S(1)}, u32[]{:S(2)}, u32[]{:S(2)}) %all-to-all-start) | async-done | bytes 393248 | tf_op jit(solution)/shard_map/all_to_all | solution.py:315
  46.6 0.0 copy-start
  46.6 0.8 copy-done
  47.4 11.5 %prefix.1 = bf16[64,2,16,128]{3,2,1,0:T(8,128)(2,1)} custom-call(bf16[64,24,128]{2,1,0:T(8,128)(2,1)} %copy-done, bf16[128,2304]{1,0:T(8,128)(2,1)} %bitcast.22), custom_call_target="tpu_custom_call" | custom-call | flops 8000000000 | bytes 4000000 | tf_op jit(solution)/shard_map/prefix/pallas_call | solution.py:223
  58.9 36.9 %all_to_all.20 = bf16[64,32,128]{2,1,0:T(8,128)(2,1)} all-to-all(bf16[64,32,128]{2,1,0:T(8,128)(2,1)} %bitcast.17), channel_id=1, replica_groups=mesh['prefix'=64,'tensor'=8] {'prefix'}, dimensions={0} | all-to-all | bytes 1048576 | tf_op jit(solution)/shard_map/all_to_all | solution.py:321
  95.7 5.6 %merge.1 = bf16[2,4,192,360]{3,2,1,0:T(8,128)(2,1)} custom-call(s32[64]{0:T(128)} %get-tuple-element.12.code_ref, bf16[128,16,128]{2,1,0:T(8,128)(2,1)} %bitcast.16, f32[1024,128]{1,0:T(8,128)} %get-tuple-element.17.suffix_ref, f32[1024,128]{1,0:T(8,128)} %get-tuple-element.18.suffix_lse_ref, bf16[8,360,512]{2,1,0:T(8,128)(2,1)} %bitcast.15), custom_call_target="tpu_custom_call" | custom-call | tf_op jit(solution)/shard_map/merge/pallas_call | solution.py:288
  101.3 9.9 %all_to_all.21 = bf16[2,4,192,360]{3,2,1,0:T(8,128)(2,1)S(1)} all-to-all(bf16[2,4,192,360]{3,2,1,0:T(8,128)(2,1)} %merge.1), channel_id=1, replica_groups={{0,1},{2,3},{4,5},{6,7},{8,9},{10,11},{12,13},{14,15},{16,17},{18,19},{..., dimensions={0} | all-to-all | bytes 2211840 | tf_op jit(solution)/shard_map/all_to_all | solution.py:328
  111.2 0.5 reduce_sum.24
  111.7 13.6 %all_to_all.22 = bf16[4,192,360]{2,1,0:T(8,128)(2,1)S(1)} all-to-all(bf16[4,192,360]{2,1,0:T(8,128)(2,1)S(1)} %reduce_sum.24), channel_id=1, replica_groups={{0,2,4,6},{1,3,5,7},{8,10,12,14},{9,11,13,15},{16,18,20,22},{17,19,21,2..., dimensions={0} | all-to-all | bytes 1105920 | tf_op jit(solution)/shard_map/all_to_all | solution.py:328
  125.3 0.8 reduce_sum.25
Async XLA Ops:
  2.6 44.0 %all-to-all-start = ((bf16[64,24,128]{2,1,0:T(8,128)(2,1)}), bf16[64,24,128]{2,1,0:T(8,128)(2,1)S(1)}, u32[]{:S(2)}, u32[]{:S(2)}) async-start(bf16[64,24,128]{2,1,0:T(8,128)(2,1)} %get-tuple-element.13), calls=%async_computation | async-start | bytes 786432 | tf_op jit(solution)/shard_map/all_to_all | solution.py:315
  46.6 0.8 copy-start

commit v4 on v2

--- a/solution.py
+++ b/solution.py
@@ -69,7 +69,7 @@
         rank = taken[name]
         taken[name] = rank + 1
         offset = (owner - x_own) & (X_SIZE - 1)
-        code = (owner >> 2) * GROUPS + offset * CAPACITY + rank
+        code = (owner >> 2) * GROUPS + (offset ^ (offset >> 1)) * CAPACITY + rank
         code_ref[r] = code
         source[code] = r
         return 0
@@ -169,20 +169,32 @@
 
 
 CHUNKS = 2
-
-
-def prefix_kernel(me_ref, recv_ref, kv_ref, ret_ref, values, queries, acc):
-    group = pl.program_id(0)
+OFFSETS = (0, 1, 3, 2)
+
+
+def prefix_kernel(first, count, *refs):
+    recv_ref, sources = refs[0], refs[1 : 1 + count]
+    before = refs[1 + count : len(refs) - 6]
+    ret_ref, cache, values, queries, acc, sems = refs[-6:]
+    index = pl.program_id(0)
+    group = index + first
     z_size = recv_ref.shape[0]
     span = CAPACITY * ROWS
     rows = z_size * span
-
-    @pl.when(group == 0)
+    copies = [pltpu.make_async_copy(sources[i], cache.at[i], sems.at[i]) for i in range(count)]
+
+    @pl.when(index == 0)
     def _():
+        for copy in copies:
+            copy.start()
         queries[...] = recv_ref[...].astype(jnp.float32) * SCALE
         values[HALF:, :] = jnp.ones_like(values[HALF:, :])
-
-    values[:HALF, :] = kv_ref[0, HALF:]
+        if before:
+            acc[...] = before[0][...].astype(jnp.float32)
+
+    for i in range(count):
+        pl.when(index == i)(copies[i].wait)
+    values[:HALF, :] = cache[index, HALF:]
     place = pl.ds(pl.multiple_of(group * span, 8), span)
     query = jnp.concatenate(split_heads(queries[:, place, :].reshape(rows, LANES)), axis=0)
     query = query.astype(jnp.bfloat16)
@@ -191,7 +203,7 @@
     for stage in range(CHUNKS + 2):
         if stage < CHUNKS:
             here = query[stage * size : (stage + 1) * size]
-            scores[stage] = jnp.dot(here, kv_ref[0], preferred_element_type=jnp.float32)
+            scores[stage] = jnp.dot(here, cache[index], preferred_element_type=jnp.float32)
         if stage >= 2:
             weight, highest = weights[stage - 2]
             mixed = nt_dot(weight, values[...])
@@ -233,39 +245,36 @@
     own = lax.broadcasted_iota(jnp.int32, (GROUPS, LANES), 0) // CAPACITY == group
     acc[:, GROUPS * ROWS :, :] = jnp.where(own[None], lse_rows, acc[:, GROUPS * ROWS :, :])
 
-    @pl.when(group == pl.num_programs(0) - 1)
+    @pl.when(index == count - 1)
     def _():
         ret_ref[...] = acc[...].astype(jnp.bfloat16)
 
 
-def prefix_attention(me, recv, kv):
+def prefix_attention(recv, caches, first, before=()):
     z_size = recv.shape[0]
-    length = kv.shape[2]
-    whole = lambda *shape: pl.BlockSpec(shape, lambda g, me: (0,) * len(shape))
-    out_rows = GROUPS * ROWS + GROUPS
+    count = len(caches)
+    length = caches[0].shape[1]
+    out_shape = (z_size, GROUPS * ROWS + GROUPS, LANES)
+    vmem = pl.BlockSpec(memory_space=pltpu.VMEM)
     return pl.pallas_call(
-        prefix_kernel,
-        out_shape=jax.ShapeDtypeStruct((z_size, out_rows, LANES), jnp.bfloat16),
-        grid_spec=pltpu.PrefetchScalarGridSpec(
-            num_scalar_prefetch=1,
-            grid=(X_SIZE,),
-            in_specs=[
-                whole(*recv.shape),
-                pl.BlockSpec((1, LANES, length), lambda g, me: ((me[0] + g) % X_SIZE, 0, 0)),
-            ],
-            out_specs=whole(z_size, out_rows, LANES),
-            scratch_shapes=[
-                pltpu.VMEM((LANES, length), jnp.bfloat16),
-                pltpu.VMEM(recv.shape, jnp.float32),
-                pltpu.VMEM((z_size, out_rows, LANES), jnp.float32),
-            ],
-        ),
+        functools.partial(prefix_kernel, first, count),
+        grid=(count,),
+        out_shape=jax.ShapeDtypeStruct(out_shape, jnp.bfloat16),
+        in_specs=[vmem] + [pl.BlockSpec(memory_space=pl.ANY)] * count + [vmem] * len(before),
+        out_specs=vmem,
+        scratch_shapes=[
+            pltpu.VMEM((count, LANES, length), jnp.bfloat16),
+            pltpu.VMEM((LANES, length), jnp.bfloat16),
+            pltpu.VMEM(recv.shape, jnp.float32),
+            pltpu.VMEM(out_shape, jnp.float32),
+            pltpu.SemaphoreType.DMA((count,)),
+        ],
         compiler_params=pltpu.CompilerParams(vmem_limit_bytes=VMEM_LIMIT),
         cost_estimate=pl.CostEstimate(
-            flops=8_000_000_000, bytes_accessed=4_000_000, transcendentals=0
+            flops=2_500_000_000 * count, bytes_accessed=1_000_000 * count, transcendentals=0
         ),
         name="prefix",
-    )(me, recv, kv)
+    )(recv, *caches, *before)
 
 
 def merge_kernel(code_ref, ret_ref, suffix_ref, suffix_lse_ref, w_ref, out_ref, wide, picked, packed, merged, left):
@@ -347,19 +356,28 @@
     prefix_size = lax.axis_size("prefix")
     tensor_size = lax.axis_size("tensor")
     z_size = prefix_size // X_SIZE
-    x_groups = [[z * X_SIZE + x for x in range(X_SIZE)] for z in range(z_size)]
     z_groups = [[z * X_SIZE + x for z in range(z_size)] for x in range(X_SIZE)]
     me = lax.axis_index("prefix").astype(jnp.int32).reshape(1)
-    kv = lax.all_gather(prefix_cache[0, 0], "prefix", axis=0, axis_index_groups=x_groups)
+    kv = prefix_cache[0, 0]
     q3 = queries.transpose(1, 0, 2)
     send, codes = route(me, request_prefix.reshape(-1), prefix_owner, q3, z_size)
+    kv_out, send = lax.optimization_barrier((kv, send))
+    caches = [kv]
+    for offset in OFFSETS[1:]:
+        pairs = [
+            (z * X_SIZE + (x + offset) % X_SIZE, z * X_SIZE + x)
+            for z in range(z_size)
+            for x in range(X_SIZE)
+        ]
+        caches.append(lax.ppermute(kv_out, "prefix", pairs))
     recv = lax.all_to_all(
         send, "prefix", split_axis=0, concat_axis=0, axis_index_groups=z_groups, tiled=True
     )
     suffix_rows = suffix_cache[:, 0].transpose(0, 2, 1)
     suffix_out, suffix_lse = suffix_attention(suffix_lengths, q3, suffix_rows)
     recv, suffix_out, suffix_lse = lax.optimization_barrier((recv, suffix_out, suffix_lse))
-    ret = prefix_attention(me, recv, kv)
+    ret = prefix_attention(recv, caches[:3], 0)
+    ret = prefix_attention(recv, caches[3:], 3, (ret,))
     homed = lax.all_to_all(
         ret, "prefix", split_axis=0, concat_axis=0, axis_index_groups=z_groups, tiled=True
     )

time: 139 us -> 128 us (0.921); the launches traced: 139 us -> 126 us
  waiting for transfers between devices: 21.8 us -> 3.49 us
  between operations: 13.4 us -> 0.1 us
  starting transfers between devices: 15.8 us -> 25.7 us
  Pallas kernels: 29.5 us -> 33.2 us
  blocking collectives: 56.9 us -> 60.5 us
  local copies, waits for them, and re-layouts: 0.01 us -> 1.64 us
    all_gather x1 -> x0, waiting for transfers between devices: 11.8 us -> none  [shards(): lax.all_gather(prefix_cache[0, 0], 'prefix', axis=0, axis_index_groups=x_...]
    ppermute x0 -> x3, starting transfers between devices: none -> 9.94 us  [shards(): caches.append(lax.ppermute(kv_out, 'prefix', pairs))]
    all_to_all x1, waiting for transfers between devices: 9.28 us -> 0.01 us  [shards(): lax.all_to_all(send, 'prefix', split_axis=0, concat_axis=0, axis_index_gr...]
    all_to_all x2, blocking collectives: 25 us -> 34.3 us  [shards(): lax.all_to_all(parts, 'tensor', split_axis=0, concat_axis=0, axis_index_g...]
    all_to_all x1, blocking collectives: 31.9 us -> 26.3 us  [shards(): lax.all_to_all(ret, 'prefix', split_axis=0, concat_axis=0, axis_index_gro...]
    pallas_call x1 -> x2, Pallas kernels: 12.1 us -> 15.8 us  [prefix_attention(): pl.pallas_call(functools.partial(prefix_kernel, first, count), grid=(coun...]
    ppermute x0 -> x3, waiting for transfers between devices: none -> 3.49 us  [shards(): caches.append(lax.ppermute(kv_out, 'prefix', pairs))]
    unnamed x2 -> x8, local copies, waits for them, and re-layouts: 0.01 us -> 1.64 us
  transfers between devices with their start and end apart: 2 -> 4, of which waited for: 2 -> 1; matrix products, arithmetic and copies ran while one was open for 0% -> 0% of each run, Pallas kernels for 8% -> 15%
where the time goes in v4:
time: 128 us; the launch traced here: 126 us
  blocking collectives  60.5 us (47%)
  Pallas kernels  33.2 us (26%)
  starting transfers between devices  25.7 us (20%)
  waiting for transfers between devices  3.49 us (3%)
  local copies, waits for them, and re-layouts  1.64 us (1%)
  other arithmetic  1.3 us (1%)
    all_to_all x2, blocking collectives, shards(): lax.all_to_all(parts, 'tensor', split_axis=0, concat_axis=0, axis_index_g...  34.3 us
    all_to_all x1, blocking collectives, shards(): lax.all_to_all(ret, 'prefix', split_axis=0, concat_axis=0, axis_index_gro...  26.3 us
    pallas_call x2, Pallas kernels, prefix_attention(): pl.pallas_call(functools.partial(prefix_kernel, first, count), grid=(coun...  15.8 us
    all_to_all x1, starting transfers between devices, shards(): lax.all_to_all(send, 'prefix', split_axis=0, concat_axis=0, axis_index_gr...  15.8 us
    ppermute x3, starting transfers between devices, shards(): caches.append(lax.ppermute(kv_out, 'prefix', pairs))  9.94 us
    pallas_call x1, Pallas kernels, suffix_attention(): pl.pallas_call(suffix_kernel, out_shape=(shape, shape), in_specs=[pl.Bloc...  8.76 us
    pallas_call x1, Pallas kernels, merge_project(): pl.pallas_call(merge_kernel, grid=(parts // CORES,), out_shape=jax.ShapeD...  5.99 us
    ppermute x3, waiting for transfers between devices, shards(): caches.append(lax.ppermute(kv_out, 'prefix', pairs))  3.49 us
  transfers between devices with their start and end apart: 4, of which 1 were waited for; matrix products, arithmetic and copies ran while one was open for 0% of the time, Pallas kernels for 15%

profile of v4, /device:TPU:1, one launch (start us, length us, event | category | flops | bytes accessed | tf_op | source)
XLA Modules:
  0.0 126.0 jit_solution(2733519250861026676)
XLA Ops:
  0.0 2.6 %route.1 = (bf16[16,96,128]{2,1,0:T(8,128)(2,1)}, s32[64]{0:T(128)}) custom-call(s32[1]{0:T(128)} %bitcast.me_ref, s32[4096]{0:T(1024)} %bitcast.16, s32[64]{0:T(128)} %owner_ref.1, bf16[3,64,512]{2,1,0:T(8,128)(2,1)} %bitcast.14), custom_call_target="tpu_custom_call" | custom-call | tf_op jit(solution)/shard_map/route/pallas_call | solution.py:96
  2.6 15.8 %all-to-all-start = ((bf16[16,96,128]{2,1,0:T(8,128)(2,1)}), bf16[16,96,128]{2,1,0:T(8,128)(2,1)S(1)}, u32[]{:S(2)}, u32[]{:S(2)}) async-start(bf16[16,96,128]{2,1,0:T(8,128)(2,1)} %get-tuple-element.16), calls=%async_computation | async-start | bytes 786432 | tf_op jit(solution)/shard_map/all_to_all | solution.py:373
  18.4 4.4 %collective-permute-start.1 = (bf16[128,2304]{1,0:T(8,128)(2,1)}, bf16[128,2304]{1,0:T(8,128)(2,1)S(1)}, u32[]{:S(2)}, u32[]{:S(2)}) collective-permute-start(bf16[128,2304]{1,0:T(8,128)(2,1)} %bitcast.18), channel_id=1, source_target_pairs={{8,0},{16,8},{24,16},{0,24},{40,32},{48,40},{56,48},{32,56},{72,64... | collective-permute-start | bytes 1769480 | tf_op jit(solution)/shard_map/ppermute | solution.py:372
  22.8 1.9 %collective-permute-start.2 = (bf16[128,2304]{1,0:T(8,128)(2,1)}, bf16[128,2304]{1,0:T(8,128)(2,1)S(1)}, u32[]{:S(2)}, u32[]{:S(2)}) collective-permute-start(bf16[128,2304]{1,0:T(8,128)(2,1)} %bitcast.19), channel_id=1, source_target_pairs={{24,0},{0,8},{8,16},{16,24},{56,32},{32,40},{40,48},{48,56},{88,64... | collective-permute-start | bytes 1769480 | tf_op jit(solution)/shard_map/ppermute | solution.py:372
  24.7 3.6 %collective-permute-start = (bf16[128,2304]{1,0:T(8,128)(2,1)}, bf16[128,2304]{1,0:T(8,128)(2,1)S(1)}, u32[]{:S(2)}, u32[]{:S(2)}) collective-permute-start(bf16[128,2304]{1,0:T(8,128)(2,1)} %bitcast.20), channel_id=1, source_target_pairs={{16,0},{24,8},{0,16},{8,24},{48,32},{56,40},{32,48},{40,56},{80,64... | collective-permute-start | bytes 1769480 | tf_op jit(solution)/shard_map/ppermute | solution.py:372
  28.4 8.8 %suffix.1 = (f32[1024,128]{1,0:T(8,128)}, f32[1024,128]{1,0:T(8,128)}) custom-call(s32[64]{0:T(128)} %length_ref.1, bf16[3,64,512]{2,1,0:T(8,128)(2,1)} %bitcast.15, bf16[64,80,128]{2,1,0:T(8,128)(2,1)} %bitcast.17), custom_call_target="tpu_custom_call" | custom-call | flops 8000000000 | bytes 8000000 | tf_op jit(solution)/shard_map/suffix/pallas_call | solution.py:157
  37.1 0.0 all-to-all-done.refs_0_
  37.1 0.0 copy-start
  37.1 0.0 collective-permute-done.1.refs_2_
  37.2 0.0 copy-start.1
  37.2 3.5 %collective-permute-done.2.refs_3_ = bf16[128,2304]{1,0:T(8,128)(2,1)S(1)} collective-permute-done((bf16[128,2304]{1,0:T(8,128)(2,1)}, bf16[128,2304]{1,0:T(8,128)(2,1)S(1)}, u32[]{:S(2)}, u32[]{:S(2)}) %collective-permute-start.2) | collective-permute-done | bytes 589856 | tf_op jit(solution)/shard_map/ppermute | solution.py:372
  40.6 0.0 copy-done
  40.6 0.0 copy-done.1
  40.7 0.0 copy-start.3
  40.7 0.8 copy-done.3
  41.5 10.4 %prefix.2.refs_2_ = bf16[16,104,128]{2,1,0:T(8,128)(2,1)} custom-call(bf16[16,96,128]{2,1,0:T(8,128)(2,1)} %copy-done, bf16[128,2304]{1,0:T(8,128)(2,1)} %bitcast.21, bf16[128,2304]{1,0:T(8,128)(2,1)} %copy-done.1, bf16[128,2304]{1,0:T(8,128)(2,1)} %copy-done.3), custom_call_target="tpu_custom_call" | custom-call | flops 7500000256 | bytes 3000000 | tf_op jit(solution)/shard_map/prefix/pallas_call | solution.py:259
  51.9 0.0 collective-permute-done.refs_1_
  51.9 0.0 copy-start.2
  51.9 0.8 copy-done.2
  52.7 5.4 %prefix.3 = bf16[16,104,128]{2,1,0:T(8,128)(2,1)} custom-call(bf16[16,96,128]{2,1,0:T(8,128)(2,1)} %copy-done, bf16[128,2304]{1,0:T(8,128)(2,1)} %copy-done.2, bf16[16,104,128]{2,1,0:T(8,128)(2,1)} %prefix.2.refs_2_), custom_call_target="tpu_custom_call" | custom-call | flops 2500000000 | bytes 1000000 | tf_op jit(solution)/shard_map/prefix/pallas_call | solution.py:259
  58.2 26.3 %all_to_all.20.ret_ref = bf16[16,104,128]{2,1,0:T(8,128)(2,1)} all-to-all(bf16[16,104,128]{2,1,0:T(8,128)(2,1)} %prefix.3), channel_id=1, replica_groups={{0,32,64,96,128,160,192,224,256,288,320,352,384,416,448,480},{8,40,72,1..., dimensions={0} | all-to-all | bytes 851968 | tf_op jit(solution)/shard_map/all_to_all | solution.py:381
  84.4 6.0 %merge.1 = bf16[2,4,192,360]{3,2,1,0:T(8,128)(2,1)} custom-call(s32[64]{0:T(128)} %get-tuple-element.14.code_ref, bf16[16,104,128]{2,1,0:T(8,128)(2,1)} %all_to_all.20.ret_ref, f32[1024,128]{1,0:T(8,128)} %get-tuple-element.21.suffix_ref, f32[1024,128]{1,0:T(8,128)} %get-tuple-element.22.suffix_lse_ref, bf16[8,360,512]{2,1,0:T(8,128)(2,1)} %bitcast.13), custom_call_target="tpu_custom_call" | custom-call | tf_op jit(solution)/shard_map/merge/pallas_call | solution.py:331
  90.4 20.7 %all_to_all.21 = bf16[2,4,192,360]{3,2,1,0:T(8,128)(2,1)S(1)} all-to-all(bf16[2,4,192,360]{3,2,1,0:T(8,128)(2,1)} %merge.1), channel_id=1, replica_groups={{0,1},{2,3},{4,5},{6,7},{8,9},{10,11},{12,13},{14,15},{16,17},{18,19},{..., dimensions={0} | all-to-all | bytes 2211840 | tf_op jit(solution)/shard_map/all_to_all | solution.py:389
  111.1 0.5 reduce_sum.24
  111.6 13.6 %all_to_all.22 = bf16[4,192,360]{2,1,0:T(8,128)(2,1)S(1)} all-to-all(bf16[4,192,360]{2,1,0:T(8,128)(2,1)S(1)} %reduce_sum.24), channel_id=1, replica_groups={{0,2,4,6},{1,3,5,7},{8,10,12,14},{9,11,13,15},{16,18,20,22},{17,19,21,2..., dimensions={0} | all-to-all | bytes 1105920 | tf_op jit(solution)/shard_map/all_to_all | solution.py:389
  125.2 0.8 reduce_sum.25
Async XLA Ops:
  2.6 34.5 %all-to-all-start = ((bf16[16,96,128]{2,1,0:T(8,128)(2,1)}), bf16[16,96,128]{2,1,0:T(8,128)(2,1)S(1)}, u32[]{:S(2)}, u32[]{:S(2)}) async-start(bf16[16,96,128]{2,1,0:T(8,128)(2,1)} %get-tuple-element.16), calls=%async_computation | async-start | bytes 786432 | tf_op jit(solution)/shard_map/all_to_all | solution.py:373
  18.4 18.7 %collective-permute-start.1 = (bf16[128,2304]{1,0:T(8,128)(2,1)}, bf16[128,2304]{1,0:T(8,128)(2,1)S(1)}, u32[]{:S(2)}, u32[]{:S(2)}) collective-permute-start(bf16[128,2304]{1,0:T(8,128)(2,1)} %bitcast.18), channel_id=1, source_target_pairs={{8,0},{16,8},{24,16},{0,24},{40,32},{48,40},{56,48},{32,56},{72,64... | collective-permute-start | bytes 1769480 | tf_op jit(solution)/shard_map/ppermute | solution.py:372
  22.8 17.8 %collective-permute-start.2 = (bf16[128,2304]{1,0:T(8,128)(2,1)}, bf16[128,2304]{1,0:T(8,128)(2,1)S(1)}, u32[]{:S(2)}, u32[]{:S(2)}) collective-permute-start(bf16[128,2304]{1,0:T(8,128)(2,1)} %bitcast.19), channel_id=1, source_target_pairs={{24,0},{0,8},{8,16},{16,24},{56,32},{32,40},{40,48},{48,56},{88,64... | collective-permute-start | bytes 1769480 | tf_op jit(solution)/shard_map/ppermute | solution.py:372
  24.7 27.1 %collective-permute-start = (bf16[128,2304]{1,0:T(8,128)(2,1)}, bf16[128,2304]{1,0:T(8,128)(2,1)S(1)}, u32[]{:S(2)}, u32[]{:S(2)}) collective-permute-start(bf16[128,2304]{1,0:T(8,128)(2,1)} %bitcast.20), channel_id=1, source_target_pairs={{16,0},{24,8},{0,16},{8,24},{48,32},{56,40},{32,48},{40,56},{80,64... | collective-permute-start | bytes 1769480 | tf_op jit(solution)/shard_map/ppermute | solution.py:372
  37.1 3.5 %copy-start = (bf16[16,96,128]{2,1,0:T(8,128)(2,1)}, bf16[16,96,128]{2,1,0:T(8,128)(2,1)S(1)}, u32[]{:S(2)}) copy-start(bf16[16,96,128]{2,1,0:T(8,128)(2,1)S(1)} %all-to-all-done.refs_0_) | copy-start | bytes 1179652
  37.2 3.5 %copy-start.1 = (bf16[128,2304]{1,0:T(8,128)(2,1)}, bf16[128,2304]{1,0:T(8,128)(2,1)S(1)}, u32[]{:S(2)}) copy-start(bf16[128,2304]{1,0:T(8,128)(2,1)S(1)} %collective-permute-done.1.refs_2_) | copy-start | bytes 1769476
  40.7 0.8 copy-start.3
  51.9 0.8 copy-start.2

commit v5 on v4

--- a/solution.py
+++ b/solution.py
@@ -169,33 +169,47 @@
 
 
 CHUNKS = 2
-OFFSETS = (0, 1, 3, 2)
-
-
-def prefix_kernel(first, count, *refs):
-    recv_ref, sources = refs[0], refs[1 : 1 + count]
-    before = refs[1 + count : len(refs) - 6]
-    ret_ref, cache, values, queries, acc, sems = refs[-6:]
+
+
+def prefix_kernel(count, start, recv_ref, *refs):
+    sources = refs[: len(refs) - 8]
+    ret_ref, cache, values, queries, acc, stage_out, sems, out_sem = refs[-8:]
     index = pl.program_id(0)
-    group = index + first
     z_size = recv_ref.shape[0]
     span = CAPACITY * ROWS
     rows = z_size * span
-    copies = [pltpu.make_async_copy(sources[i], cache.at[i], sems.at[i]) for i in range(count)]
+    per_group = 1 if count > 1 else 2
+    copies = []
+    for i in range(count):
+        size = LANES // per_group
+        copies.append(
+            [
+                pltpu.make_async_copy(
+                    sources[i + p], cache.at[i, p * size : (p + 1) * size], sems.at[i + p]
+                )
+                for p in range(per_group)
+            ]
+        )
 
     @pl.when(index == 0)
     def _():
-        for copy in copies:
+        for copy in sum(copies, []):
             copy.start()
         queries[...] = recv_ref[...].astype(jnp.float32) * SCALE
         values[HALF:, :] = jnp.ones_like(values[HALF:, :])
-        if before:
-            acc[...] = before[0][...].astype(jnp.float32)
-
+        acc[...] = jnp.zeros_like(acc)
+
+    group = index + (X_SIZE - count if start else 0)
     for i in range(count):
-        pl.when(index == i)(copies[i].wait)
+
+        @pl.when(index == i)
+        def _():
+            for copy in copies[i]:
+                copy.wait()
+
     values[:HALF, :] = cache[index, HALF:]
     place = pl.ds(pl.multiple_of(group * span, 8), span)
+    own_place = pl.ds(pl.multiple_of(index * span, 8), span)
     query = jnp.concatenate(split_heads(queries[:, place, :].reshape(rows, LANES)), axis=0)
     query = query.astype(jnp.bfloat16)
     size = 2 * rows // CHUNKS
@@ -220,7 +234,7 @@
     for i in range(half):
         out = jnp.where(low, mixes[i][0], pltpu.roll(mixes[i + half][0], HALF, 1))
         sources = slice(i * z_size // half, (i + 1) * z_size // half)
-        acc[sources, place, :] = out.reshape(z_size // half, span, LANES)
+        acc[sources, own_place, :] = out.reshape(z_size // half, span, LANES)
         lse.append(jnp.where(low, mixes[i][1], mixes[i + half][1]))
     lse = jnp.concatenate(lse, axis=0)
     lane = lax.broadcasted_iota(jnp.int32, (span, LANES), 1) & (HALF - 1)
@@ -236,45 +250,68 @@
     packed = packed.reshape(rows, LANES).astype(jnp.bfloat16)
     shape = (z_size * GROUPS, rows)
     slot = lax.broadcasted_iota(jnp.int32, shape, 0)
-    inside = (slot & (GROUPS - 1)) // CAPACITY == group
+    inside = (slot & (GROUPS - 1)) // CAPACITY == index
     slot = slot // GROUPS * CAPACITY + (slot & (CAPACITY - 1))
     first = lax.broadcasted_iota(jnp.int32, shape, 1) - slot * ROWS
     pick = jnp.logical_and(inside, jnp.logical_and(first >= 0, first < ROWS))
     lse_rows = jnp.dot(pick.astype(jnp.bfloat16), packed, preferred_element_type=jnp.float32)
     lse_rows = lse_rows.reshape(z_size, GROUPS, LANES)
-    own = lax.broadcasted_iota(jnp.int32, (GROUPS, LANES), 0) // CAPACITY == group
-    acc[:, GROUPS * ROWS :, :] = jnp.where(own[None], lse_rows, acc[:, GROUPS * ROWS :, :])
+    own = lax.broadcasted_iota(jnp.int32, (GROUPS, LANES), 0) // CAPACITY == index
+    acc[:, count * span :, :] = jnp.where(own[None], lse_rows, acc[:, count * span :, :])
 
     @pl.when(index == count - 1)
     def _():
-        ret_ref[...] = acc[...].astype(jnp.bfloat16)
-
-
-def prefix_attention(recv, caches, first, before=()):
+        stage_out[...] = acc[...].astype(jnp.bfloat16)
+        copy = pltpu.make_async_copy(
+            stage_out, ret_ref.at[:, start : start + stage_out.shape[1], :], out_sem
+        )
+        copy.start()
+        copy.wait()
+
+
+FIRST_GROUPS = 3
+FIRST_ROWS = FIRST_GROUPS * CAPACITY * ROWS + GROUPS
+ALL_ROWS = FIRST_ROWS + CAPACITY * ROWS + GROUPS
+
+
+def prefix_attention(recv, caches, before=None):
     z_size = recv.shape[0]
-    count = len(caches)
+    count = len(caches) if before is None else 1
+    start = 0 if before is None else FIRST_ROWS
     length = caches[0].shape[1]
-    out_shape = (z_size, GROUPS * ROWS + GROUPS, LANES)
+    rows = count * CAPACITY * ROWS + GROUPS
     vmem = pl.BlockSpec(memory_space=pltpu.VMEM)
+    anywhere = pl.BlockSpec(memory_space=pl.ANY)
+    kernel = functools.partial(prefix_kernel, count, start)
+    operands = [recv, *caches]
+    aliases = {}
+    if before is not None:
+        aliases = {len(operands): 0}
+        operands.append(before)
+        inner = kernel
+        kernel = lambda *refs: inner(*refs[:3], *refs[4:])
     return pl.pallas_call(
-        functools.partial(prefix_kernel, first, count),
+        kernel,
         grid=(count,),
-        out_shape=jax.ShapeDtypeStruct(out_shape, jnp.bfloat16),
-        in_specs=[vmem] + [pl.BlockSpec(memory_space=pl.ANY)] * count + [vmem] * len(before),
-        out_specs=vmem,
+        out_shape=jax.ShapeDtypeStruct((z_size, ALL_ROWS, LANES), jnp.bfloat16),
+        in_specs=[vmem] + [anywhere] * (len(operands) - 1),
+        out_specs=anywhere,
         scratch_shapes=[
             pltpu.VMEM((count, LANES, length), jnp.bfloat16),
             pltpu.VMEM((LANES, length), jnp.bfloat16),
             pltpu.VMEM(recv.shape, jnp.float32),
-            pltpu.VMEM(out_shape, jnp.float32),
-            pltpu.SemaphoreType.DMA((count,)),
+            pltpu.VMEM((z_size, rows, LANES), jnp.float32),
+            pltpu.VMEM((z_size, rows, LANES), jnp.bfloat16),
+            pltpu.SemaphoreType.DMA((len(caches),)),
+            pltpu.SemaphoreType.DMA,
         ],
+        input_output_aliases=aliases,
         compiler_params=pltpu.CompilerParams(vmem_limit_bytes=VMEM_LIMIT),
         cost_estimate=pl.CostEstimate(
             flops=2_500_000_000 * count, bytes_accessed=1_000_000 * count, transcendentals=0
         ),
         name="prefix",
-    )(recv, *caches, *before)
+    )(*operands)
 
 
 def merge_kernel(code_ref, ret_ref, suffix_ref, suffix_lse_ref, w_ref, out_ref, wide, picked, packed, merged, left):
@@ -287,11 +324,16 @@
         for r in range(requests):
             code = code_ref[r]
             z, slot = code // GROUPS, code % GROUPS
-            start = pl.multiple_of(slot // CAPACITY * pair_rows, 8)
+            group = slot // CAPACITY
+            last = group == FIRST_GROUPS
+            start = pl.multiple_of(jnp.where(last, FIRST_ROWS, group * pair_rows), 8)
+            lse_row = slot + jnp.where(
+                last, ALL_ROWS - GROUPS - FIRST_GROUPS * CAPACITY, FIRST_ROWS - GROUPS
+            )
             pair = wide[z, pl.ds(start, pair_rows), :]
             second = jnp.concatenate([pair[ROWS:], pair[: PAD_ROWS - ROWS]], axis=0)
             picked[r] = jnp.where(slot % CAPACITY == 0, pair[:PAD_ROWS], second)
-            packed[r : r + 1, :] = wide[z, pl.ds(GROUPS * ROWS + slot, 1), :]
+            packed[r : r + 1, :] = wide[z, pl.ds(lse_row, 1), :]
         lane = lane_iota(PAD_ROWS) % HALF
         row = lax.broadcasted_iota(jnp.int32, (PAD_ROWS, LANES), 0)
         own = jnp.logical_or(lane == row, jnp.logical_or(lane == row + ROWS, lane == row + 2 * ROWS))
@@ -362,22 +404,26 @@
     q3 = queries.transpose(1, 0, 2)
     send, codes = route(me, request_prefix.reshape(-1), prefix_owner, q3, z_size)
     kv_out, send = lax.optimization_barrier((kv, send))
-    caches = [kv]
-    for offset in OFFSETS[1:]:
+
+    def from_offset(array, offset):
         pairs = [
             (z * X_SIZE + (x + offset) % X_SIZE, z * X_SIZE + x)
             for z in range(z_size)
             for x in range(X_SIZE)
         ]
-        caches.append(lax.ppermute(kv_out, "prefix", pairs))
+        return lax.ppermute(array, "prefix", pairs)
+
+    right = from_offset(kv_out, 1)
+    left = from_offset(kv_out, -1)
+    opposite = (from_offset(right[:HALF], 1), from_offset(left[HALF:], -1))
     recv = lax.all_to_all(
         send, "prefix", split_axis=0, concat_axis=0, axis_index_groups=z_groups, tiled=True
     )
     suffix_rows = suffix_cache[:, 0].transpose(0, 2, 1)
     suffix_out, suffix_lse = suffix_attention(suffix_lengths, q3, suffix_rows)
     recv, suffix_out, suffix_lse = lax.optimization_barrier((recv, suffix_out, suffix_lse))
-    ret = prefix_attention(recv, caches[:3], 0)
-    ret = prefix_attention(recv, caches[3:], 3, (ret,))
+    ret = prefix_attention(recv, (kv, right, left))
+    ret = prefix_attention(recv, opposite, ret)
     homed = lax.all_to_all(
         ret, "prefix", split_axis=0, concat_axis=0, axis_index_groups=z_groups, tiled=True
     )

time: 128 us -> 126 us (0.984)
  blocking collectives: 60.5 us -> 56.9 us
  starting transfers between devices: 25.7 us -> 29.2 us
  waiting for transfers between devices: 3.49 us -> 1.29 us
    all_to_all x2, blocking collectives: 34.3 us -> 26.3 us  [shards(): lax.all_to_all(parts, 'tensor', split_axis=0, concat_axis=0, axis_index_g...]
    all_to_all x1, blocking collectives: 26.3 us -> 30.6 us  [shards(): lax.all_to_all(ret, 'prefix', split_axis=0, concat_axis=0, axis_index_gro...]
    ppermute x3 -> x4, starting transfers between devices: 9.94 us -> 13.4 us  [from_offset(): return lax.ppermute(array, 'prefix', pairs)]
    ppermute x3 -> x4, waiting for transfers between devices: 3.49 us -> 1.29 us  [from_offset(): return lax.ppermute(array, 'prefix', pairs)]
  transfers between devices with their start and end apart: 4 -> 5, of which waited for: 1 -> 1; matrix products, arithmetic and copies ran while one was open for 0% -> 0% of each run, Pallas kernels for 15% -> 15%
where the time goes in v5:
time: 126 us; the launch traced here: 124 us
  blocking collectives  56.9 us (45%)
  Pallas kernels  33.2 us (26%)
  starting transfers between devices  29.2 us (23%)
  local copies, waits for them, and re-layouts  2.19 us (2%)
  other arithmetic  1.3 us (1%)
  waiting for transfers between devices  1.29 us (1%)
    all_to_all x1, blocking collectives, shards(): lax.all_to_all(ret, 'prefix', split_axis=0, concat_axis=0, axis_index_gro...  30.6 us
    all_to_all x2, blocking collectives, shards(): lax.all_to_all(parts, 'tensor', split_axis=0, concat_axis=0, axis_index_g...  26.3 us
    all_to_all x1, starting transfers between devices, shards(): lax.all_to_all(send, 'prefix', split_axis=0, concat_axis=0, axis_index_gr...  15.8 us
    pallas_call x2, Pallas kernels, prefix_attention(): pl.pallas_call(kernel, grid=(count,), out_shape=jax.ShapeDtypeStruct((z_s...  15.6 us
    ppermute x4, starting transfers between devices, from_offset(): return lax.ppermute(array, 'prefix', pairs)  13.4 us
    pallas_call x1, Pallas kernels, suffix_attention(): pl.pallas_call(suffix_kernel, out_shape=(shape, shape), in_specs=[pl.Bloc...  8.76 us
    pallas_call x1, Pallas kernels, merge_project(): pl.pallas_call(merge_kernel, grid=(parts // CORES,), out_shape=jax.ShapeD...  6.22 us
    pallas_call x1, Pallas kernels, route(): pl.pallas_call(route_kernel, out_shape=(jax.ShapeDtypeStruct(shape, jnp.b...  2.64 us
  transfers between devices with their start and end apart: 5, of which 1 were waited for; matrix products, arithmetic and copies ran while one was open for 0% of the time, Pallas kernels for 15%

profile of v5, /device:TPU:1, one launch (start us, length us, event | category | flops | bytes accessed | tf_op | source)
XLA Modules:
  0.0 124.2 jit_solution(5738321297283751297)
XLA Ops:
  0.0 2.6 %route.1 = (bf16[16,96,128]{2,1,0:T(8,128)(2,1)}, s32[64]{0:T(128)}) custom-call(s32[1]{0:T(128)} %bitcast.me_ref, s32[4096]{0:T(1024)} %bitcast.16, s32[64]{0:T(128)} %owner_ref.1, bf16[3,64,512]{2,1,0:T(8,128)(2,1)} %bitcast.14), custom_call_target="tpu_custom_call" | custom-call | tf_op jit(solution)/shard_map/route/pallas_call | solution.py:96
  2.6 15.8 %all-to-all-start = ((bf16[16,96,128]{2,1,0:T(8,128)(2,1)}), bf16[16,96,128]{2,1,0:T(8,128)(2,1)S(1)}, u32[]{:S(2)}, u32[]{:S(2)}) async-start(bf16[16,96,128]{2,1,0:T(8,128)(2,1)} %get-tuple-element.16), calls=%async_computation | async-start | bytes 786432 | tf_op jit(solution)/shard_map/all_to_all | solution.py:419
  18.4 4.4 %collective-permute-start = (bf16[128,2304]{1,0:T(8,128)(2,1)}, bf16[128,2304]{1,0:T(8,128)(2,1)S(1)}, u32[]{:S(2)}, u32[]{:S(2)}) collective-permute-start(bf16[128,2304]{1,0:T(8,128)(2,1)} %bitcast.18), channel_id=1, source_target_pairs={{8,0},{16,8},{24,16},{0,24},{40,32},{48,40},{56,48},{32,56},{72,64... | collective-permute-start | bytes 1769480 | tf_op jit(solution)/shard_map/ppermute | solution.py:414
  22.8 1.9 %collective-permute-start.2 = (bf16[128,2304]{1,0:T(8,128)(2,1)}, bf16[128,2304]{1,0:T(8,128)(2,1)S(1)}, u32[]{:S(2)}, u32[]{:S(2)}) collective-permute-start(bf16[128,2304]{1,0:T(8,128)(2,1)} %bitcast.19), channel_id=1, source_target_pairs={{24,0},{0,8},{8,16},{16,24},{56,32},{32,40},{40,48},{48,56},{88,64... | collective-permute-start | bytes 1769480 | tf_op jit(solution)/shard_map/ppermute | solution.py:414
  24.7 8.8 %suffix.1 = (f32[1024,128]{1,0:T(8,128)}, f32[1024,128]{1,0:T(8,128)}) custom-call(s32[64]{0:T(128)} %length_ref.1, bf16[3,64,512]{2,1,0:T(8,128)(2,1)} %bitcast.15, bf16[64,80,128]{2,1,0:T(8,128)(2,1)} %bitcast.17), custom_call_target="tpu_custom_call" | custom-call | flops 8000000000 | bytes 8000000 | tf_op jit(solution)/shard_map/suffix/pallas_call | solution.py:157
  33.5 1.3 %collective-permute-done.refs_1_ = bf16[128,2304]{1,0:T(8,128)(2,1)S(1)} collective-permute-done((bf16[128,2304]{1,0:T(8,128)(2,1)}, bf16[128,2304]{1,0:T(8,128)(2,1)S(1)}, u32[]{:S(2)}, u32[]{:S(2)}) %collective-permute-start) | collective-permute-done | bytes 589856 | tf_op jit(solution)/shard_map/ppermute | solution.py:414
  34.8 0.0 copy-start.1
  34.8 5.2 %collective-permute-start.1 = (bf16[64,2304]{1,0:T(8,128)(2,1)S(1)}, bf16[64,2304]{1,0:T(8,128)(2,1)S(1)}, u32[]{:S(2)}, u32[]{:S(2)}) collective-permute-start(bf16[64,2304]{1,0:T(8,128)(2,1)S(1)} %slice.8), channel_id=1, source_target_pairs={{8,0},{16,8},{24,16},{0,24},{40,32},{48,40},{56,48},{32,56},{72,64... | collective-permute-start | bytes 884744 | tf_op jit(solution)/shard_map/ppermute | solution.py:414
  40.0 0.0 collective-permute-done.2.refs_2_
  40.0 0.0 copy-start.2
  40.1 1.9 %collective-permute-start.3 = (bf16[64,2304]{1,0:T(8,128)(2,1)S(1)}, bf16[64,2304]{1,0:T(8,128)(2,1)S(1)}, u32[]{:S(2)}, u32[]{:S(2)}) collective-permute-start(bf16[64,2304]{1,0:T(8,128)(2,1)S(1)} %slice.9), channel_id=1, source_target_pairs={{24,0},{0,8},{8,16},{16,24},{56,32},{32,40},{40,48},{48,56},{88,64... | collective-permute-start | bytes 884744 | tf_op jit(solution)/shard_map/ppermute | solution.py:414
  42.0 0.0 all-to-all-done.recv_ref.refs_0_
  42.0 0.0 copy-start
  42.0 0.0 copy-done.1
  42.0 0.0 copy-done.2
  42.1 0.7 copy-done
  42.8 10.4 %prefix.2.refs_3_ = bf16[16,112,128]{2,1,0:T(8,128)(2,1)} custom-call(bf16[16,96,128]{2,1,0:T(8,128)(2,1)} %copy-done, bf16[128,2304]{1,0:T(8,128)(2,1)} %bitcast.20, bf16[128,2304]{1,0:T(8,128)(2,1)} %copy-done.1, bf16[128,2304]{1,0:T(8,128)(2,1)} %copy-done.2), custom_call_target="tpu_custom_call" | custom-call | flops 7500000256 | bytes 3000000 | tf_op jit(solution)/shard_map/prefix/pallas_call | solution.py:293
  53.2 0.0 collective-permute-done.1.refs_1_
  53.2 0.0 copy-start.3
  53.2 0.0 collective-permute-done.3.refs_2_
  53.2 0.7 copy-done.3
  53.9 0.0 copy-start.4
  53.9 0.7 copy-done.4
  54.6 5.2 %prefix.3 = bf16[16,112,128]{2,1,0:T(8,128)(2,1)} custom-call(bf16[16,96,128]{2,1,0:T(8,128)(2,1)} %copy-done, bf16[64,2304]{1,0:T(8,128)(2,1)} %copy-done.3, bf16[64,2304]{1,0:T(8,128)(2,1)} %copy-done.4, bf16[16,112,128]{2,1,0:T(8,128)(2,1)} %prefix.2.refs_3_), custom_call_target="tpu_custom_call", output_to_operand_aliasing={{}: (3, {})} | custom-call | flops 2500000000 | bytes 1000000 | tf_op jit(solution)/shard_map/prefix/pallas_call | solution.py:293
  59.8 30.6 %all_to_all.20.ret_ref = bf16[16,112,128]{2,1,0:T(8,128)(2,1)} all-to-all(bf16[16,112,128]{2,1,0:T(8,128)(2,1)} %prefix.3), channel_id=1, replica_groups={{0,32,64,96,128,160,192,224,256,288,320,352,384,416,448,480},{8,40,72,1..., dimensions={0} | all-to-all | bytes 917504 | tf_op jit(solution)/shard_map/all_to_all | solution.py:427
  90.4 6.2 %merge.1 = bf16[2,4,192,360]{3,2,1,0:T(8,128)(2,1)} custom-call(s32[64]{0:T(128)} %get-tuple-element.14.code_ref, bf16[16,112,128]{2,1,0:T(8,128)(2,1)} %all_to_all.20.ret_ref, f32[1024,128]{1,0:T(8,128)} %get-tuple-element.21.suffix_ref, f32[1024,128]{1,0:T(8,128)} %get-tuple-element.22.suffix_lse_ref, bf16[8,360,512]{2,1,0:T(8,128)(2,1)} %bitcast.13), custom_call_target="tpu_custom_call" | custom-call | tf_op jit(solution)/shard_map/merge/pallas_call | solution.py:373
  96.6 12.7 %all_to_all.21 = bf16[2,4,192,360]{3,2,1,0:T(8,128)(2,1)S(1)} all-to-all(bf16[2,4,192,360]{3,2,1,0:T(8,128)(2,1)} %merge.1), channel_id=1, replica_groups={{0,1},{2,3},{4,5},{6,7},{8,9},{10,11},{12,13},{14,15},{16,17},{18,19},{..., dimensions={0} | all-to-all | bytes 2211840 | tf_op jit(solution)/shard_map/all_to_all | solution.py:435
  109.3 0.5 reduce_sum.24
  109.9 13.6 %all_to_all.22 = bf16[4,192,360]{2,1,0:T(8,128)(2,1)S(1)} all-to-all(bf16[4,192,360]{2,1,0:T(8,128)(2,1)S(1)} %reduce_sum.24), channel_id=1, replica_groups={{0,2,4,6},{1,3,5,7},{8,10,12,14},{9,11,13,15},{16,18,20,22},{17,19,21,2..., dimensions={0} | all-to-all | bytes 1105920 | tf_op jit(solution)/shard_map/all_to_all | solution.py:435
  123.5 0.8 reduce_sum.25
  (2 shorter events, 0.0 us)
Async XLA Ops:
  2.6 39.4 %all-to-all-start = ((bf16[16,96,128]{2,1,0:T(8,128)(2,1)}), bf16[16,96,128]{2,1,0:T(8,128)(2,1)S(1)}, u32[]{:S(2)}, u32[]{:S(2)}) async-start(bf16[16,96,128]{2,1,0:T(8,128)(2,1)} %get-tuple-element.16), calls=%async_computation | async-start | bytes 786432 | tf_op jit(solution)/shard_map/all_to_all | solution.py:419
  18.4 16.4 %collective-permute-start = (bf16[128,2304]{1,0:T(8,128)(2,1)}, bf16[128,2304]{1,0:T(8,128)(2,1)S(1)}, u32[]{:S(2)}, u32[]{:S(2)}) collective-permute-start(bf16[128,2304]{1,0:T(8,128)(2,1)} %bitcast.18), channel_id=1, source_target_pairs={{8,0},{16,8},{24,16},{0,24},{40,32},{48,40},{56,48},{32,56},{72,64... | collective-permute-start | bytes 1769480 | tf_op jit(solution)/shard_map/ppermute | solution.py:414
  22.8 17.2 %collective-permute-start.2 = (bf16[128,2304]{1,0:T(8,128)(2,1)}, bf16[128,2304]{1,0:T(8,128)(2,1)S(1)}, u32[]{:S(2)}, u32[]{:S(2)}) collective-permute-start(bf16[128,2304]{1,0:T(8,128)(2,1)} %bitcast.19), channel_id=1, source_target_pairs={{24,0},{0,8},{8,16},{16,24},{56,32},{32,40},{40,48},{48,56},{88,64... | collective-permute-start | bytes 1769480 | tf_op jit(solution)/shard_map/ppermute | solution.py:414
  34.8 7.2 %copy-start.1 = (bf16[128,2304]{1,0:T(8,128)(2,1)}, bf16[128,2304]{1,0:T(8,128)(2,1)S(1)}, u32[]{:S(2)}) copy-start(bf16[128,2304]{1,0:T(8,128)(2,1)S(1)} %collective-permute-done.refs_1_) | copy-start | bytes 1769476
  34.8 18.4 %collective-permute-start.1 = (bf16[64,2304]{1,0:T(8,128)(2,1)S(1)}, bf16[64,2304]{1,0:T(8,128)(2,1)S(1)}, u32[]{:S(2)}, u32[]{:S(2)}) collective-permute-start(bf16[64,2304]{1,0:T(8,128)(2,1)S(1)} %slice.8), channel_id=1, source_target_pairs={{8,0},{16,8},{24,16},{0,24},{40,32},{48,40},{56,48},{32,56},{72,64... | collective-permute-start | bytes 884744 | tf_op jit(solution)/shard_map/ppermute | solution.py:414
  40.0 2.0 %copy-start.2 = (bf16[128,2304]{1,0:T(8,128)(2,1)}, bf16[128,2304]{1,0:T(8,128)(2,1)S(1)}, u32[]{:S(2)}) copy-start(bf16[128,2304]{1,0:T(8,128)(2,1)S(1)} %collective-permute-done.2.refs_2_) | copy-start | bytes 1769476
  40.1 13.1 %collective-permute-start.3 = (bf16[64,2304]{1,0:T(8,128)(2,1)S(1)}, bf16[64,2304]{1,0:T(8,128)(2,1)S(1)}, u32[]{:S(2)}, u32[]{:S(2)}) collective-permute-start(bf16[64,2304]{1,0:T(8,128)(2,1)S(1)} %slice.9), channel_id=1, source_target_pairs={{24,0},{0,8},{8,16},{16,24},{56,32},{32,40},{40,48},{48,56},{88,64... | collective-permute-start | bytes 884744 | tf_op jit(solution)/shard_map/ppermute | solution.py:414
  42.0 0.8 copy-start
  53.2 0.7 copy-start.3
  53.9 0.7 copy-start.4

commit v6 on v5

--- a/solution.py
+++ b/solution.py
@@ -18,6 +18,7 @@
 PAD_ROWS = 16
 SCALE = 0.125
 VMEM_LIMIT = 56 * 1024 * 1024
+SMALL_LIMIT = 32 * 1024 * 1024
 
 
 def lane_iota(rows):
@@ -178,22 +179,11 @@
     z_size = recv_ref.shape[0]
     span = CAPACITY * ROWS
     rows = z_size * span
-    per_group = 1 if count > 1 else 2
-    copies = []
-    for i in range(count):
-        size = LANES // per_group
-        copies.append(
-            [
-                pltpu.make_async_copy(
-                    sources[i + p], cache.at[i, p * size : (p + 1) * size], sems.at[i + p]
-                )
-                for p in range(per_group)
-            ]
-        )
+    copies = [pltpu.make_async_copy(sources[i], cache.at[i], sems.at[i]) for i in range(count)]
 
     @pl.when(index == 0)
     def _():
-        for copy in sum(copies, []):
+        for copy in copies:
             copy.start()
         queries[...] = recv_ref[...].astype(jnp.float32) * SCALE
         values[HALF:, :] = jnp.ones_like(values[HALF:, :])
@@ -201,12 +191,7 @@
 
     group = index + (X_SIZE - count if start else 0)
     for i in range(count):
-
-        @pl.when(index == i)
-        def _():
-            for copy in copies[i]:
-                copy.wait()
-
+        pl.when(index == i)(copies[i].wait)
     values[:HALF, :] = cache[index, HALF:]
     place = pl.ds(pl.multiple_of(group * span, 8), span)
     own_place = pl.ds(pl.multiple_of(index * span, 8), span)
@@ -276,7 +261,7 @@
 
 def prefix_attention(recv, caches, before=None):
     z_size = recv.shape[0]
-    count = len(caches) if before is None else 1
+    count = len(caches)
     start = 0 if before is None else FIRST_ROWS
     length = caches[0].shape[1]
     rows = count * CAPACITY * ROWS + GROUPS
@@ -289,7 +274,7 @@
         aliases = {len(operands): 0}
         operands.append(before)
         inner = kernel
-        kernel = lambda *refs: inner(*refs[:3], *refs[4:])
+        kernel = lambda *refs: inner(*refs[:2], *refs[3:])
     return pl.pallas_call(
         kernel,
         grid=(count,),
@@ -302,11 +287,11 @@
             pltpu.VMEM(recv.shape, jnp.float32),
             pltpu.VMEM((z_size, rows, LANES), jnp.float32),
             pltpu.VMEM((z_size, rows, LANES), jnp.bfloat16),
-            pltpu.SemaphoreType.DMA((len(caches),)),
+            pltpu.SemaphoreType.DMA((count,)),
             pltpu.SemaphoreType.DMA,
         ],
         input_output_aliases=aliases,
-        compiler_params=pltpu.CompilerParams(vmem_limit_bytes=VMEM_LIMIT),
+        compiler_params=pltpu.CompilerParams(vmem_limit_bytes=SMALL_LIMIT),
         cost_estimate=pl.CostEstimate(
             flops=2_500_000_000 * count, bytes_accessed=1_000_000 * count, transcendentals=0
         ),
@@ -314,7 +299,7 @@
     )(*operands)
 
 
-def merge_kernel(code_ref, ret_ref, suffix_ref, suffix_lse_ref, w_ref, out_ref, wide, picked, packed, merged, left):
+def merge_kernel(core_ref, code_ref, ret_ref, suffix_ref, suffix_lse_ref, w_ref, out_ref, left, wide, picked, packed, merged):
     requests = code_ref.shape[0]
 
     @pl.when(pl.program_id(0) == 0)
@@ -361,37 +346,66 @@
                     pl.ds(step * pairs + pair, requests, stride=PAD_ROWS), :
                 ].astype(jnp.bfloat16)
 
-    for core in range(CORES):
-        out_ref[core, 0] = nt_dot(left[...], w_ref[core]).astype(jnp.bfloat16)
-
-
-def merge_project(codes, ret, suffix_out, suffix_lse, weights, parts):
+    out_ref[0] = nt_dot(left[...], w_ref[0]).astype(jnp.bfloat16)
+
+
+def project_kernel(core_ref, left_ref, w_ref, out_ref):
+    out_ref[0] = nt_dot(left_ref[...], w_ref[0]).astype(jnp.bfloat16)
+
+
+def merge_project(core, codes, ret, suffix_out, suffix_lse, weights, parts):
     requests = codes.shape[0]
     width = weights.shape[0] // parts
     depth = weights.shape[1]
-    whole = lambda array: pl.BlockSpec(array.shape, lambda t: (0,) * array.ndim)
-    return pl.pallas_call(
+    rows = STEPS * requests
+    weights = weights.reshape(parts, width, depth)
+    whole = lambda shape: pl.BlockSpec(shape, lambda t, core: (0,) * len(shape))
+    out_spec = pl.BlockSpec((1, rows, width), lambda t, core: (t, 0, 0))
+    out_shape = jax.ShapeDtypeStruct((parts // CORES, rows, width), jnp.bfloat16)
+    other, left = pl.pallas_call(
         merge_kernel,
-        grid=(parts // CORES,),
-        out_shape=jax.ShapeDtypeStruct((CORES, parts // CORES, STEPS * requests, width), jnp.bfloat16),
-        in_specs=[
-            pl.BlockSpec(memory_space=pltpu.SMEM),
-            whole(ret),
-            whole(suffix_out),
-            whole(suffix_lse),
-            pl.BlockSpec((CORES, width, depth), lambda t: (t, 0, 0)),
-        ],
-        out_specs=pl.BlockSpec((CORES, 1, STEPS * requests, width), lambda t: (0, t, 0, 0)),
-        scratch_shapes=[
-            pltpu.VMEM(ret.shape, jnp.float32),
-            pltpu.VMEM((requests, PAD_ROWS, LANES), jnp.float32),
-            pltpu.VMEM((requests, LANES), jnp.float32),
-            pltpu.VMEM((requests * PAD_ROWS, LANES), jnp.float32),
-            pltpu.VMEM((STEPS * requests, depth), jnp.bfloat16),
-        ],
+        out_shape=(out_shape, jax.ShapeDtypeStruct((rows, depth), jnp.bfloat16)),
+        grid_spec=pltpu.PrefetchScalarGridSpec(
+            num_scalar_prefetch=1,
+            grid=(parts // CORES,),
+            in_specs=[
+                pl.BlockSpec(memory_space=pltpu.SMEM),
+                whole(ret.shape),
+                whole(suffix_out.shape),
+                whole(suffix_lse.shape),
+                pl.BlockSpec((1, width, depth), lambda t, core: (t * CORES + 1 - core[0], 0, 0)),
+            ],
+            out_specs=(out_spec, whole((rows, depth))),
+            scratch_shapes=[
+                pltpu.VMEM(ret.shape, jnp.float32),
+                pltpu.VMEM((requests, PAD_ROWS, LANES), jnp.float32),
+                pltpu.VMEM((requests, LANES), jnp.float32),
+                pltpu.VMEM((requests * PAD_ROWS, LANES), jnp.float32),
+            ],
+        ),
         compiler_params=pltpu.CompilerParams(vmem_limit_bytes=VMEM_LIMIT),
         name="merge",
-    )(codes, ret, suffix_out, suffix_lse, weights.reshape(parts, width, depth))
+    )(core, codes, ret, suffix_out, suffix_lse, weights)
+    received = lax.ppermute(other, "tensor", [(i, i ^ 1) for i in range(parts)])
+    own = pl.pallas_call(
+        project_kernel,
+        out_shape=out_shape,
+        grid_spec=pltpu.PrefetchScalarGridSpec(
+            num_scalar_prefetch=1,
+            grid=(parts // CORES,),
+            in_specs=[
+                whole((rows, depth)),
+                pl.BlockSpec((1, width, depth), lambda t, core: (t * CORES + core[0], 0, 0)),
+            ],
+            out_specs=out_spec,
+        ),
+        compiler_params=pltpu.CompilerParams(vmem_limit_bytes=VMEM_LIMIT),
+        cost_estimate=pl.CostEstimate(
+            flops=2_000_000_000, bytes_accessed=2_000_000, transcendentals=0
+        ),
+        name="project",
+    )(core, left, weights)
+    return (own.astype(jnp.float32) + received.astype(jnp.float32)).astype(jnp.bfloat16)
 
 
 def shards(queries, prefix_cache, suffix_cache, suffix_lengths, request_prefix, prefix_owner, out_proj):
@@ -415,7 +429,7 @@
 
     right = from_offset(kv_out, 1)
     left = from_offset(kv_out, -1)
-    opposite = (from_offset(right[:HALF], 1), from_offset(left[HALF:], -1))
+    opposite = from_offset(right, 1)
     recv = lax.all_to_all(
         send, "prefix", split_axis=0, concat_axis=0, axis_index_groups=z_groups, tiled=True
     )
@@ -423,19 +437,17 @@
     suffix_out, suffix_lse = suffix_attention(suffix_lengths, q3, suffix_rows)
     recv, suffix_out, suffix_lse = lax.optimization_barrier((recv, suffix_out, suffix_lse))
     ret = prefix_attention(recv, (kv, right, left))
-    ret = prefix_attention(recv, opposite, ret)
+    ret = prefix_attention(recv, (opposite,), ret)
     homed = lax.all_to_all(
         ret, "prefix", split_axis=0, concat_axis=0, axis_index_groups=z_groups, tiled=True
     )
-    parts = merge_project(codes, homed, suffix_out, suffix_lse, out_proj.T, tensor_size)
-    y_size = tensor_size // CORES
-    core_groups = [[y * CORES + c for c in range(CORES)] for y in range(y_size)]
-    y_groups = [[y * CORES + c for y in range(y_size)] for c in range(CORES)]
-    for groups in (core_groups, y_groups):
-        parts = lax.all_to_all(
-            parts, "tensor", split_axis=0, concat_axis=0, axis_index_groups=groups, tiled=True
-        )
-        parts = jnp.sum(parts.astype(jnp.float32), axis=0).astype(jnp.bfloat16)
+    core = (lax.axis_index("tensor").astype(jnp.int32) % CORES).reshape(1)
+    parts = merge_project(core, codes, homed, suffix_out, suffix_lse, out_proj.T, tensor_size)
+    y_groups = [[y * CORES + c for y in range(tensor_size // CORES)] for c in range(CORES)]
+    parts = lax.all_to_all(
+        parts, "tensor", split_axis=0, concat_axis=0, axis_index_groups=y_groups, tiled=True
+    )
+    parts = jnp.sum(parts.astype(jnp.float32), axis=0).astype(jnp.bfloat16)
     return parts.reshape(STEPS, queries.shape[0], -1).transpose(1, 0, 2)
 
 

time: 126 us -> 121 us (0.960)
  blocking collectives: 56.9 us -> 13.7 us
  waiting for transfers between devices: 1.29 us -> 22.2 us
  starting transfers between devices: 29.2 us -> 47.6 us
  local copies, waits for them, and re-layouts: 2.19 us -> 0.79 us
    all_to_all x1 -> x0, blocking collectives: 30.6 us -> none  [shards(): lax.all_to_all(ret, 'prefix', split_axis=0, concat_axis=0, axis_index_gro...]
    all_to_all x0 -> x1, waiting for transfers between devices: none -> 19 us  [shards(): lax.all_to_all(ret, 'prefix', split_axis=0, concat_axis=0, axis_index_gro...]
    all_to_all x2 -> x1, blocking collectives: 26.3 us -> 13.7 us  [shards(): lax.all_to_all(parts, 'tensor', split_axis=0, concat_axis=0, axis_index_g...]
    all_to_all x0 -> x1, starting transfers between devices: none -> 10.9 us  [shards(): lax.all_to_all(ret, 'prefix', split_axis=0, concat_axis=0, axis_index_gro...]
    ppermute x0 -> x1, starting transfers between devices: none -> 9.45 us  [merge_project(): received = lax.ppermute(other, 'tensor', [(i, i ^ 1) for i in range(parts)])]
    pallas_call x2, Pallas kernels: 15.6 us -> 12.1 us  [prefix_attention(): pl.pallas_call(kernel, grid=(count,), out_shape=jax.ShapeDtypeStruct((z_s...]
    pallas_call x1 -> x2, Pallas kernels: 6.22 us -> 9.62 us  [the longest x1 5.63 us: merge_project(): pl.pallas_call(merge_kernel, out_shape=(out_shape, jax.ShapeDtypeStruct((...]
    ppermute x4 -> x3, starting transfers between devices: 13.4 us -> 11.5 us  [from_offset(): return lax.ppermute(array, 'prefix', pairs)]
  transfers between devices with their start and end apart: 5 -> 6, of which waited for: 1 -> 3; matrix products, arithmetic and copies ran while one was open for 0% -> 0% of each run, Pallas kernels for 15% -> 18%
where the time goes in v6:
time: 121 us; the launch traced here: 120 us
  starting transfers between devices  47.6 us (39%)
  Pallas kernels  33.2 us (27%)
  waiting for transfers between devices  22.2 us (18%)
  blocking collectives  13.7 us (11%)
  other arithmetic  1.99 us (2%)
    all_to_all x1, waiting for transfers between devices, shards(): lax.all_to_all(ret, 'prefix', split_axis=0, concat_axis=0, axis_index_gro...  19 us
    all_to_all x1, starting transfers between devices, shards(): lax.all_to_all(send, 'prefix', split_axis=0, concat_axis=0, axis_index_gr...  15.8 us
    all_to_all x1, blocking collectives, shards(): lax.all_to_all(parts, 'tensor', split_axis=0, concat_axis=0, axis_index_g...  13.7 us
    pallas_call x2, Pallas kernels, prefix_attention(): pl.pallas_call(kernel, grid=(count,), out_shape=jax.ShapeDtypeStruct((z_s...  12.1 us
    ppermute x3, starting transfers between devices, from_offset(): return lax.ppermute(array, 'prefix', pairs)  11.5 us
    all_to_all x1, starting transfers between devices, shards(): lax.all_to_all(ret, 'prefix', split_axis=0, concat_axis=0, axis_index_gro...  10.9 us
    ppermute x1, starting transfers between devices, merge_project(): received = lax.ppermute(other, 'tensor', [(i, i ^ 1) for i in range(parts)])  9.45 us
    pallas_call x1, Pallas kernels, suffix_attention(): pl.pallas_call(suffix_kernel, out_shape=(shape, shape), in_specs=[pl.Bloc...  8.78 us
  transfers between devices with their start and end apart: 6, of which 3 were waited for; matrix products, arithmetic and copies ran while one was open for 0% of the time, Pallas kernels for 18%

profile of v6, /device:TPU:1, one launch (start us, length us, event | category | flops | bytes accessed | tf_op | source)
XLA Modules:
  0.0 119.6 jit_solution(6277733259373719869)
XLA Ops:
  0.0 2.6 %route.1 = (bf16[16,96,128]{2,1,0:T(8,128)(2,1)}, s32[64]{0:T(128)}) custom-call(s32[1]{0:T(128)} %bitcast.1.me_ref, s32[4096]{0:T(1024)} %bitcast.21, s32[64]{0:T(128)} %owner_ref.1, bf16[3,64,512]{2,1,0:T(8,128)(2,1)} %bitcast.19), custom_call_target="tpu_custom_call" | custom-call | tf_op jit(solution)/shard_map/route/pallas_call | solution.py:97
  2.7 15.8 %all-to-all-start = ((bf16[16,96,128]{2,1,0:T(8,128)(2,1)}), bf16[16,96,128]{2,1,0:T(8,128)(2,1)S(1)}, u32[]{:S(2)}, u32[]{:S(2)}) async-start(bf16[16,96,128]{2,1,0:T(8,128)(2,1)} %get-tuple-element.18), calls=%async_computation | async-start | bytes 786432 | tf_op jit(solution)/shard_map/all_to_all | solution.py:433
  18.4 4.4 %collective-permute-start = (bf16[128,2304]{1,0:T(8,128)(2,1)}, bf16[128,2304]{1,0:T(8,128)(2,1)S(1)}, u32[]{:S(2)}, u32[]{:S(2)}) collective-permute-start(bf16[128,2304]{1,0:T(8,128)(2,1)} %bitcast.14), channel_id=1, source_target_pairs={{8,0},{16,8},{24,16},{0,24},{40,32},{48,40},{56,48},{32,56},{72,64... | collective-permute-start | bytes 1769480 | tf_op jit(solution)/shard_map/ppermute | solution.py:428
  22.8 1.9 %collective-permute-start.2 = (bf16[128,2304]{1,0:T(8,128)(2,1)}, bf16[128,2304]{1,0:T(8,128)(2,1)S(1)}, u32[]{:S(2)}, u32[]{:S(2)}) collective-permute-start(bf16[128,2304]{1,0:T(8,128)(2,1)} %bitcast.15), channel_id=1, source_target_pairs={{24,0},{0,8},{8,16},{16,24},{56,32},{32,40},{40,48},{48,56},{88,64... | collective-permute-start | bytes 1769480 | tf_op jit(solution)/shard_map/ppermute | solution.py:428
  24.7 0.0 copy-start
  24.8 8.8 %suffix.1 = (f32[1024,128]{1,0:T(8,128)}, f32[1024,128]{1,0:T(8,128)}) custom-call(s32[64]{0:T(128)} %length_ref.1, bf16[3,64,512]{2,1,0:T(8,128)(2,1)} %bitcast.20, bf16[64,80,128]{2,1,0:T(8,128)(2,1)} %bitcast.22), custom_call_target="tpu_custom_call" | custom-call | flops 8000000000 | bytes 8000000 | tf_op jit(solution)/shard_map/suffix/pallas_call | solution.py:158
  33.5 1.2 %collective-permute-done.refs_1_ = bf16[128,2304]{1,0:T(8,128)(2,1)S(1)} collective-permute-done((bf16[128,2304]{1,0:T(8,128)(2,1)}, bf16[128,2304]{1,0:T(8,128)(2,1)S(1)}, u32[]{:S(2)}, u32[]{:S(2)}) %collective-permute-start) | collective-permute-done | bytes 589856 | tf_op jit(solution)/shard_map/ppermute | solution.py:428
  34.8 5.2 %collective-permute-start.1 = (bf16[128,2304]{1,0:T(8,128)(2,1)S(1)}, bf16[128,2304]{1,0:T(8,128)(2,1)S(1)}, u32[]{:S(2)}, u32[]{:S(2)}) collective-permute-start(bf16[128,2304]{1,0:T(8,128)(2,1)S(1)} %collective-permute-done.refs_1_), channel_id=1, source_target_pairs={{8,0},{16,8},{24,16},{0,24},{40,32},{48,40},{56,48},{32,56},{72,64... | collective-permute-start | bytes 1769480 | tf_op jit(solution)/shard_map/ppermute | solution.py:428
  40.0 0.0 all-to-all-done.recv_ref.refs_0_
  40.0 0.0 collective-permute-done.2.refs_2_
  40.0 0.0 copy-done
  40.0 8.8 %prefix.2.refs_2_ = bf16[16,112,128]{2,1,0:T(8,128)(2,1)} custom-call(bf16[16,96,128]{2,1,0:T(8,128)(2,1)S(1)} %all-to-all-done.recv_ref.refs_0_, bf16[128,2304]{1,0:T(8,128)(2,1)S(1)} %bitcast.16, bf16[128,2304]{1,0:T(8,128)(2,1)S(1)} %collective-permute-done.refs_1_, bf16[128,2304]{1,0:T(8,128)(2,1)S(1)} %collective-permute-done.2.refs_2_), custom_call_target="tpu_custom_call" | custom-call | flops 7500000256 | bytes 3000000 | tf_op jit(solution)/shard_map/prefix/pallas_call | solution.py:278
  48.8 1.9 %collective-permute-done.1.refs_1_ = bf16[128,2304]{1,0:T(8,128)(2,1)S(1)} collective-permute-done((bf16[128,2304]{1,0:T(8,128)(2,1)S(1)}, bf16[128,2304]{1,0:T(8,128)(2,1)S(1)}, u32[]{:S(2)}, u32[]{:S(2)}) %collective-permute-start.1) | collective-permute-done | bytes 589856 | tf_op jit(solution)/shard_map/ppermute | solution.py:428
  50.7 3.3 %prefix.3 = bf16[16,112,128]{2,1,0:T(8,128)(2,1)} custom-call(bf16[16,96,128]{2,1,0:T(8,128)(2,1)S(1)} %all-to-all-done.recv_ref.refs_0_, bf16[128,2304]{1,0:T(8,128)(2,1)S(1)} %collective-permute-done.1.refs_1_, bf16[16,112,128]{2,1,0:T(8,128)(2,1)} %prefix.2.refs_2_), custom_call_target="tpu_custom_call", output_to_operand_aliasing={{}: (2, {})} | custom-call | flops 2500000000 | bytes 1000000 | tf_op jit(solution)/shard_map/prefix/pallas_call | solution.py:278
  54.1 10.9 %all-to-all-start.1 = ((bf16[16,112,128]{2,1,0:T(8,128)(2,1)}), bf16[16,112,128]{2,1,0:T(8,128)(2,1)S(1)}, u32[]{:S(2)}, u32[]{:S(2)}) async-start(bf16[16,112,128]{2,1,0:T(8,128)(2,1)} %prefix.3), calls=%async_computation.1 | async-start | bytes 917504 | tf_op jit(solution)/shard_map/all_to_all | solution.py:441
  64.9 19.0 %all-to-all-done.1.ret_ref = bf16[16,112,128]{2,1,0:T(8,128)(2,1)S(1)} async-done(((bf16[16,112,128]{2,1,0:T(8,128)(2,1)}), bf16[16,112,128]{2,1,0:T(8,128)(2,1)S(1)}, u32[]{:S(2)}, u32[]{:S(2)}) %all-to-all-start.1) | async-done | bytes 458784 | tf_op jit(solution)/shard_map/all_to_all | solution.py:441
  84.0 0.0 copy-start.1
  84.0 0.8 copy-done.1
  84.8 5.6 %merge.1 = (bf16[4,192,360]{2,1,0:T(8,128)(2,1)}, bf16[192,512]{1,0:T(8,128)(2,1)}) custom-call(s32[1]{0:T(128)} %bitcast.core_ref, s32[64]{0:T(128)} %get-tuple-element.16.code_ref, bf16[16,112,128]{2,1,0:T(8,128)(2,1)} %copy-done.1, f32[1024,128]{1,0:T(8,128)} %get-tuple-element.23.suffix_ref, f32[1024,128]{1,0:T(8,128)} %get-tuple-element.24.suffix_lse_ref, ...), custom_call_target="tpu_custom_call" | custom-call | tf_op jit(solution)/shard_map/merge/pallas_call | solution.py:365
  90.4 9.4 %collective-permute-start.3 = (bf16[4,192,360]{2,1,0:T(8,128)(2,1)}, bf16[4,192,360]{2,1,0:T(8,128)(2,1)S(1)}, u32[]{:S(2)}, u32[]{:S(2)}) collective-permute-start(bf16[4,192,360]{2,1,0:T(8,128)(2,1)} %get-tuple-element.26), channel_id=1, source_target_pairs={{0,1},{1,0},{2,3},{3,2},{4,5},{5,4},{6,7},{7,6},{8,9},{9,8},{10,11... | collective-permute-start | bytes 1658888 | tf_op jit(solution)/shard_map/ppermute | solution.py:389
  99.9 4.0 %project.1 = bf16[4,192,360]{2,1,0:T(8,128)(2,1)} custom-call(s32[1]{0:T(128)} %bitcast.core_ref, bf16[192,512]{1,0:T(8,128)(2,1)} %get-tuple-element.25.left_ref, bf16[8,360,512]{2,1,0:T(8,128)(2,1)} %bitcast.18), custom_call_target="tpu_custom_call" | custom-call | flops 2000000000 | bytes 2000000 | tf_op jit(solution)/shard_map/project/pallas_call | solution.py:390
  103.9 0.0 collective-permute-done.3
  103.9 1.2 %add_convert_fusion = bf16[4,192,360]{2,1,0:T(8,128)(2,1)S(1)} fusion(bf16[4,192,360]{2,1,0:T(8,128)(2,1)S(1)} %collective-permute-done.3, bf16[4,192,360]{2,1,0:T(8,128)(2,1)} %project.1), kind=kLoop, calls=%fused_computation | loop fusion | flops 1105920 | bytes 1658880 | tf_op jit(solution)/shard_map/convert_element_type | solution.py:408
  105.1 13.7 %all_to_all.15 = bf16[4,192,360]{2,1,0:T(8,128)(2,1)S(1)} all-to-all(bf16[4,192,360]{2,1,0:T(8,128)(2,1)S(1)} %add_convert_fusion), channel_id=1, replica_groups={{0,2,4,6},{1,3,5,7},{8,10,12,14},{9,11,13,15},{16,18,20,22},{17,19,21,2..., dimensions={0} | all-to-all | bytes 1105920 | tf_op jit(solution)/shard_map/all_to_all | solution.py:447
  118.8 0.8 reduce_sum.12
Async XLA Ops:
  2.7 37.3 %all-to-all-start = ((bf16[16,96,128]{2,1,0:T(8,128)(2,1)}), bf16[16,96,128]{2,1,0:T(8,128)(2,1)S(1)}, u32[]{:S(2)}, u32[]{:S(2)}) async-start(bf16[16,96,128]{2,1,0:T(8,128)(2,1)} %get-tuple-element.18), calls=%async_computation | async-start | bytes 786432 | tf_op jit(solution)/shard_map/all_to_all | solution.py:433
  18.4 16.4 %collective-permute-start = (bf16[128,2304]{1,0:T(8,128)(2,1)}, bf16[128,2304]{1,0:T(8,128)(2,1)S(1)}, u32[]{:S(2)}, u32[]{:S(2)}) collective-permute-start(bf16[128,2304]{1,0:T(8,128)(2,1)} %bitcast.14), channel_id=1, source_target_pairs={{8,0},{16,8},{24,16},{0,24},{40,32},{48,40},{56,48},{32,56},{72,64... | collective-permute-start | bytes 1769480 | tf_op jit(solution)/shard_map/ppermute | solution.py:428
  22.8 17.2 %collective-permute-start.2 = (bf16[128,2304]{1,0:T(8,128)(2,1)}, bf16[128,2304]{1,0:T(8,128)(2,1)S(1)}, u32[]{:S(2)}, u32[]{:S(2)}) collective-permute-start(bf16[128,2304]{1,0:T(8,128)(2,1)} %bitcast.15), channel_id=1, source_target_pairs={{24,0},{0,8},{8,16},{16,24},{56,32},{32,40},{40,48},{48,56},{88,64... | collective-permute-start | bytes 1769480 | tf_op jit(solution)/shard_map/ppermute | solution.py:428
  24.7 15.3 %copy-start = (bf16[1,1,128,2304]{3,2,1,0:T(8,128)(2,1)S(1)}, bf16[1,1,128,2304]{3,2,1,0:T(8,128)(2,1)}, u32[]{:S(2)}) copy-start(bf16[1,1,128,2304]{3,2,1,0:T(8,128)(2,1)} %param.8) | copy-start | bytes 1769476
  34.8 15.9 %collective-permute-start.1 = (bf16[128,2304]{1,0:T(8,128)(2,1)S(1)}, bf16[128,2304]{1,0:T(8,128)(2,1)S(1)}, u32[]{:S(2)}, u32[]{:S(2)}) collective-permute-start(bf16[128,2304]{1,0:T(8,128)(2,1)S(1)} %collective-permute-done.refs_1_), channel_id=1, source_target_pairs={{8,0},{16,8},{24,16},{0,24},{40,32},{48,40},{56,48},{32,56},{72,64... | collective-permute-start | bytes 1769480 | tf_op jit(solution)/shard_map/ppermute | solution.py:428
  54.1 29.9 %all-to-all-start.1 = ((bf16[16,112,128]{2,1,0:T(8,128)(2,1)}), bf16[16,112,128]{2,1,0:T(8,128)(2,1)S(1)}, u32[]{:S(2)}, u32[]{:S(2)}) async-start(bf16[16,112,128]{2,1,0:T(8,128)(2,1)} %prefix.3), calls=%async_computation.1 | async-start | bytes 917504 | tf_op jit(solution)/shard_map/all_to_all | solution.py:441
  84.0 0.8 copy-start.1
  90.4 13.5 %collective-permute-start.3 = (bf16[4,192,360]{2,1,0:T(8,128)(2,1)}, bf16[4,192,360]{2,1,0:T(8,128)(2,1)S(1)}, u32[]{:S(2)}, u32[]{:S(2)}) collective-permute-start(bf16[4,192,360]{2,1,0:T(8,128)(2,1)} %get-tuple-element.26), channel_id=1, source_target_pairs={{0,1},{1,0},{2,3},{3,2},{4,5},{5,4},{6,7},{7,6},{8,9},{9,8},{10,11... | collective-permute-start | bytes 1658888 | tf_op jit(solution)/shard_map/ppermute | solution.py:389

commit v7 on v6

--- a/solution.py
+++ b/solution.py
@@ -346,11 +346,13 @@
                     pl.ds(step * pairs + pair, requests, stride=PAD_ROWS), :
                 ].astype(jnp.bfloat16)
 
-    out_ref[0] = nt_dot(left[...], w_ref[0]).astype(jnp.bfloat16)
+    for part in range(w_ref.shape[0]):
+        out_ref[part] = nt_dot(left[...], w_ref[part, 0]).astype(jnp.bfloat16)
 
 
 def project_kernel(core_ref, left_ref, w_ref, out_ref):
-    out_ref[0] = nt_dot(left_ref[...], w_ref[0]).astype(jnp.bfloat16)
+    for part in range(w_ref.shape[0]):
+        out_ref[part] = nt_dot(left_ref[...], w_ref[part, core_ref[0]]).astype(jnp.bfloat16)
 
 
 def merge_project(core, codes, ret, suffix_out, suffix_lse, weights, parts):
@@ -358,22 +360,22 @@
     width = weights.shape[0] // parts
     depth = weights.shape[1]
     rows = STEPS * requests
-    weights = weights.reshape(parts, width, depth)
+    weights = weights.reshape(parts // CORES, CORES, width, depth)
     whole = lambda shape: pl.BlockSpec(shape, lambda t, core: (0,) * len(shape))
-    out_spec = pl.BlockSpec((1, rows, width), lambda t, core: (t, 0, 0))
+    out_spec = whole((parts // CORES, rows, width))
     out_shape = jax.ShapeDtypeStruct((parts // CORES, rows, width), jnp.bfloat16)
     other, left = pl.pallas_call(
         merge_kernel,
         out_shape=(out_shape, jax.ShapeDtypeStruct((rows, depth), jnp.bfloat16)),
         grid_spec=pltpu.PrefetchScalarGridSpec(
             num_scalar_prefetch=1,
-            grid=(parts // CORES,),
+            grid=(1,),
             in_specs=[
                 pl.BlockSpec(memory_space=pltpu.SMEM),
                 whole(ret.shape),
                 whole(suffix_out.shape),
                 whole(suffix_lse.shape),
-                pl.BlockSpec((1, width, depth), lambda t, core: (t * CORES + 1 - core[0], 0, 0)),
+                pl.BlockSpec((parts // CORES, 1, width, depth), lambda t, core: (0, 1 - core[0], 0, 0)),
             ],
             out_specs=(out_spec, whole((rows, depth))),
             scratch_shapes=[
@@ -387,19 +389,13 @@
         name="merge",
     )(core, codes, ret, suffix_out, suffix_lse, weights)
     received = lax.ppermute(other, "tensor", [(i, i ^ 1) for i in range(parts)])
+    vmem = pl.BlockSpec(memory_space=pltpu.VMEM)
     own = pl.pallas_call(
         project_kernel,
         out_shape=out_shape,
-        grid_spec=pltpu.PrefetchScalarGridSpec(
-            num_scalar_prefetch=1,
-            grid=(parts // CORES,),
-            in_specs=[
-                whole((rows, depth)),
-                pl.BlockSpec((1, width, depth), lambda t, core: (t * CORES + core[0], 0, 0)),
-            ],
-            out_specs=out_spec,
-        ),
-        compiler_params=pltpu.CompilerParams(vmem_limit_bytes=VMEM_LIMIT),
+        in_specs=[pl.BlockSpec(memory_space=pltpu.SMEM), vmem, vmem],
+        out_specs=vmem,
+        compiler_params=pltpu.CompilerParams(vmem_limit_bytes=SMALL_LIMIT),
         cost_estimate=pl.CostEstimate(
             flops=2_000_000_000, bytes_accessed=2_000_000, transcendentals=0
         ),
@@ -427,7 +423,7 @@
         ]
         return lax.ppermute(array, "prefix", pairs)
 
-    right = from_offset(kv_out, 1)
+    right = from_offset(kv, 1)
     left = from_offset(kv_out, -1)
     opposite = from_offset(right, 1)
     recv = lax.all_to_all(

time: 121 us -> 117 us (0.967)
  Pallas kernels: 33.2 us -> 28.8 us
    pallas_call x1, Pallas kernels: 3.99 us -> 0.66 us  [merge_project(): pl.pallas_call(project_kernel, out_shape=out_shape, in_specs=[pl.BlockSpe...]
  transfers between devices with their start and end apart: 6 -> 6, of which waited for: 3 -> 4; matrix products, arithmetic and copies ran while one was open for 0% -> 0% of each run, Pallas kernels for 18% -> 16%
where the time goes in v7:
time: 117 us; the launch traced here: 115 us
  starting transfers between devices  47.6 us (41%)
  Pallas kernels  28.8 us (25%)
  waiting for transfers between devices  22.4 us (19%)
  blocking collectives  13.6 us (12%)
  local copies, waits for them, and re-layouts  1.72 us (1%)
    all_to_all x1, waiting for transfers between devices, shards(): lax.all_to_all(ret, 'prefix', split_axis=0, concat_axis=0, axis_index_gro...  19 us
    all_to_all x1, starting transfers between devices, shards(): lax.all_to_all(send, 'prefix', split_axis=0, concat_axis=0, axis_index_gr...  15.8 us
    all_to_all x1, blocking collectives, shards(): lax.all_to_all(parts, 'tensor', split_axis=0, concat_axis=0, axis_index_g...  13.6 us
    pallas_call x2, Pallas kernels, prefix_attention(): pl.pallas_call(kernel, grid=(count,), out_shape=jax.ShapeDtypeStruct((z_s...  12.1 us
    ppermute x3, starting transfers between devices, from_offset(): return lax.ppermute(array, 'prefix', pairs)  11.5 us
    all_to_all x1, starting transfers between devices, shards(): lax.all_to_all(ret, 'prefix', split_axis=0, concat_axis=0, axis_index_gro...  10.9 us
    ppermute x1, starting transfers between devices, merge_project(): received = lax.ppermute(other, 'tensor', [(i, i ^ 1) for i in range(parts)])  9.45 us
    pallas_call x1, Pallas kernels, suffix_attention(): pl.pallas_call(suffix_kernel, out_shape=(shape, shape), in_specs=[pl.Bloc...  8.78 us
  transfers between devices with their start and end apart: 6, of which 4 were waited for; matrix products, arithmetic and copies ran while one was open for 0% of the time, Pallas kernels for 16%

profile of v7, /device:TPU:1, one launch (start us, length us, event | category | flops | bytes accessed | tf_op | source)
XLA Modules:
  0.0 115.2 jit_solution(7488059228952217956)
XLA Ops:
  0.0 2.6 %route.1 = (bf16[16,96,128]{2,1,0:T(8,128)(2,1)}, s32[64]{0:T(128)}) custom-call(s32[1]{0:T(128)} %bitcast.1.me_ref, s32[4096]{0:T(1024)} %bitcast.21, s32[64]{0:T(128)} %owner_ref.1, bf16[3,64,512]{2,1,0:T(8,128)(2,1)} %bitcast.19), custom_call_target="tpu_custom_call" | custom-call | tf_op jit(solution)/shard_map/route/pallas_call | solution.py:97
  2.7 15.8 %all-to-all-start = ((bf16[16,96,128]{2,1,0:T(8,128)(2,1)}), bf16[16,96,128]{2,1,0:T(8,128)(2,1)S(1)}, u32[]{:S(2)}, u32[]{:S(2)}) async-start(bf16[16,96,128]{2,1,0:T(8,128)(2,1)} %get-tuple-element.18), calls=%async_computation | async-start | bytes 786432 | tf_op jit(solution)/shard_map/all_to_all | solution.py:429
  18.4 4.4 %collective-permute-start = (bf16[128,2304]{1,0:T(8,128)(2,1)}, bf16[128,2304]{1,0:T(8,128)(2,1)S(1)}, u32[]{:S(2)}, u32[]{:S(2)}) collective-permute-start(bf16[128,2304]{1,0:T(8,128)(2,1)} %bitcast.16), channel_id=1, source_target_pairs={{8,0},{16,8},{24,16},{0,24},{40,32},{48,40},{56,48},{32,56},{72,64... | collective-permute-start | bytes 1769480 | tf_op jit(solution)/shard_map/ppermute | solution.py:424
  22.8 1.9 %collective-permute-start.2 = (bf16[128,2304]{1,0:T(8,128)(2,1)}, bf16[128,2304]{1,0:T(8,128)(2,1)S(1)}, u32[]{:S(2)}, u32[]{:S(2)}) collective-permute-start(bf16[128,2304]{1,0:T(8,128)(2,1)} %bitcast.17), channel_id=1, source_target_pairs={{24,0},{0,8},{8,16},{16,24},{56,32},{32,40},{40,48},{48,56},{88,64... | collective-permute-start | bytes 1769480 | tf_op jit(solution)/shard_map/ppermute | solution.py:424
  24.7 0.0 copy-start.1
  24.8 8.8 %suffix.1 = (f32[1024,128]{1,0:T(8,128)}, f32[1024,128]{1,0:T(8,128)}) custom-call(s32[64]{0:T(128)} %length_ref.1, bf16[3,64,512]{2,1,0:T(8,128)(2,1)} %bitcast.20, bf16[64,80,128]{2,1,0:T(8,128)(2,1)} %bitcast.22), custom_call_target="tpu_custom_call" | custom-call | flops 8000000000 | bytes 8000000 | tf_op jit(solution)/shard_map/suffix/pallas_call | solution.py:158
  33.5 1.2 %collective-permute-done.refs_1_ = bf16[128,2304]{1,0:T(8,128)(2,1)S(1)} collective-permute-done((bf16[128,2304]{1,0:T(8,128)(2,1)}, bf16[128,2304]{1,0:T(8,128)(2,1)S(1)}, u32[]{:S(2)}, u32[]{:S(2)}) %collective-permute-start) | collective-permute-done | bytes 589856 | tf_op jit(solution)/shard_map/ppermute | solution.py:424
  34.8 5.2 %collective-permute-start.1 = (bf16[128,2304]{1,0:T(8,128)(2,1)S(1)}, bf16[128,2304]{1,0:T(8,128)(2,1)S(1)}, u32[]{:S(2)}, u32[]{:S(2)}) collective-permute-start(bf16[128,2304]{1,0:T(8,128)(2,1)S(1)} %collective-permute-done.refs_1_), channel_id=1, source_target_pairs={{8,0},{16,8},{24,16},{0,24},{40,32},{48,40},{56,48},{32,56},{72,64... | collective-permute-start | bytes 1769480 | tf_op jit(solution)/shard_map/ppermute | solution.py:424
  40.0 0.0 all-to-all-done.recv_ref.refs_0_
  40.0 0.0 collective-permute-done.2.refs_2_
  40.0 0.0 copy-done.1
  40.0 8.8 %prefix.2.refs_2_ = bf16[16,112,128]{2,1,0:T(8,128)(2,1)} custom-call(bf16[16,96,128]{2,1,0:T(8,128)(2,1)S(1)} %all-to-all-done.recv_ref.refs_0_, bf16[128,2304]{1,0:T(8,128)(2,1)S(1)} %bitcast.18, bf16[128,2304]{1,0:T(8,128)(2,1)S(1)} %collective-permute-done.refs_1_, bf16[128,2304]{1,0:T(8,128)(2,1)S(1)} %collective-permute-done.2.refs_2_), custom_call_target="tpu_custom_call" | custom-call | flops 7500000256 | bytes 3000000 | tf_op jit(solution)/shard_map/prefix/pallas_call | solution.py:278
  48.8 1.9 %collective-permute-done.1.refs_1_ = bf16[128,2304]{1,0:T(8,128)(2,1)S(1)} collective-permute-done((bf16[128,2304]{1,0:T(8,128)(2,1)S(1)}, bf16[128,2304]{1,0:T(8,128)(2,1)S(1)}, u32[]{:S(2)}, u32[]{:S(2)}) %collective-permute-start.1) | collective-permute-done | bytes 589856 | tf_op jit(solution)/shard_map/ppermute | solution.py:424
  50.7 3.3 %prefix.3 = bf16[16,112,128]{2,1,0:T(8,128)(2,1)} custom-call(bf16[16,96,128]{2,1,0:T(8,128)(2,1)S(1)} %all-to-all-done.recv_ref.refs_0_, bf16[128,2304]{1,0:T(8,128)(2,1)S(1)} %collective-permute-done.1.refs_1_, bf16[16,112,128]{2,1,0:T(8,128)(2,1)} %prefix.2.refs_2_), custom_call_target="tpu_custom_call", output_to_operand_aliasing={{}: (2, {})} | custom-call | flops 2500000000 | bytes 1000000 | tf_op jit(solution)/shard_map/prefix/pallas_call | solution.py:278
  54.0 10.9 %all-to-all-start.1 = ((bf16[16,112,128]{2,1,0:T(8,128)(2,1)}), bf16[16,112,128]{2,1,0:T(8,128)(2,1)S(1)}, u32[]{:S(2)}, u32[]{:S(2)}) async-start(bf16[16,112,128]{2,1,0:T(8,128)(2,1)} %prefix.3), calls=%async_computation.1 | async-start | bytes 917504 | tf_op jit(solution)/shard_map/all_to_all | solution.py:437
  64.9 19.0 %all-to-all-done.1.ret_ref = bf16[16,112,128]{2,1,0:T(8,128)(2,1)S(1)} async-done(((bf16[16,112,128]{2,1,0:T(8,128)(2,1)}), bf16[16,112,128]{2,1,0:T(8,128)(2,1)S(1)}, u32[]{:S(2)}, u32[]{:S(2)}) %all-to-all-start.1) | async-done | bytes 458784 | tf_op jit(solution)/shard_map/all_to_all | solution.py:437
  84.0 0.0 copy-start.3
  84.0 0.8 copy-done.3
  84.8 0.0 copy-start
  84.8 4.6 %merge.1 = (bf16[4,192,360]{2,1,0:T(8,128)(2,1)}, bf16[192,512]{1,0:T(8,128)(2,1)}) custom-call(s32[1]{0:T(128)} %bitcast.core_ref, s32[64]{0:T(128)} %get-tuple-element.16.code_ref, bf16[16,112,128]{2,1,0:T(8,128)(2,1)} %copy-done.3, f32[1024,128]{1,0:T(8,128)} %get-tuple-element.23.suffix_ref, f32[1024,128]{1,0:T(8,128)} %get-tuple-element.24.suffix_lse_ref, ...), custom_call_target="tpu_custom_call" | custom-call | tf_op jit(solution)/shard_map/merge/pallas_call | solution.py:367
  89.4 9.5 %collective-permute-start.3 = (bf16[4,192,360]{2,1,0:T(8,128)(2,1)}, bf16[4,192,360]{2,1,0:T(8,128)(2,1)S(1)}, u32[]{:S(2)}, u32[]{:S(2)}) collective-permute-start(bf16[4,192,360]{2,1,0:T(8,128)(2,1)} %get-tuple-element.26), channel_id=1, source_target_pairs={{0,1},{1,0},{2,3},{3,2},{4,5},{5,4},{6,7},{7,6},{8,9},{9,8},{10,11... | collective-permute-start | bytes 1658888 | tf_op jit(solution)/shard_map/ppermute | solution.py:391
  98.8 0.0 copy-done
  98.9 0.0 copy-start.2
  98.9 0.9 copy-done.2
  99.8 0.7 project.1
  100.5 0.2 collective-permute-done.3
  100.7 0.1 add_convert_fusion
  100.8 13.6 %all_to_all.15 = bf16[4,192,360]{2,1,0:T(8,128)(2,1)S(1)} all-to-all(bf16[4,192,360]{2,1,0:T(8,128)(2,1)S(1)} %add_convert_fusion), channel_id=1, replica_groups={{0,2,4,6},{1,3,5,7},{8,10,12,14},{9,11,13,15},{16,18,20,22},{17,19,21,2..., dimensions={0} | all-to-all | bytes 1105920 | tf_op jit(solution)/shard_map/all_to_all | solution.py:443
  114.4 0.8 reduce_sum.12
Async XLA Ops:
  2.7 37.3 %all-to-all-start = ((bf16[16,96,128]{2,1,0:T(8,128)(2,1)}), bf16[16,96,128]{2,1,0:T(8,128)(2,1)S(1)}, u32[]{:S(2)}, u32[]{:S(2)}) async-start(bf16[16,96,128]{2,1,0:T(8,128)(2,1)} %get-tuple-element.18), calls=%async_computation | async-start | bytes 786432 | tf_op jit(solution)/shard_map/all_to_all | solution.py:429
  18.4 16.4 %collective-permute-start = (bf16[128,2304]{1,0:T(8,128)(2,1)}, bf16[128,2304]{1,0:T(8,128)(2,1)S(1)}, u32[]{:S(2)}, u32[]{:S(2)}) collective-permute-start(bf16[128,2304]{1,0:T(8,128)(2,1)} %bitcast.16), channel_id=1, source_target_pairs={{8,0},{16,8},{24,16},{0,24},{40,32},{48,40},{56,48},{32,56},{72,64... | collective-permute-start | bytes 1769480 | tf_op jit(solution)/shard_map/ppermute | solution.py:424
  22.8 17.2 %collective-permute-start.2 = (bf16[128,2304]{1,0:T(8,128)(2,1)}, bf16[128,2304]{1,0:T(8,128)(2,1)S(1)}, u32[]{:S(2)}, u32[]{:S(2)}) collective-permute-start(bf16[128,2304]{1,0:T(8,128)(2,1)} %bitcast.17), channel_id=1, source_target_pairs={{24,0},{0,8},{8,16},{16,24},{56,32},{32,40},{40,48},{48,56},{88,64... | collective-permute-start | bytes 1769480 | tf_op jit(solution)/shard_map/ppermute | solution.py:424
  24.7 15.3 %copy-start.1 = (bf16[1,1,128,2304]{3,2,1,0:T(8,128)(2,1)S(1)}, bf16[1,1,128,2304]{3,2,1,0:T(8,128)(2,1)}, u32[]{:S(2)}) copy-start(bf16[1,1,128,2304]{3,2,1,0:T(8,128)(2,1)} %param.8) | copy-start | bytes 1769476
  34.8 15.9 %collective-permute-start.1 = (bf16[128,2304]{1,0:T(8,128)(2,1)S(1)}, bf16[128,2304]{1,0:T(8,128)(2,1)S(1)}, u32[]{:S(2)}, u32[]{:S(2)}) collective-permute-start(bf16[128,2304]{1,0:T(8,128)(2,1)S(1)} %collective-permute-done.refs_1_), channel_id=1, source_target_pairs={{8,0},{16,8},{24,16},{0,24},{40,32},{48,40},{56,48},{32,56},{72,64... | collective-permute-start | bytes 1769480 | tf_op jit(solution)/shard_map/ppermute | solution.py:424
  54.0 29.9 %all-to-all-start.1 = ((bf16[16,112,128]{2,1,0:T(8,128)(2,1)}), bf16[16,112,128]{2,1,0:T(8,128)(2,1)S(1)}, u32[]{:S(2)}, u32[]{:S(2)}) async-start(bf16[16,112,128]{2,1,0:T(8,128)(2,1)} %prefix.3), calls=%async_computation.1 | async-start | bytes 917504 | tf_op jit(solution)/shard_map/all_to_all | solution.py:437
  84.0 0.8 copy-start.3
  84.8 14.1 %copy-start = (bf16[512,2880]{0,1:T(8,128)(2,1)S(1)}, bf16[512,2880]{0,1:T(8,128)(2,1)}, u32[]{:S(2)}) copy-start(bf16[512,2880]{0,1:T(8,128)(2,1)} %param.13) | copy-start | bytes 8847364
  89.4 11.3 %collective-permute-start.3 = (bf16[4,192,360]{2,1,0:T(8,128)(2,1)}, bf16[4,192,360]{2,1,0:T(8,128)(2,1)S(1)}, u32[]{:S(2)}, u32[]{:S(2)}) collective-permute-start(bf16[4,192,360]{2,1,0:T(8,128)(2,1)} %get-tuple-element.26), channel_id=1, source_target_pairs={{0,1},{1,0},{2,3},{3,2},{4,5},{5,4},{6,7},{7,6},{8,9},{9,8},{10,11... | collective-permute-start | bytes 1658888 | tf_op jit(solution)/shard_map/ppermute | solution.py:391
  98.9 0.9 copy-start.2

commit v8 on v7

--- a/solution.py
+++ b/solution.py
@@ -19,6 +19,7 @@
 SCALE = 0.125
 VMEM_LIMIT = 56 * 1024 * 1024
 SMALL_LIMIT = 32 * 1024 * 1024
+MERGE_LIMIT = 52 * 1024 * 1024
 
 
 def lane_iota(rows):
@@ -385,7 +386,7 @@
                 pltpu.VMEM((requests * PAD_ROWS, LANES), jnp.float32),
             ],
         ),
-        compiler_params=pltpu.CompilerParams(vmem_limit_bytes=VMEM_LIMIT),
+        compiler_params=pltpu.CompilerParams(vmem_limit_bytes=MERGE_LIMIT),
         name="merge",
     )(core, codes, ret, suffix_out, suffix_lse, weights)
     received = lax.ppermute(other, "tensor", [(i, i ^ 1) for i in range(parts)])

time: 117 us -> 116 us (level)
  local copies, waits for them, and re-layouts: 1.72 us -> 0.02 us
    unnamed x8 -> x10, local copies, waits for them, and re-layouts: 1.72 us -> 0.02 us
where the time goes in v8:
time: 116 us; the launch traced here: 114 us
  starting transfers between devices  47.7 us (41%)
  Pallas kernels  28.4 us (24%)
  waiting for transfers between devices  23.3 us (20%)
  blocking collectives  13.6 us (12%)
    all_to_all x1, waiting for transfers between devices, shards(): lax.all_to_all(ret, 'prefix', split_axis=0, concat_axis=0, axis_index_gro...  19 us
    all_to_all x1, starting transfers between devices, shards(): lax.all_to_all(send, 'prefix', split_axis=0, concat_axis=0, axis_index_gr...  15.8 us
    all_to_all x1, blocking collectives, shards(): lax.all_to_all(parts, 'tensor', split_axis=0, concat_axis=0, axis_index_g...  13.6 us
    pallas_call x2, Pallas kernels, prefix_attention(): pl.pallas_call(kernel, grid=(count,), out_shape=jax.ShapeDtypeStruct((z_s...  12.1 us
    ppermute x3, starting transfers between devices, from_offset(): return lax.ppermute(array, 'prefix', pairs)  11.5 us
    all_to_all x1, starting transfers between devices, shards(): lax.all_to_all(ret, 'prefix', split_axis=0, concat_axis=0, axis_index_gro...  11 us
    ppermute x1, starting transfers between devices, merge_project(): received = lax.ppermute(other, 'tensor', [(i, i ^ 1) for i in range(parts)])  9.45 us
    pallas_call x1, Pallas kernels, suffix_attention(): pl.pallas_call(suffix_kernel, out_shape=(shape, shape), in_specs=[pl.Bloc...  8.77 us
  transfers between devices with their start and end apart: 6, of which 4 were waited for; matrix products, arithmetic and copies ran while one was open for 0% of the time, Pallas kernels for 16%

profile of v8, /device:TPU:1, one launch (start us, length us, event | category | flops | bytes accessed | tf_op | source)
XLA Modules:
  0.0 114.1 jit_solution(11018520315213621012)
XLA Ops:
  0.0 2.7 %route.1 = (bf16[16,96,128]{2,1,0:T(8,128)(2,1)}, s32[64]{0:T(128)}) custom-call(s32[1]{0:T(128)} %bitcast.1.me_ref, s32[4096]{0:T(1024)} %bitcast.21, s32[64]{0:T(128)} %owner_ref.1, bf16[3,64,512]{2,1,0:T(8,128)(2,1)} %bitcast.19), custom_call_target="tpu_custom_call" | custom-call | tf_op jit(solution)/shard_map/route/pallas_call | solution.py:98
  2.7 15.8 %all-to-all-start = ((bf16[16,96,128]{2,1,0:T(8,128)(2,1)}), bf16[16,96,128]{2,1,0:T(8,128)(2,1)S(1)}, u32[]{:S(2)}, u32[]{:S(2)}) async-start(bf16[16,96,128]{2,1,0:T(8,128)(2,1)} %get-tuple-element.18), calls=%async_computation | async-start | bytes 786432 | tf_op jit(solution)/shard_map/all_to_all | solution.py:430
  18.4 4.4 %collective-permute-start = (bf16[128,2304]{1,0:T(8,128)(2,1)}, bf16[128,2304]{1,0:T(8,128)(2,1)S(1)}, u32[]{:S(2)}, u32[]{:S(2)}) collective-permute-start(bf16[128,2304]{1,0:T(8,128)(2,1)} %bitcast.16), channel_id=1, source_target_pairs={{8,0},{16,8},{24,16},{0,24},{40,32},{48,40},{56,48},{32,56},{72,64... | collective-permute-start | bytes 1769480 | tf_op jit(solution)/shard_map/ppermute | solution.py:425
  22.8 1.9 %collective-permute-start.2 = (bf16[128,2304]{1,0:T(8,128)(2,1)}, bf16[128,2304]{1,0:T(8,128)(2,1)S(1)}, u32[]{:S(2)}, u32[]{:S(2)}) collective-permute-start(bf16[128,2304]{1,0:T(8,128)(2,1)} %bitcast.17), channel_id=1, source_target_pairs={{24,0},{0,8},{8,16},{16,24},{56,32},{32,40},{40,48},{48,56},{88,64... | collective-permute-start | bytes 1769480 | tf_op jit(solution)/shard_map/ppermute | solution.py:425
  24.8 0.0 copy-start.4
  24.8 8.8 %suffix.1 = (f32[1024,128]{1,0:T(8,128)}, f32[1024,128]{1,0:T(8,128)}) custom-call(s32[64]{0:T(128)} %length_ref.1, bf16[3,64,512]{2,1,0:T(8,128)(2,1)} %bitcast.20, bf16[64,80,128]{2,1,0:T(8,128)(2,1)} %bitcast.22), custom_call_target="tpu_custom_call" | custom-call | flops 8000000000 | bytes 8000000 | tf_op jit(solution)/shard_map/suffix/pallas_call | solution.py:159
  33.5 1.3 %collective-permute-done.refs_1_ = bf16[128,2304]{1,0:T(8,128)(2,1)S(1)} collective-permute-done((bf16[128,2304]{1,0:T(8,128)(2,1)}, bf16[128,2304]{1,0:T(8,128)(2,1)S(1)}, u32[]{:S(2)}, u32[]{:S(2)}) %collective-permute-start) | collective-permute-done | bytes 589856 | tf_op jit(solution)/shard_map/ppermute | solution.py:425
  34.8 5.2 %collective-permute-start.1 = (bf16[128,2304]{1,0:T(8,128)(2,1)S(1)}, bf16[128,2304]{1,0:T(8,128)(2,1)S(1)}, u32[]{:S(2)}, u32[]{:S(2)}) collective-permute-start(bf16[128,2304]{1,0:T(8,128)(2,1)S(1)} %collective-permute-done.refs_1_), channel_id=1, source_target_pairs={{8,0},{16,8},{24,16},{0,24},{40,32},{48,40},{56,48},{32,56},{72,64... | collective-permute-start | bytes 1769480 | tf_op jit(solution)/shard_map/ppermute | solution.py:425
  40.0 0.0 all-to-all-done.recv_ref.refs_0_
  40.0 0.0 collective-permute-done.2.refs_2_
  40.0 0.0 copy-done.4
  40.0 8.8 %prefix.2.refs_2_ = bf16[16,112,128]{2,1,0:T(8,128)(2,1)} custom-call(bf16[16,96,128]{2,1,0:T(8,128)(2,1)S(1)} %all-to-all-done.recv_ref.refs_0_, bf16[128,2304]{1,0:T(8,128)(2,1)S(1)} %bitcast.18, bf16[128,2304]{1,0:T(8,128)(2,1)S(1)} %collective-permute-done.refs_1_, bf16[128,2304]{1,0:T(8,128)(2,1)S(1)} %collective-permute-done.2.refs_2_), custom_call_target="tpu_custom_call" | custom-call | flops 7500000256 | bytes 3000000 | tf_op jit(solution)/shard_map/prefix/pallas_call | solution.py:279
  48.9 0.0 copy-start.3
  48.9 1.9 %collective-permute-done.1.refs_1_ = bf16[128,2304]{1,0:T(8,128)(2,1)S(1)} collective-permute-done((bf16[128,2304]{1,0:T(8,128)(2,1)S(1)}, bf16[128,2304]{1,0:T(8,128)(2,1)S(1)}, u32[]{:S(2)}, u32[]{:S(2)}) %collective-permute-start.1) | collective-permute-done | bytes 589856 | tf_op jit(solution)/shard_map/ppermute | solution.py:425
  50.7 0.0 copy-start.2
  50.7 3.3 %prefix.3 = bf16[16,112,128]{2,1,0:T(8,128)(2,1)} custom-call(bf16[16,96,128]{2,1,0:T(8,128)(2,1)S(1)} %all-to-all-done.recv_ref.refs_0_, bf16[128,2304]{1,0:T(8,128)(2,1)S(1)} %collective-permute-done.1.refs_1_, bf16[16,112,128]{2,1,0:T(8,128)(2,1)} %prefix.2.refs_2_), custom_call_target="tpu_custom_call", output_to_operand_aliasing={{}: (2, {})} | custom-call | flops 2500000000 | bytes 1000000 | tf_op jit(solution)/shard_map/prefix/pallas_call | solution.py:279
  54.1 0.0 copy-start.1
  54.1 11.0 %all-to-all-start.1 = ((bf16[16,112,128]{2,1,0:T(8,128)(2,1)}), bf16[16,112,128]{2,1,0:T(8,128)(2,1)S(1)}, u32[]{:S(2)}, u32[]{:S(2)}) async-start(bf16[16,112,128]{2,1,0:T(8,128)(2,1)} %prefix.3), calls=%async_computation.1 | async-start | bytes 917504 | tf_op jit(solution)/shard_map/all_to_all | solution.py:438
  65.1 19.0 %all-to-all-done.1.ret_ref = bf16[16,112,128]{2,1,0:T(8,128)(2,1)S(1)} async-done(((bf16[16,112,128]{2,1,0:T(8,128)(2,1)}), bf16[16,112,128]{2,1,0:T(8,128)(2,1)S(1)}, u32[]{:S(2)}, u32[]{:S(2)}) %all-to-all-start.1) | async-done | bytes 458784 | tf_op jit(solution)/shard_map/all_to_all | solution.py:438
  84.2 0.0 copy-done.3
  84.2 0.0 copy-done.2
  84.2 0.0 copy-done.1
  84.2 0.0 copy-start
  84.2 4.2 %merge.1 = (bf16[4,192,360]{2,1,0:T(8,128)(2,1)}, bf16[192,512]{1,0:T(8,128)(2,1)S(1)}) custom-call(s32[1]{0:T(128)} %bitcast.core_ref, s32[64]{0:T(128)S(1)} %copy-done.3, bf16[16,112,128]{2,1,0:T(8,128)(2,1)S(1)} %all-to-all-done.1.ret_ref, f32[1024,128]{1,0:T(8,128)S(1)} %copy-done.1, f32[1024,128]{1,0:T(8,128)S(1)} %copy-done.2, ...), custom_call_target="tpu_custom_call" | custom-call | tf_op jit(solution)/shard_map/merge/pallas_call | solution.py:368
  88.3 9.5 %collective-permute-start.3 = (bf16[4,192,360]{2,1,0:T(8,128)(2,1)}, bf16[4,192,360]{2,1,0:T(8,128)(2,1)S(1)}, u32[]{:S(2)}, u32[]{:S(2)}) collective-permute-start(bf16[4,192,360]{2,1,0:T(8,128)(2,1)} %get-tuple-element.26), channel_id=1, source_target_pairs={{0,1},{1,0},{2,3},{3,2},{4,5},{5,4},{6,7},{7,6},{8,9},{9,8},{10,11... | collective-permute-start | bytes 1658888 | tf_op jit(solution)/shard_map/ppermute | solution.py:392
  97.8 0.0 copy-done
  97.8 0.7 project.1
  98.5 1.1 %collective-permute-done.3 = bf16[4,192,360]{2,1,0:T(8,128)(2,1)S(1)} collective-permute-done((bf16[4,192,360]{2,1,0:T(8,128)(2,1)}, bf16[4,192,360]{2,1,0:T(8,128)(2,1)S(1)}, u32[]{:S(2)}, u32[]{:S(2)}) %collective-permute-start.3) | collective-permute-done | bytes 552992 | tf_op jit(solution)/shard_map/ppermute | solution.py:392
  99.6 0.1 add_convert_fusion
  99.8 13.6 %all_to_all.15 = bf16[4,192,360]{2,1,0:T(8,128)(2,1)S(1)} all-to-all(bf16[4,192,360]{2,1,0:T(8,128)(2,1)S(1)} %add_convert_fusion), channel_id=1, replica_groups={{0,2,4,6},{1,3,5,7},{8,10,12,14},{9,11,13,15},{16,18,20,22},{17,19,21,2..., dimensions={0} | all-to-all | bytes 1105920 | tf_op jit(solution)/shard_map/all_to_all | solution.py:444
  113.4 0.8 reduce_sum.12
Async XLA Ops:
  2.7 37.3 %all-to-all-start = ((bf16[16,96,128]{2,1,0:T(8,128)(2,1)}), bf16[16,96,128]{2,1,0:T(8,128)(2,1)S(1)}, u32[]{:S(2)}, u32[]{:S(2)}) async-start(bf16[16,96,128]{2,1,0:T(8,128)(2,1)} %get-tuple-element.18), calls=%async_computation | async-start | bytes 786432 | tf_op jit(solution)/shard_map/all_to_all | solution.py:430
  18.4 16.4 %collective-permute-start = (bf16[128,2304]{1,0:T(8,128)(2,1)}, bf16[128,2304]{1,0:T(8,128)(2,1)S(1)}, u32[]{:S(2)}, u32[]{:S(2)}) collective-permute-start(bf16[128,2304]{1,0:T(8,128)(2,1)} %bitcast.16), channel_id=1, source_target_pairs={{8,0},{16,8},{24,16},{0,24},{40,32},{48,40},{56,48},{32,56},{72,64... | collective-permute-start | bytes 1769480 | tf_op jit(solution)/shard_map/ppermute | solution.py:425
  22.8 17.2 %collective-permute-start.2 = (bf16[128,2304]{1,0:T(8,128)(2,1)}, bf16[128,2304]{1,0:T(8,128)(2,1)S(1)}, u32[]{:S(2)}, u32[]{:S(2)}) collective-permute-start(bf16[128,2304]{1,0:T(8,128)(2,1)} %bitcast.17), channel_id=1, source_target_pairs={{24,0},{0,8},{8,16},{16,24},{56,32},{32,40},{40,48},{48,56},{88,64... | collective-permute-start | bytes 1769480 | tf_op jit(solution)/shard_map/ppermute | solution.py:425
  24.8 15.3 %copy-start.4 = (bf16[1,1,128,2304]{3,2,1,0:T(8,128)(2,1)S(1)}, bf16[1,1,128,2304]{3,2,1,0:T(8,128)(2,1)}, u32[]{:S(2)}) copy-start(bf16[1,1,128,2304]{3,2,1,0:T(8,128)(2,1)} %param.8) | copy-start | bytes 1769476
  34.8 15.9 %collective-permute-start.1 = (bf16[128,2304]{1,0:T(8,128)(2,1)S(1)}, bf16[128,2304]{1,0:T(8,128)(2,1)S(1)}, u32[]{:S(2)}, u32[]{:S(2)}) collective-permute-start(bf16[128,2304]{1,0:T(8,128)(2,1)S(1)} %collective-permute-done.refs_1_), channel_id=1, source_target_pairs={{8,0},{16,8},{24,16},{0,24},{40,32},{48,40},{56,48},{32,56},{72,64... | collective-permute-start | bytes 1769480 | tf_op jit(solution)/shard_map/ppermute | solution.py:425
  48.9 35.3 %copy-start.3 = (s32[64]{0:T(128)S(1)}, s32[64]{0:T(128)}, u32[]{:S(2)}) copy-start(s32[64]{0:T(128)} %get-tuple-element.16.code_ref) | copy-start | bytes 772
  50.7 33.4 %copy-start.2 = (f32[1024,128]{1,0:T(8,128)S(1)}, f32[1024,128]{1,0:T(8,128)}, u32[]{:S(2)}) copy-start(f32[1024,128]{1,0:T(8,128)} %get-tuple-element.24.suffix_lse_ref) | copy-start | bytes 1572868
  54.1 30.1 %copy-start.1 = (f32[1024,128]{1,0:T(8,128)S(1)}, f32[1024,128]{1,0:T(8,128)}, u32[]{:S(2)}) copy-start(f32[1024,128]{1,0:T(8,128)} %get-tuple-element.23.suffix_ref) | copy-start | bytes 1572868
  54.1 30.1 %all-to-all-start.1 = ((bf16[16,112,128]{2,1,0:T(8,128)(2,1)}), bf16[16,112,128]{2,1,0:T(8,128)(2,1)S(1)}, u32[]{:S(2)}, u32[]{:S(2)}) async-start(bf16[16,112,128]{2,1,0:T(8,128)(2,1)} %prefix.3), calls=%async_computation.1 | async-start | bytes 917504 | tf_op jit(solution)/shard_map/all_to_all | solution.py:438
  84.2 13.6 %copy-start = (bf16[512,2880]{0,1:T(8,128)(2,1)S(1)}, bf16[512,2880]{0,1:T(8,128)(2,1)}, u32[]{:S(2)}) copy-start(bf16[512,2880]{0,1:T(8,128)(2,1)} %param.13) | copy-start | bytes 8847364
  88.3 11.3 %collective-permute-start.3 = (bf16[4,192,360]{2,1,0:T(8,128)(2,1)}, bf16[4,192,360]{2,1,0:T(8,128)(2,1)S(1)}, u32[]{:S(2)}, u32[]{:S(2)}) collective-permute-start(bf16[4,192,360]{2,1,0:T(8,128)(2,1)} %get-tuple-element.26), channel_id=1, source_target_pairs={{0,1},{1,0},{2,3},{3,2},{4,5},{5,4},{6,7},{7,6},{8,9},{9,8},{10,11... | collective-permute-start | bytes 1658888 | tf_op jit(solution)/shard_map/ppermute | solution.py:392

commit v9 on v8

--- a/solution.py
+++ b/solution.py
@@ -180,7 +180,14 @@
     z_size = recv_ref.shape[0]
     span = CAPACITY * ROWS
     rows = z_size * span
-    copies = [pltpu.make_async_copy(sources[i], cache.at[i], sems.at[i]) for i in range(count)]
+    if start:
+        places = [cache.at[0, :HALF], cache.at[0, HALF:]]
+    else:
+        places = [cache.at[i] for i in range(count)]
+    copies = [
+        pltpu.make_async_copy(source, place, sems.at[i])
+        for i, (source, place) in enumerate(zip(sources, places))
+    ]
 
     @pl.when(index == 0)
     def _():
@@ -192,7 +199,12 @@
 
     group = index + (X_SIZE - count if start else 0)
     for i in range(count):
-        pl.when(index == i)(copies[i].wait)
+
+        @pl.when(index == i)
+        def _():
+            for copy in copies if start else copies[i : i + 1]:
+                copy.wait()
+
     values[:HALF, :] = cache[index, HALF:]
     place = pl.ds(pl.multiple_of(group * span, 8), span)
     own_place = pl.ds(pl.multiple_of(index * span, 8), span)
@@ -262,7 +274,7 @@
 
 def prefix_attention(recv, caches, before=None):
     z_size = recv.shape[0]
-    count = len(caches)
+    count = len(caches) if before is None else 1
     start = 0 if before is None else FIRST_ROWS
     length = caches[0].shape[1]
     rows = count * CAPACITY * ROWS + GROUPS
@@ -275,7 +287,7 @@
         aliases = {len(operands): 0}
         operands.append(before)
         inner = kernel
-        kernel = lambda *refs: inner(*refs[:2], *refs[3:])
+        kernel = lambda *refs: inner(*refs[:3], *refs[4:])
     return pl.pallas_call(
         kernel,
         grid=(count,),
@@ -288,7 +300,7 @@
             pltpu.VMEM(recv.shape, jnp.float32),
             pltpu.VMEM((z_size, rows, LANES), jnp.float32),
             pltpu.VMEM((z_size, rows, LANES), jnp.bfloat16),
-            pltpu.SemaphoreType.DMA((count,)),
+            pltpu.SemaphoreType.DMA((len(caches),)),
             pltpu.SemaphoreType.DMA,
         ],
         input_output_aliases=aliases,
@@ -426,7 +438,7 @@
 
     right = from_offset(kv, 1)
     left = from_offset(kv_out, -1)
-    opposite = from_offset(right, 1)
+    opposite = (from_offset(right[:HALF], 1), from_offset(left[HALF:], -1))
     recv = lax.all_to_all(
         send, "prefix", split_axis=0, concat_axis=0, axis_index_groups=z_groups, tiled=True
     )
@@ -434,7 +446,7 @@
     suffix_out, suffix_lse = suffix_attention(suffix_lengths, q3, suffix_rows)
     recv, suffix_out, suffix_lse = lax.optimization_barrier((recv, suffix_out, suffix_lse))
     ret = prefix_attention(recv, (kv, right, left))
-    ret = prefix_attention(recv, (opposite,), ret)
+    ret = prefix_attention(recv, opposite, ret)
     homed = lax.all_to_all(
         ret, "prefix", split_axis=0, concat_axis=0, axis_index_groups=z_groups, tiled=True
     )

time: 116 us -> 121 us (1.043)
  waiting for transfers between devices: 23.3 us -> 26.4 us
  starting transfers between devices: 47.7 us -> 49.3 us
    ppermute x3 -> x4, waiting for transfers between devices: 3.14 us -> 6.24 us  [from_offset(): return lax.ppermute(array, 'prefix', pairs)]
    ppermute x3 -> x4, starting transfers between devices: 11.5 us -> 12.8 us  [from_offset(): return lax.ppermute(array, 'prefix', pairs)]
  transfers between devices with their start and end apart: 6 -> 7, of which waited for: 4 -> 3; matrix products, arithmetic and copies ran while one was open for 0% -> 1% of each run, Pallas kernels for 16% -> 15%
where the time goes in v9:
time: 121 us; the launch traced here: 120 us
  starting transfers between devices  49.3 us (41%)
  Pallas kernels  28.4 us (23%)
  waiting for transfers between devices  26.4 us (22%)
  blocking collectives  13.6 us (11%)
    all_to_all x1, waiting for transfers between devices, shards(): lax.all_to_all(ret, 'prefix', split_axis=0, concat_axis=0, axis_index_gro...  19 us
    all_to_all x1, starting transfers between devices, shards(): lax.all_to_all(send, 'prefix', split_axis=0, concat_axis=0, axis_index_gr...  15.8 us
    all_to_all x1, blocking collectives, shards(): lax.all_to_all(parts, 'tensor', split_axis=0, concat_axis=0, axis_index_g...  13.6 us
    ppermute x4, starting transfers between devices, from_offset(): return lax.ppermute(array, 'prefix', pairs)  12.8 us
    pallas_call x2, Pallas kernels, prefix_attention(): pl.pallas_call(kernel, grid=(count,), out_shape=jax.ShapeDtypeStruct((z_s...  12.1 us
    all_to_all x1, starting transfers between devices, shards(): lax.all_to_all(ret, 'prefix', split_axis=0, concat_axis=0, axis_index_gro...  11.3 us
    ppermute x1, starting transfers between devices, merge_project(): received = lax.ppermute(other, 'tensor', [(i, i ^ 1) for i in range(parts)])  9.45 us
    pallas_call x1, Pallas kernels, suffix_attention(): pl.pallas_call(suffix_kernel, out_shape=(shape, shape), in_specs=[pl.Bloc...  8.73 us
  transfers between devices with their start and end apart: 7, of which 3 were waited for; matrix products, arithmetic and copies ran while one was open for 1% of the time, Pallas kernels for 15%

profile of v9, /device:TPU:1, one launch (start us, length us, event | category | flops | bytes accessed | tf_op | source)
XLA Modules:
  0.0 119.6 jit_solution(2353397782149329294)
XLA Ops:
  0.0 2.7 %route.1 = (bf16[16,96,128]{2,1,0:T(8,128)(2,1)}, s32[64]{0:T(128)}) custom-call(s32[1]{0:T(128)} %bitcast.1.me_ref, s32[4096]{0:T(1024)} %bitcast.21, s32[64]{0:T(128)} %owner_ref.1, bf16[3,64,512]{2,1,0:T(8,128)(2,1)} %bitcast.19), custom_call_target="tpu_custom_call" | custom-call | tf_op jit(solution)/shard_map/route/pallas_call | solution.py:98
  2.7 15.8 %all-to-all-start = ((bf16[16,96,128]{2,1,0:T(8,128)(2,1)}), bf16[16,96,128]{2,1,0:T(8,128)(2,1)S(1)}, u32[]{:S(2)}, u32[]{:S(2)}) async-start(bf16[16,96,128]{2,1,0:T(8,128)(2,1)} %get-tuple-element.18), calls=%async_computation | async-start | bytes 786432 | tf_op jit(solution)/shard_map/all_to_all | solution.py:442
  18.4 4.4 %collective-permute-start = (bf16[128,2304]{1,0:T(8,128)(2,1)}, bf16[128,2304]{1,0:T(8,128)(2,1)S(1)}, u32[]{:S(2)}, u32[]{:S(2)}) collective-permute-start(bf16[128,2304]{1,0:T(8,128)(2,1)} %bitcast.16), channel_id=1, source_target_pairs={{8,0},{16,8},{24,16},{0,24},{40,32},{48,40},{56,48},{32,56},{72,64... | collective-permute-start | bytes 1769480 | tf_op jit(solution)/shard_map/ppermute | solution.py:437
  22.8 1.9 %collective-permute-start.2 = (bf16[128,2304]{1,0:T(8,128)(2,1)}, bf16[128,2304]{1,0:T(8,128)(2,1)S(1)}, u32[]{:S(2)}, u32[]{:S(2)}) collective-permute-start(bf16[128,2304]{1,0:T(8,128)(2,1)} %bitcast.17), channel_id=1, source_target_pairs={{24,0},{0,8},{8,16},{16,24},{56,32},{32,40},{40,48},{48,56},{88,64... | collective-permute-start | bytes 1769480 | tf_op jit(solution)/shard_map/ppermute | solution.py:437
  24.8 8.7 %suffix.1 = (f32[1024,128]{1,0:T(8,128)}, f32[1024,128]{1,0:T(8,128)}) custom-call(s32[64]{0:T(128)} %length_ref.1, bf16[3,64,512]{2,1,0:T(8,128)(2,1)} %bitcast.20, bf16[64,80,128]{2,1,0:T(8,128)(2,1)} %bitcast.22), custom_call_target="tpu_custom_call" | custom-call | flops 8000000000 | bytes 8000000 | tf_op jit(solution)/shard_map/suffix/pallas_call | solution.py:159
  33.5 0.0 copy-start.4
  33.5 6.2 %collective-permute-done.2.refs_2_ = bf16[128,2304]{1,0:T(8,128)(2,1)S(1)} collective-permute-done((bf16[128,2304]{1,0:T(8,128)(2,1)}, bf16[128,2304]{1,0:T(8,128)(2,1)S(1)}, u32[]{:S(2)}, u32[]{:S(2)}) %collective-permute-start.2) | collective-permute-done | bytes 589856 | tf_op jit(solution)/shard_map/ppermute | solution.py:437
  39.7 1.9 %collective-permute-start.3 = (bf16[64,2304]{1,0:T(8,128)(2,1)S(1)}, bf16[64,2304]{1,0:T(8,128)(2,1)S(1)}, u32[]{:S(2)}, u32[]{:S(2)}) collective-permute-start(bf16[64,2304]{1,0:T(8,128)(2,1)S(1)} %slice.9), channel_id=1, source_target_pairs={{24,0},{0,8},{8,16},{16,24},{56,32},{32,40},{40,48},{48,56},{88,64... | collective-permute-start | bytes 884744 | tf_op jit(solution)/shard_map/ppermute | solution.py:437
  41.7 0.0 collective-permute-done.refs_1_
  41.7 0.7 slice.8
  42.4 4.6 %collective-permute-start.1 = (bf16[64,2304]{1,0:T(8,128)(2,1)}, bf16[64,2304]{1,0:T(8,128)(2,1)S(1)}, u32[]{:S(2)}, u32[]{:S(2)}) collective-permute-start(bf16[64,2304]{1,0:T(8,128)(2,1)} %slice.8), channel_id=1, source_target_pairs={{8,0},{16,8},{24,16},{0,24},{40,32},{48,40},{56,48},{32,56},{72,64... | collective-permute-start | bytes 884744 | tf_op jit(solution)/shard_map/ppermute | solution.py:437
  47.0 0.0 all-to-all-done.recv_ref.refs_0_
  47.0 0.0 copy-done.4
  47.0 8.8 %prefix.2.refs_3_ = bf16[16,112,128]{2,1,0:T(8,128)(2,1)} custom-call(bf16[16,96,128]{2,1,0:T(8,128)(2,1)S(1)} %all-to-all-done.recv_ref.refs_0_, bf16[128,2304]{1,0:T(8,128)(2,1)S(1)} %bitcast.18, bf16[128,2304]{1,0:T(8,128)(2,1)S(1)} %collective-permute-done.refs_1_, bf16[128,2304]{1,0:T(8,128)(2,1)S(1)} %collective-permute-done.2.refs_2_), custom_call_target="tpu_custom_call" | custom-call | flops 7500000256 | bytes 3000000 | tf_op jit(solution)/shard_map/prefix/pallas_call | solution.py:291
  55.8 0.0 copy-start.3
  55.9 0.0 collective-permute-done.3.refs_2_
  55.9 0.0 collective-permute-done.1.refs_1_
  55.9 0.0 copy-start.2
  55.9 3.3 %prefix.3 = bf16[16,112,128]{2,1,0:T(8,128)(2,1)} custom-call(bf16[16,96,128]{2,1,0:T(8,128)(2,1)S(1)} %all-to-all-done.recv_ref.refs_0_, bf16[64,2304]{1,0:T(8,128)(2,1)S(1)} %collective-permute-done.1.refs_1_, bf16[64,2304]{1,0:T(8,128)(2,1)S(1)} %collective-permute-done.3.refs_2_, bf16[16,112,128]{2,1,0:T(8,128)(2,1)} %prefix.2.refs_3_), custom_call_target="tpu_custom_call", output_to_operand_aliasing={{}: (3, {})} | custom-call | flops 2500000000 | bytes 1000000 | tf_op jit(solution)/shard_map/prefix/pallas_call | solution.py:291
  59.2 0.0 copy-start.1
  59.2 11.3 %all-to-all-start.1 = ((bf16[16,112,128]{2,1,0:T(8,128)(2,1)}), bf16[16,112,128]{2,1,0:T(8,128)(2,1)S(1)}, u32[]{:S(2)}, u32[]{:S(2)}) async-start(bf16[16,112,128]{2,1,0:T(8,128)(2,1)} %prefix.3), calls=%async_computation.1 | async-start | bytes 917504 | tf_op jit(solution)/shard_map/all_to_all | solution.py:450
  70.5 19.0 %all-to-all-done.1.ret_ref = bf16[16,112,128]{2,1,0:T(8,128)(2,1)S(1)} async-done(((bf16[16,112,128]{2,1,0:T(8,128)(2,1)}), bf16[16,112,128]{2,1,0:T(8,128)(2,1)S(1)}, u32[]{:S(2)}, u32[]{:S(2)}) %all-to-all-start.1) | async-done | bytes 458784 | tf_op jit(solution)/shard_map/all_to_all | solution.py:450
  89.6 0.0 copy-done.3
  89.6 0.0 copy-done.2
  89.6 0.0 copy-done.1
  89.6 0.0 copy-start
  89.6 4.2 %merge.1 = (bf16[4,192,360]{2,1,0:T(8,128)(2,1)}, bf16[192,512]{1,0:T(8,128)(2,1)S(1)}) custom-call(s32[1]{0:T(128)} %bitcast.core_ref, s32[64]{0:T(128)S(1)} %copy-done.3, bf16[16,112,128]{2,1,0:T(8,128)(2,1)S(1)} %all-to-all-done.1.ret_ref, f32[1024,128]{1,0:T(8,128)S(1)} %copy-done.1, f32[1024,128]{1,0:T(8,128)S(1)} %copy-done.2, ...), custom_call_target="tpu_custom_call" | custom-call | tf_op jit(solution)/shard_map/merge/pallas_call | solution.py:380
  93.8 9.5 %collective-permute-start.4 = (bf16[4,192,360]{2,1,0:T(8,128)(2,1)}, bf16[4,192,360]{2,1,0:T(8,128)(2,1)S(1)}, u32[]{:S(2)}, u32[]{:S(2)}) collective-permute-start(bf16[4,192,360]{2,1,0:T(8,128)(2,1)} %get-tuple-element.26), channel_id=1, source_target_pairs={{0,1},{1,0},{2,3},{3,2},{4,5},{5,4},{6,7},{7,6},{8,9},{9,8},{10,11... | collective-permute-start | bytes 1658888 | tf_op jit(solution)/shard_map/ppermute | solution.py:404
  103.3 0.0 copy-done
  103.3 0.7 project.1
  103.9 1.1 collective-permute-done.4
  105.1 0.1 add_convert_fusion
  105.2 13.6 %all_to_all.15 = bf16[4,192,360]{2,1,0:T(8,128)(2,1)S(1)} all-to-all(bf16[4,192,360]{2,1,0:T(8,128)(2,1)S(1)} %add_convert_fusion), channel_id=1, replica_groups={{0,2,4,6},{1,3,5,7},{8,10,12,14},{9,11,13,15},{16,18,20,22},{17,19,21,2..., dimensions={0} | all-to-all | bytes 1105920 | tf_op jit(solution)/shard_map/all_to_all | solution.py:456
  118.8 0.8 reduce_sum.12
  (1 shorter events, 0.0 us)
Async XLA Ops:
  2.7 44.3 %all-to-all-start = ((bf16[16,96,128]{2,1,0:T(8,128)(2,1)}), bf16[16,96,128]{2,1,0:T(8,128)(2,1)S(1)}, u32[]{:S(2)}, u32[]{:S(2)}) async-start(bf16[16,96,128]{2,1,0:T(8,128)(2,1)} %get-tuple-element.18), calls=%async_computation | async-start | bytes 786432 | tf_op jit(solution)/shard_map/all_to_all | solution.py:442
  18.4 23.3 %collective-permute-start = (bf16[128,2304]{1,0:T(8,128)(2,1)}, bf16[128,2304]{1,0:T(8,128)(2,1)S(1)}, u32[]{:S(2)}, u32[]{:S(2)}) collective-permute-start(bf16[128,2304]{1,0:T(8,128)(2,1)} %bitcast.16), channel_id=1, source_target_pairs={{8,0},{16,8},{24,16},{0,24},{40,32},{48,40},{56,48},{32,56},{72,64... | collective-permute-start | bytes 1769480 | tf_op jit(solution)/shard_map/ppermute | solution.py:437
  22.8 16.9 %collective-permute-start.2 = (bf16[128,2304]{1,0:T(8,128)(2,1)}, bf16[128,2304]{1,0:T(8,128)(2,1)S(1)}, u32[]{:S(2)}, u32[]{:S(2)}) collective-permute-start(bf16[128,2304]{1,0:T(8,128)(2,1)} %bitcast.17), channel_id=1, source_target_pairs={{24,0},{0,8},{8,16},{16,24},{56,32},{32,40},{40,48},{48,56},{88,64... | collective-permute-start | bytes 1769480 | tf_op jit(solution)/shard_map/ppermute | solution.py:437
  33.5 13.5 %copy-start.4 = (bf16[1,1,128,2304]{3,2,1,0:T(8,128)(2,1)S(1)}, bf16[1,1,128,2304]{3,2,1,0:T(8,128)(2,1)}, u32[]{:S(2)}) copy-start(bf16[1,1,128,2304]{3,2,1,0:T(8,128)(2,1)} %param.8) | copy-start | bytes 1769476
  39.7 16.1 %collective-permute-start.3 = (bf16[64,2304]{1,0:T(8,128)(2,1)S(1)}, bf16[64,2304]{1,0:T(8,128)(2,1)S(1)}, u32[]{:S(2)}, u32[]{:S(2)}) collective-permute-start(bf16[64,2304]{1,0:T(8,128)(2,1)S(1)} %slice.9), channel_id=1, source_target_pairs={{24,0},{0,8},{8,16},{16,24},{56,32},{32,40},{40,48},{48,56},{88,64... | collective-permute-start | bytes 884744 | tf_op jit(solution)/shard_map/ppermute | solution.py:437
  42.4 13.4 %collective-permute-start.1 = (bf16[64,2304]{1,0:T(8,128)(2,1)}, bf16[64,2304]{1,0:T(8,128)(2,1)S(1)}, u32[]{:S(2)}, u32[]{:S(2)}) collective-permute-start(bf16[64,2304]{1,0:T(8,128)(2,1)} %slice.8), channel_id=1, source_target_pairs={{8,0},{16,8},{24,16},{0,24},{40,32},{48,40},{56,48},{32,56},{72,64... | collective-permute-start | bytes 884744 | tf_op jit(solution)/shard_map/ppermute | solution.py:437
  55.8 33.8 %copy-start.3 = (s32[64]{0:T(128)S(1)}, s32[64]{0:T(128)}, u32[]{:S(2)}) copy-start(s32[64]{0:T(128)} %get-tuple-element.16.code_ref) | copy-start | bytes 772
  55.9 33.7 %copy-start.2 = (f32[1024,128]{1,0:T(8,128)S(1)}, f32[1024,128]{1,0:T(8,128)}, u32[]{:S(2)}) copy-start(f32[1024,128]{1,0:T(8,128)} %get-tuple-element.24.suffix_lse_ref) | copy-start | bytes 1572868
  59.2 30.4 %copy-start.1 = (f32[1024,128]{1,0:T(8,128)S(1)}, f32[1024,128]{1,0:T(8,128)}, u32[]{:S(2)}) copy-start(f32[1024,128]{1,0:T(8,128)} %get-tuple-element.23.suffix_ref) | copy-start | bytes 1572868
  59.2 30.4 %all-to-all-start.1 = ((bf16[16,112,128]{2,1,0:T(8,128)(2,1)}), bf16[16,112,128]{2,1,0:T(8,128)(2,1)S(1)}, u32[]{:S(2)}, u32[]{:S(2)}) async-start(bf16[16,112,128]{2,1,0:T(8,128)(2,1)} %prefix.3), calls=%async_computation.1 | async-start | bytes 917504 | tf_op jit(solution)/shard_map/all_to_all | solution.py:450
  89.6 13.6 %copy-start = (bf16[512,2880]{0,1:T(8,128)(2,1)S(1)}, bf16[512,2880]{0,1:T(8,128)(2,1)}, u32[]{:S(2)}) copy-start(bf16[512,2880]{0,1:T(8,128)(2,1)} %param.13) | copy-start | bytes 8847364
  93.8 11.3 %collective-permute-start.4 = (bf16[4,192,360]{2,1,0:T(8,128)(2,1)}, bf16[4,192,360]{2,1,0:T(8,128)(2,1)S(1)}, u32[]{:S(2)}, u32[]{:S(2)}) collective-permute-start(bf16[4,192,360]{2,1,0:T(8,128)(2,1)} %get-tuple-element.26), channel_id=1, source_target_pairs={{0,1},{1,0},{2,3},{3,2},{4,5},{5,4},{6,7},{7,6},{8,9},{9,8},{10,11... | collective-permute-start | bytes 1658888 | tf_op jit(solution)/shard_map/ppermute | solution.py:404
